TPU v7x, 256 devices: a whole 4x4x8 slice. The times are simulated.
256 devices in a mesh: group: 8 (over y, x_hi), blk: 32 (over z, x_lo, core).
Axes of the slice: x: 4 (x_hi: 2, x_lo: 2; x = x_hi * 2 + x_lo), y: 4, z: 8, core: 2. Of those that a mesh axis runs over, the one named last changes fastest.
Arguments:
- picture_embedding_matrix: float32 [32768, 1152], P(('group', 'blk')), parts along dimension 0, may hold values from -0.1875 to 0.1875
- caption_embedding_matrix: float32 [32768, 1152], P(('group', 'blk')), parts along dimension 0, may hold values from -0.1875 to 0.1875
- sharpness_scale: float32 [1], replicated, may hold values from 5 to 15
- offset_shift_vector: float32 [1], replicated, may hold values from -3 to -1
Outputs:
- loss_rows: float32 [32768], P(('group', 'blk')), parts along dimension 0
- grad_image: float32 [32768, 1152], P(('group', 'blk')), parts along dimension 0
- grad_text: float32 [32768, 1152], P(('group', 'blk')), parts along dimension 0
There are 8 independent parts, one for each index of `group`. A program takes and returns all parts, laid end to end along the dimension named above; an argument that names none is the same for every part. Nothing has to cross between parts.
All inputs are finite; a program needn't handle non-finite values.
Results may differ from a plain program's by a relative error of at most 0.014.
Values may be sent and summed in bfloat16 or wider, within the bound.
No kernel may reach another device: no remote copies, remote signals or barrier semaphores. Data moves between devices by JAX's collectives and lax.ppermute only.
A program may use at most 128 MiB of HBM per device.

v0:
```python
import jax
import jax.numpy as jnp
from jax import lax
from jax.sharding import PartitionSpec as P


def passed_along(block, axis, distance):
    devices = range(lax.axis_size(axis))
    route = [((i - distance) % len(devices), i) for i in devices]
    return lax.ppermute(block, axis, route)


def normalize(feats):
    scale = 1.0 / jnp.sqrt(jnp.sum(feats * feats, axis=1, keepdims=True) + 1e-06)
    return (feats * scale, scale)


def back_norm(hat, scale, grad):
    return scale * (grad - hat * jnp.sum(hat * grad, axis=1, keepdims=True))


def submatrix_weight(
    first_factor_matrix,
    second_factor_matrix,
    source_positions,
    target_positions,
    sharpness_scale,
    offset_shift_vector,
):
    cosine_scores = lax.dot_general(
        first_factor_matrix,
        second_factor_matrix,
        (((1,), (1,)), ((), ())),
        preferred_element_type=jnp.float32,
    )
    match_scores = sharpness_scale[0] * cosine_scores + offset_shift_vector[0]
    match_polarity = jnp.where(
        source_positions[:, None] == target_positions[None, :], jnp.float32(1.0), jnp.float32(-1.0)
    )
    match_weight_factor = (
        -match_polarity * jax.nn.sigmoid(-match_polarity * match_scores) * sharpness_scale[0]
    ).astype(jnp.bfloat16)
    return (match_scores, match_polarity, match_weight_factor)


def submatrix_penalty_entries(
    picture_gradient_total,
    submatrix_portion,
    source_positions,
    first_target_position,
    sharpness_scale,
    offset_shift_vector,
):
    target_positions = first_target_position + jnp.arange(
        submatrix_portion.shape[0], dtype=jnp.int32
    )
    match_scores, match_polarity, match_weight_factor = submatrix_weight(
        picture_gradient_total,
        submatrix_portion,
        source_positions,
        target_positions,
        sharpness_scale,
        offset_shift_vector,
    )
    losses = -jnp.sum(jax.nn.log_sigmoid(match_polarity * match_scores), axis=1)
    partial_image = jnp.dot(
        match_weight_factor, submatrix_portion, preferred_element_type=jnp.float32
    )
    return (losses, partial_image, match_weight_factor)


def text_terms(match_weight_factor, picture_gradient_total):
    return lax.dot_general(
        match_weight_factor,
        picture_gradient_total,
        (((0,), (0,)), ((), ())),
        preferred_element_type=jnp.float32,
    )


def body(picture_embedding_matrix, caption_embedding_matrix, sharpness_scale, offset_shift_vector):
    source_span = picture_embedding_matrix.shape[0]
    blocks = lax.axis_size("blk")
    replica_position = lax.axis_index("blk")
    image_hat, image_scale = normalize(picture_embedding_matrix)
    text_hat, text_scale = normalize(caption_embedding_matrix)
    picture_gradient_total = image_hat.astype(jnp.bfloat16)
    caption_gradient_total = text_hat.astype(jnp.bfloat16)
    source_positions = replica_position * source_span + jnp.arange(source_span, dtype=jnp.int32)
    losses, partial_image, match_weight_factor = submatrix_penalty_entries(
        picture_gradient_total,
        caption_gradient_total,
        source_positions,
        replica_position * source_span,
        sharpness_scale,
        offset_shift_vector,
    )
    carried = text_terms(match_weight_factor, picture_gradient_total)

    def advance(step, state):
        submatrix_portion, carried, losses, partial_image = state
        submatrix_portion = passed_along(submatrix_portion, "blk", 1)
        carried = passed_along(carried, "blk", 1)
        holder_replica = jnp.mod(replica_position - step, blocks)
        more_loss, more_image, match_weight_factor = submatrix_penalty_entries(
            picture_gradient_total,
            submatrix_portion,
            source_positions,
            holder_replica * source_span,
            sharpness_scale,
            offset_shift_vector,
        )
        return (
            submatrix_portion,
            carried + text_terms(match_weight_factor, picture_gradient_total),
            losses + more_loss,
            partial_image + more_image,
        )

    submatrix_portion, carried, losses, partial_image = lax.fori_loop(
        1, blocks, advance, (caption_gradient_total, carried, losses, partial_image)
    )
    hat_grad_text = passed_along(carried.astype(jnp.bfloat16), "blk", 1).astype(carried.dtype)
    grad_image = back_norm(image_hat, image_scale, partial_image)
    grad_text = back_norm(text_hat, text_scale, hat_grad_text)
    return (losses, grad_image, grad_text)


def solution(mesh):
    in_specs = (P(("group", "blk"), None), P(("group", "blk"), None), P(), P())
    out_specs = (P(("group", "blk")), P(("group", "blk"), None), P(("group", "blk"), None))
    return jax.shard_map(body, mesh=mesh, in_specs=in_specs, out_specs=out_specs, check_vma=False)
```

profile of v0, /device:TPU:1, one launch (start us, length us, event | category | flops | bytes accessed | tf_op | source)
XLA Modules:
  0.0 504.5 jit_solution(7086082172008319645)
XLA Ops:
  7.1 484.2 %while.22 = (s32[]{:T(128)}, bf16[128,1152]{1,0:T(8,128)(2,1)}, f32[128,1152]{1,0:T(8,128)S(1)}, f32[128]{0:T(128)S(1)}, f32[128,1152]{1,0:T(8,128)S(1)}, /*inde...) while((s32[]{:T(128)}, bf16[128,1152]{1,0:T(8,128)(2,1)}, ...), condition=%wide.region_5.6_spmd.clone, body=%wide.region_3.5_spmd.clone.sunk | while | flops 114082064 | bytes 7870842 | solution.py:120
  7.1 2.7 collective-permute-start
  9.9 3.9 collective-permute-done
  13.8 1.6 fusion.53
  17.1 2.9 collective-permute-done.1
  21.0 2.6 collective-permute-start
  23.6 4.6 collective-permute-done
  28.2 1.6 fusion.53
  31.5 2.2 collective-permute-done.1
  34.7 2.6 collective-permute-start
  37.7 6.4 %collective-permute-done = bf16[128,1152]{1,0:T(8,128)(2,1)S(1)} collective-permute-done((bf16[128,1152]{1,0:T(8,128)(2,1)}, bf16[128,1152]{1,0:T(8,128)(2,1)S(1)}, u32[]{:S(2)}, u32[]{:S(2)}) %collective-permute-start) | collective-permute-done | bytes 294944 | tf_op jit(solution)/shard_map/while/body/eval_jaxpr/ppermute | solution.py:10
  44.0 1.6 fusion.53
  48.4 2.6 collective-permute-start
  52.3 7.6 %collective-permute-done = bf16[128,1152]{1,0:T(8,128)(2,1)S(1)} collective-permute-done((bf16[128,1152]{1,0:T(8,128)(2,1)}, bf16[128,1152]{1,0:T(8,128)(2,1)S(1)}, u32[]{:S(2)}, u32[]{:S(2)}) %collective-permute-start) | collective-permute-done | bytes 294944 | tf_op jit(solution)/shard_map/while/body/eval_jaxpr/ppermute | solution.py:10
  59.8 1.6 fusion.53
  64.7 2.2 collective-permute-start.1
  66.9 8.8 %collective-permute-done = bf16[128,1152]{1,0:T(8,128)(2,1)S(1)} collective-permute-done((bf16[128,1152]{1,0:T(8,128)(2,1)}, bf16[128,1152]{1,0:T(8,128)(2,1)S(1)}, u32[]{:S(2)}, u32[]{:S(2)}) %collective-permute-start) | collective-permute-done | bytes 294944 | tf_op jit(solution)/shard_map/while/body/eval_jaxpr/ppermute | solution.py:10
  75.7 1.6 fusion.53
  81.5 10.0 %collective-permute-done = bf16[128,1152]{1,0:T(8,128)(2,1)S(1)} collective-permute-done((bf16[128,1152]{1,0:T(8,128)(2,1)}, bf16[128,1152]{1,0:T(8,128)(2,1)S(1)}, u32[]{:S(2)}, u32[]{:S(2)}) %collective-permute-start) | collective-permute-done | bytes 294944 | tf_op jit(solution)/shard_map/while/body/eval_jaxpr/ppermute | solution.py:10
  91.5 1.6 fusion.53
  96.1 11.2 %collective-permute-done = bf16[128,1152]{1,0:T(8,128)(2,1)S(1)} collective-permute-done((bf16[128,1152]{1,0:T(8,128)(2,1)}, bf16[128,1152]{1,0:T(8,128)(2,1)S(1)}, u32[]{:S(2)}, u32[]{:S(2)}) %collective-permute-start) | collective-permute-done | bytes 294944 | tf_op jit(solution)/shard_map/while/body/eval_jaxpr/ppermute | solution.py:10
  107.3 1.6 fusion.53
  111.8 11.3 %collective-permute-done = bf16[128,1152]{1,0:T(8,128)(2,1)S(1)} collective-permute-done((bf16[128,1152]{1,0:T(8,128)(2,1)}, bf16[128,1152]{1,0:T(8,128)(2,1)S(1)}, u32[]{:S(2)}, u32[]{:S(2)}) %collective-permute-start) | collective-permute-done | bytes 294944 | tf_op jit(solution)/shard_map/while/body/eval_jaxpr/ppermute | solution.py:10
  123.1 1.6 fusion.53
  127.7 11.3 %collective-permute-done = bf16[128,1152]{1,0:T(8,128)(2,1)S(1)} collective-permute-done((bf16[128,1152]{1,0:T(8,128)(2,1)}, bf16[128,1152]{1,0:T(8,128)(2,1)S(1)}, u32[]{:S(2)}, u32[]{:S(2)}) %collective-permute-start) | collective-permute-done | bytes 294944 | tf_op jit(solution)/shard_map/while/body/eval_jaxpr/ppermute | solution.py:10
  139.0 1.6 fusion.53
  143.5 11.3 %collective-permute-done = bf16[128,1152]{1,0:T(8,128)(2,1)S(1)} collective-permute-done((bf16[128,1152]{1,0:T(8,128)(2,1)}, bf16[128,1152]{1,0:T(8,128)(2,1)S(1)}, u32[]{:S(2)}, u32[]{:S(2)}) %collective-permute-start) | collective-permute-done | bytes 294944 | tf_op jit(solution)/shard_map/while/body/eval_jaxpr/ppermute | solution.py:10
  154.8 1.6 fusion.53
  159.3 11.3 %collective-permute-done = bf16[128,1152]{1,0:T(8,128)(2,1)S(1)} collective-permute-done((bf16[128,1152]{1,0:T(8,128)(2,1)}, bf16[128,1152]{1,0:T(8,128)(2,1)S(1)}, u32[]{:S(2)}, u32[]{:S(2)}) %collective-permute-start) | collective-permute-done | bytes 294944 | tf_op jit(solution)/shard_map/while/body/eval_jaxpr/ppermute | solution.py:10
  170.6 1.6 fusion.53
  175.1 11.3 %collective-permute-done = bf16[128,1152]{1,0:T(8,128)(2,1)S(1)} collective-permute-done((bf16[128,1152]{1,0:T(8,128)(2,1)}, bf16[128,1152]{1,0:T(8,128)(2,1)S(1)}, u32[]{:S(2)}, u32[]{:S(2)}) %collective-permute-start) | collective-permute-done | bytes 294944 | tf_op jit(solution)/shard_map/while/body/eval_jaxpr/ppermute | solution.py:10
  186.4 1.6 fusion.53
  190.9 11.3 %collective-permute-done = bf16[128,1152]{1,0:T(8,128)(2,1)S(1)} collective-permute-done((bf16[128,1152]{1,0:T(8,128)(2,1)}, bf16[128,1152]{1,0:T(8,128)(2,1)S(1)}, u32[]{:S(2)}, u32[]{:S(2)}) %collective-permute-start) | collective-permute-done | bytes 294944 | tf_op jit(solution)/shard_map/while/body/eval_jaxpr/ppermute | solution.py:10
  202.3 1.6 fusion.53
  206.8 11.3 %collective-permute-done = bf16[128,1152]{1,0:T(8,128)(2,1)S(1)} collective-permute-done((bf16[128,1152]{1,0:T(8,128)(2,1)}, bf16[128,1152]{1,0:T(8,128)(2,1)S(1)}, u32[]{:S(2)}, u32[]{:S(2)}) %collective-permute-start) | collective-permute-done | bytes 294944 | tf_op jit(solution)/shard_map/while/body/eval_jaxpr/ppermute | solution.py:10
  218.1 1.6 fusion.53
  222.6 11.3 %collective-permute-done = bf16[128,1152]{1,0:T(8,128)(2,1)S(1)} collective-permute-done((bf16[128,1152]{1,0:T(8,128)(2,1)}, bf16[128,1152]{1,0:T(8,128)(2,1)S(1)}, u32[]{:S(2)}, u32[]{:S(2)}) %collective-permute-start) | collective-permute-done | bytes 294944 | tf_op jit(solution)/shard_map/while/body/eval_jaxpr/ppermute | solution.py:10
  233.9 1.6 fusion.53
  238.4 11.3 %collective-permute-done = bf16[128,1152]{1,0:T(8,128)(2,1)S(1)} collective-permute-done((bf16[128,1152]{1,0:T(8,128)(2,1)}, bf16[128,1152]{1,0:T(8,128)(2,1)S(1)}, u32[]{:S(2)}, u32[]{:S(2)}) %collective-permute-start) | collective-permute-done | bytes 294944 | tf_op jit(solution)/shard_map/while/body/eval_jaxpr/ppermute | solution.py:10
  249.7 1.6 fusion.53
  254.2 11.3 %collective-permute-done = bf16[128,1152]{1,0:T(8,128)(2,1)S(1)} collective-permute-done((bf16[128,1152]{1,0:T(8,128)(2,1)}, bf16[128,1152]{1,0:T(8,128)(2,1)S(1)}, u32[]{:S(2)}, u32[]{:S(2)}) %collective-permute-start) | collective-permute-done | bytes 294944 | tf_op jit(solution)/shard_map/while/body/eval_jaxpr/ppermute | solution.py:10
  265.5 1.6 fusion.53
  270.1 11.3 %collective-permute-done = bf16[128,1152]{1,0:T(8,128)(2,1)S(1)} collective-permute-done((bf16[128,1152]{1,0:T(8,128)(2,1)}, bf16[128,1152]{1,0:T(8,128)(2,1)S(1)}, u32[]{:S(2)}, u32[]{:S(2)}) %collective-permute-start) | collective-permute-done | bytes 294944 | tf_op jit(solution)/shard_map/while/body/eval_jaxpr/ppermute | solution.py:10
  281.4 1.6 fusion.53
  285.9 11.3 %collective-permute-done = bf16[128,1152]{1,0:T(8,128)(2,1)S(1)} collective-permute-done((bf16[128,1152]{1,0:T(8,128)(2,1)}, bf16[128,1152]{1,0:T(8,128)(2,1)S(1)}, u32[]{:S(2)}, u32[]{:S(2)}) %collective-permute-start) | collective-permute-done | bytes 294944 | tf_op jit(solution)/shard_map/while/body/eval_jaxpr/ppermute | solution.py:10
  297.2 1.6 fusion.53
  301.7 11.3 %collective-permute-done = bf16[128,1152]{1,0:T(8,128)(2,1)S(1)} collective-permute-done((bf16[128,1152]{1,0:T(8,128)(2,1)}, bf16[128,1152]{1,0:T(8,128)(2,1)S(1)}, u32[]{:S(2)}, u32[]{:S(2)}) %collective-permute-start) | collective-permute-done | bytes 294944 | tf_op jit(solution)/shard_map/while/body/eval_jaxpr/ppermute | solution.py:10
  313.0 1.6 fusion.53
  317.5 11.3 %collective-permute-done = bf16[128,1152]{1,0:T(8,128)(2,1)S(1)} collective-permute-done((bf16[128,1152]{1,0:T(8,128)(2,1)}, bf16[128,1152]{1,0:T(8,128)(2,1)S(1)}, u32[]{:S(2)}, u32[]{:S(2)}) %collective-permute-start) | collective-permute-done | bytes 294944 | tf_op jit(solution)/shard_map/while/body/eval_jaxpr/ppermute | solution.py:10
  328.8 1.6 fusion.53
  333.4 11.3 %collective-permute-done = bf16[128,1152]{1,0:T(8,128)(2,1)S(1)} collective-permute-done((bf16[128,1152]{1,0:T(8,128)(2,1)}, bf16[128,1152]{1,0:T(8,128)(2,1)S(1)}, u32[]{:S(2)}, u32[]{:S(2)}) %collective-permute-start) | collective-permute-done | bytes 294944 | tf_op jit(solution)/shard_map/while/body/eval_jaxpr/ppermute | solution.py:10
  344.7 1.6 fusion.53
  349.2 11.3 %collective-permute-done = bf16[128,1152]{1,0:T(8,128)(2,1)S(1)} collective-permute-done((bf16[128,1152]{1,0:T(8,128)(2,1)}, bf16[128,1152]{1,0:T(8,128)(2,1)S(1)}, u32[]{:S(2)}, u32[]{:S(2)}) %collective-permute-start) | collective-permute-done | bytes 294944 | tf_op jit(solution)/shard_map/while/body/eval_jaxpr/ppermute | solution.py:10
  360.5 1.6 fusion.53
  365.0 11.3 %collective-permute-done = bf16[128,1152]{1,0:T(8,128)(2,1)S(1)} collective-permute-done((bf16[128,1152]{1,0:T(8,128)(2,1)}, bf16[128,1152]{1,0:T(8,128)(2,1)S(1)}, u32[]{:S(2)}, u32[]{:S(2)}) %collective-permute-start) | collective-permute-done | bytes 294944 | tf_op jit(solution)/shard_map/while/body/eval_jaxpr/ppermute | solution.py:10
  376.3 1.6 fusion.53
  380.8 11.3 %collective-permute-done = bf16[128,1152]{1,0:T(8,128)(2,1)S(1)} collective-permute-done((bf16[128,1152]{1,0:T(8,128)(2,1)}, bf16[128,1152]{1,0:T(8,128)(2,1)S(1)}, u32[]{:S(2)}, u32[]{:S(2)}) %collective-permute-start) | collective-permute-done | bytes 294944 | tf_op jit(solution)/shard_map/while/body/eval_jaxpr/ppermute | solution.py:10
  396.7 11.3 %collective-permute-done = bf16[128,1152]{1,0:T(8,128)(2,1)S(1)} collective-permute-done((bf16[128,1152]{1,0:T(8,128)(2,1)}, bf16[128,1152]{1,0:T(8,128)(2,1)S(1)}, u32[]{:S(2)}, u32[]{:S(2)}) %collective-permute-start) | collective-permute-done | bytes 294944 | tf_op jit(solution)/shard_map/while/body/eval_jaxpr/ppermute | solution.py:10
  412.5 11.3 %collective-permute-done = bf16[128,1152]{1,0:T(8,128)(2,1)S(1)} collective-permute-done((bf16[128,1152]{1,0:T(8,128)(2,1)}, bf16[128,1152]{1,0:T(8,128)(2,1)S(1)}, u32[]{:S(2)}, u32[]{:S(2)}) %collective-permute-start) | collective-permute-done | bytes 294944 | tf_op jit(solution)/shard_map/while/body/eval_jaxpr/ppermute | solution.py:10
  428.3 11.3 %collective-permute-done = bf16[128,1152]{1,0:T(8,128)(2,1)S(1)} collective-permute-done((bf16[128,1152]{1,0:T(8,128)(2,1)}, bf16[128,1152]{1,0:T(8,128)(2,1)S(1)}, u32[]{:S(2)}, u32[]{:S(2)}) %collective-permute-start) | collective-permute-done | bytes 294944 | tf_op jit(solution)/shard_map/while/body/eval_jaxpr/ppermute | solution.py:10
  444.1 11.3 %collective-permute-done = bf16[128,1152]{1,0:T(8,128)(2,1)S(1)} collective-permute-done((bf16[128,1152]{1,0:T(8,128)(2,1)}, bf16[128,1152]{1,0:T(8,128)(2,1)S(1)}, u32[]{:S(2)}, u32[]{:S(2)}) %collective-permute-start) | collective-permute-done | bytes 294944 | tf_op jit(solution)/shard_map/while/body/eval_jaxpr/ppermute | solution.py:10
  459.9 11.3 %collective-permute-done = bf16[128,1152]{1,0:T(8,128)(2,1)S(1)} collective-permute-done((bf16[128,1152]{1,0:T(8,128)(2,1)}, bf16[128,1152]{1,0:T(8,128)(2,1)S(1)}, u32[]{:S(2)}, u32[]{:S(2)}) %collective-permute-start) | collective-permute-done | bytes 294944 | tf_op jit(solution)/shard_map/while/body/eval_jaxpr/ppermute | solution.py:10
  475.8 11.3 %collective-permute-done = bf16[128,1152]{1,0:T(8,128)(2,1)S(1)} collective-permute-done((bf16[128,1152]{1,0:T(8,128)(2,1)}, bf16[128,1152]{1,0:T(8,128)(2,1)S(1)}, u32[]{:S(2)}, u32[]{:S(2)}) %collective-permute-start) | collective-permute-done | bytes 294944 | tf_op jit(solution)/shard_map/while/body/eval_jaxpr/ppermute | solution.py:10
  493.2 10.0 %collective-permute-done.2 = bf16[128,1152]{1,0:T(8,128)(2,1)S(1)} collective-permute-done((bf16[128,1152]{1,0:T(8,128)(2,1)S(1)}, bf16[128,1152]{1,0:T(8,128)(2,1)S(1)}, u32[]{:S(2)}, u32[]{:S(2)}) %collective-permute-start.2) | collective-permute-done | bytes 294944 | tf_op jit(solution)/shard_map/ppermute | solution.py:10
  (269 shorter events, 110.7 us)
Async XLA Ops:
  0.6 2.7 copy-start.1
  7.1 6.7 %collective-permute-start = (bf16[128,1152]{1,0:T(8,128)(2,1)}, bf16[128,1152]{1,0:T(8,128)(2,1)S(1)}, u32[]{:S(2)}, u32[]{:S(2)}) collective-permute-start(bf16[128,1152]{1,0:T(8,128)(2,1)} %get-tuple-element.387), channel_id=1, source_target_pairs={{31,0},{0,1},{1,2},{2,3},{3,4},{4,5},{5,6},{6,7},{7,8},{8,9},{9,10... | collective-permute-start | bytes 884744 | tf_op jit(solution)/shard_map/while/body/eval_jaxpr/ppermute | solution.py:10
  9.8 10.2 %collective-permute-start.1 = (f32[128,1152]{1,0:T(8,128)S(1)}, f32[128,1152]{1,0:T(8,128)S(1)}, u32[]{:S(2)}, u32[]{:S(2)}) collective-permute-start(f32[128,1152]{1,0:T(8,128)S(1)} %get-tuple-element.388), channel_id=1, source_target_pairs={{31,0},{0,1},{1,2},{2,3},{3,4},{4,5},{5,6},{6,7},{7,8},{8,9},{9,10... | collective-permute-start | bytes 1769480 | tf_op jit(solution)/shard_map/while/body/eval_jaxpr/ppermute | solution.py:10
  21.0 7.2 %collective-permute-start = (bf16[128,1152]{1,0:T(8,128)(2,1)}, bf16[128,1152]{1,0:T(8,128)(2,1)S(1)}, u32[]{:S(2)}, u32[]{:S(2)}) collective-permute-start(bf16[128,1152]{1,0:T(8,128)(2,1)} %get-tuple-element.387), channel_id=1, source_target_pairs={{31,0},{0,1},{1,2},{2,3},{3,4},{4,5},{5,6},{6,7},{7,8},{8,9},{9,10... | collective-permute-start | bytes 884744 | tf_op jit(solution)/shard_map/while/body/eval_jaxpr/ppermute | solution.py:10
  23.5 10.2 %collective-permute-start.1 = (f32[128,1152]{1,0:T(8,128)S(1)}, f32[128,1152]{1,0:T(8,128)S(1)}, u32[]{:S(2)}, u32[]{:S(2)}) collective-permute-start(f32[128,1152]{1,0:T(8,128)S(1)} %get-tuple-element.388), channel_id=1, source_target_pairs={{31,0},{0,1},{1,2},{2,3},{3,4},{4,5},{5,6},{6,7},{7,8},{8,9},{9,10... | collective-permute-start | bytes 1769480 | tf_op jit(solution)/shard_map/while/body/eval_jaxpr/ppermute | solution.py:10
  34.7 9.3 %collective-permute-start = (bf16[128,1152]{1,0:T(8,128)(2,1)}, bf16[128,1152]{1,0:T(8,128)(2,1)S(1)}, u32[]{:S(2)}, u32[]{:S(2)}) collective-permute-start(bf16[128,1152]{1,0:T(8,128)(2,1)} %get-tuple-element.387), channel_id=1, source_target_pairs={{31,0},{0,1},{1,2},{2,3},{3,4},{4,5},{5,6},{6,7},{7,8},{8,9},{9,10... | collective-permute-start | bytes 884744 | tf_op jit(solution)/shard_map/while/body/eval_jaxpr/ppermute | solution.py:10
  37.2 10.2 %collective-permute-start.1 = (f32[128,1152]{1,0:T(8,128)S(1)}, f32[128,1152]{1,0:T(8,128)S(1)}, u32[]{:S(2)}, u32[]{:S(2)}) collective-permute-start(f32[128,1152]{1,0:T(8,128)S(1)} %get-tuple-element.388), channel_id=1, source_target_pairs={{31,0},{0,1},{1,2},{2,3},{3,4},{4,5},{5,6},{6,7},{7,8},{8,9},{9,10... | collective-permute-start | bytes 1769480 | tf_op jit(solution)/shard_map/while/body/eval_jaxpr/ppermute | solution.py:10
  48.4 11.5 %collective-permute-start = (bf16[128,1152]{1,0:T(8,128)(2,1)}, bf16[128,1152]{1,0:T(8,128)(2,1)S(1)}, u32[]{:S(2)}, u32[]{:S(2)}) collective-permute-start(bf16[128,1152]{1,0:T(8,128)(2,1)} %get-tuple-element.387), channel_id=1, source_target_pairs={{31,0},{0,1},{1,2},{2,3},{3,4},{4,5},{5,6},{6,7},{7,8},{8,9},{9,10... | collective-permute-start | bytes 884744 | tf_op jit(solution)/shard_map/while/body/eval_jaxpr/ppermute | solution.py:10
  51.0 12.2 %collective-permute-start.1 = (f32[128,1152]{1,0:T(8,128)S(1)}, f32[128,1152]{1,0:T(8,128)S(1)}, u32[]{:S(2)}, u32[]{:S(2)}) collective-permute-start(f32[128,1152]{1,0:T(8,128)S(1)} %get-tuple-element.388), channel_id=1, source_target_pairs={{31,0},{0,1},{1,2},{2,3},{3,4},{4,5},{5,6},{6,7},{7,8},{8,9},{9,10... | collective-permute-start | bytes 1769480 | tf_op jit(solution)/shard_map/while/body/eval_jaxpr/ppermute | solution.py:10
  64.2 11.5 %collective-permute-start = (bf16[128,1152]{1,0:T(8,128)(2,1)}, bf16[128,1152]{1,0:T(8,128)(2,1)S(1)}, u32[]{:S(2)}, u32[]{:S(2)}) collective-permute-start(bf16[128,1152]{1,0:T(8,128)(2,1)} %get-tuple-element.387), channel_id=1, source_target_pairs={{31,0},{0,1},{1,2},{2,3},{3,4},{4,5},{5,6},{6,7},{7,8},{8,9},{9,10... | collective-permute-start | bytes 884744 | tf_op jit(solution)/shard_map/while/body/eval_jaxpr/ppermute | solution.py:10
  64.7 14.3 %collective-permute-start.1 = (f32[128,1152]{1,0:T(8,128)S(1)}, f32[128,1152]{1,0:T(8,128)S(1)}, u32[]{:S(2)}, u32[]{:S(2)}) collective-permute-start(f32[128,1152]{1,0:T(8,128)S(1)} %get-tuple-element.388), channel_id=1, source_target_pairs={{31,0},{0,1},{1,2},{2,3},{3,4},{4,5},{5,6},{6,7},{7,8},{8,9},{9,10... | collective-permute-start | bytes 1769480 | tf_op jit(solution)/shard_map/while/body/eval_jaxpr/ppermute | solution.py:10
  80.0 11.5 %collective-permute-start = (bf16[128,1152]{1,0:T(8,128)(2,1)}, bf16[128,1152]{1,0:T(8,128)(2,1)S(1)}, u32[]{:S(2)}, u32[]{:S(2)}) collective-permute-start(bf16[128,1152]{1,0:T(8,128)(2,1)} %get-tuple-element.387), channel_id=1, source_target_pairs={{31,0},{0,1},{1,2},{2,3},{3,4},{4,5},{5,6},{6,7},{7,8},{8,9},{9,10... | collective-permute-start | bytes 884744 | tf_op jit(solution)/shard_map/while/body/eval_jaxpr/ppermute | solution.py:10
  80.1 14.8 %collective-permute-start.1 = (f32[128,1152]{1,0:T(8,128)S(1)}, f32[128,1152]{1,0:T(8,128)S(1)}, u32[]{:S(2)}, u32[]{:S(2)}) collective-permute-start(f32[128,1152]{1,0:T(8,128)S(1)} %get-tuple-element.388), channel_id=1, source_target_pairs={{31,0},{0,1},{1,2},{2,3},{3,4},{4,5},{5,6},{6,7},{7,8},{8,9},{9,10... | collective-permute-start | bytes 1769480 | tf_op jit(solution)/shard_map/while/body/eval_jaxpr/ppermute | solution.py:10
  95.8 11.5 %collective-permute-start = (bf16[128,1152]{1,0:T(8,128)(2,1)}, bf16[128,1152]{1,0:T(8,128)(2,1)S(1)}, u32[]{:S(2)}, u32[]{:S(2)}) collective-permute-start(bf16[128,1152]{1,0:T(8,128)(2,1)} %get-tuple-element.387), channel_id=1, source_target_pairs={{31,0},{0,1},{1,2},{2,3},{3,4},{4,5},{5,6},{6,7},{7,8},{8,9},{9,10... | collective-permute-start | bytes 884744 | tf_op jit(solution)/shard_map/while/body/eval_jaxpr/ppermute | solution.py:10
  95.9 14.8 %collective-permute-start.1 = (f32[128,1152]{1,0:T(8,128)S(1)}, f32[128,1152]{1,0:T(8,128)S(1)}, u32[]{:S(2)}, u32[]{:S(2)}) collective-permute-start(f32[128,1152]{1,0:T(8,128)S(1)} %get-tuple-element.388), channel_id=1, source_target_pairs={{31,0},{0,1},{1,2},{2,3},{3,4},{4,5},{5,6},{6,7},{7,8},{8,9},{9,10... | collective-permute-start | bytes 1769480 | tf_op jit(solution)/shard_map/while/body/eval_jaxpr/ppermute | solution.py:10
  111.6 11.5 %collective-permute-start = (bf16[128,1152]{1,0:T(8,128)(2,1)}, bf16[128,1152]{1,0:T(8,128)(2,1)S(1)}, u32[]{:S(2)}, u32[]{:S(2)}) collective-permute-start(bf16[128,1152]{1,0:T(8,128)(2,1)} %get-tuple-element.387), channel_id=1, source_target_pairs={{31,0},{0,1},{1,2},{2,3},{3,4},{4,5},{5,6},{6,7},{7,8},{8,9},{9,10... | collective-permute-start | bytes 884744 | tf_op jit(solution)/shard_map/while/body/eval_jaxpr/ppermute | solution.py:10
  111.7 14.8 %collective-permute-start.1 = (f32[128,1152]{1,0:T(8,128)S(1)}, f32[128,1152]{1,0:T(8,128)S(1)}, u32[]{:S(2)}, u32[]{:S(2)}) collective-permute-start(f32[128,1152]{1,0:T(8,128)S(1)} %get-tuple-element.388), channel_id=1, source_target_pairs={{31,0},{0,1},{1,2},{2,3},{3,4},{4,5},{5,6},{6,7},{7,8},{8,9},{9,10... | collective-permute-start | bytes 1769480 | tf_op jit(solution)/shard_map/while/body/eval_jaxpr/ppermute | solution.py:10
  127.4 11.5 %collective-permute-start = (bf16[128,1152]{1,0:T(8,128)(2,1)}, bf16[128,1152]{1,0:T(8,128)(2,1)S(1)}, u32[]{:S(2)}, u32[]{:S(2)}) collective-permute-start(bf16[128,1152]{1,0:T(8,128)(2,1)} %get-tuple-element.387), channel_id=1, source_target_pairs={{31,0},{0,1},{1,2},{2,3},{3,4},{4,5},{5,6},{6,7},{7,8},{8,9},{9,10... | collective-permute-start | bytes 884744 | tf_op jit(solution)/shard_map/while/body/eval_jaxpr/ppermute | solution.py:10
  127.5 14.8 %collective-permute-start.1 = (f32[128,1152]{1,0:T(8,128)S(1)}, f32[128,1152]{1,0:T(8,128)S(1)}, u32[]{:S(2)}, u32[]{:S(2)}) collective-permute-start(f32[128,1152]{1,0:T(8,128)S(1)} %get-tuple-element.388), channel_id=1, source_target_pairs={{31,0},{0,1},{1,2},{2,3},{3,4},{4,5},{5,6},{6,7},{7,8},{8,9},{9,10... | collective-permute-start | bytes 1769480 | tf_op jit(solution)/shard_map/while/body/eval_jaxpr/ppermute | solution.py:10
  143.3 11.5 %collective-permute-start = (bf16[128,1152]{1,0:T(8,128)(2,1)}, bf16[128,1152]{1,0:T(8,128)(2,1)S(1)}, u32[]{:S(2)}, u32[]{:S(2)}) collective-permute-start(bf16[128,1152]{1,0:T(8,128)(2,1)} %get-tuple-element.387), channel_id=1, source_target_pairs={{31,0},{0,1},{1,2},{2,3},{3,4},{4,5},{5,6},{6,7},{7,8},{8,9},{9,10... | collective-permute-start | bytes 884744 | tf_op jit(solution)/shard_map/while/body/eval_jaxpr/ppermute | solution.py:10
  143.4 14.8 %collective-permute-start.1 = (f32[128,1152]{1,0:T(8,128)S(1)}, f32[128,1152]{1,0:T(8,128)S(1)}, u32[]{:S(2)}, u32[]{:S(2)}) collective-permute-start(f32[128,1152]{1,0:T(8,128)S(1)} %get-tuple-element.388), channel_id=1, source_target_pairs={{31,0},{0,1},{1,2},{2,3},{3,4},{4,5},{5,6},{6,7},{7,8},{8,9},{9,10... | collective-permute-start | bytes 1769480 | tf_op jit(solution)/shard_map/while/body/eval_jaxpr/ppermute | solution.py:10
  159.1 11.5 %collective-permute-start = (bf16[128,1152]{1,0:T(8,128)(2,1)}, bf16[128,1152]{1,0:T(8,128)(2,1)S(1)}, u32[]{:S(2)}, u32[]{:S(2)}) collective-permute-start(bf16[128,1152]{1,0:T(8,128)(2,1)} %get-tuple-element.387), channel_id=1, source_target_pairs={{31,0},{0,1},{1,2},{2,3},{3,4},{4,5},{5,6},{6,7},{7,8},{8,9},{9,10... | collective-permute-start | bytes 884744 | tf_op jit(solution)/shard_map/while/body/eval_jaxpr/ppermute | solution.py:10
  159.2 14.8 %collective-permute-start.1 = (f32[128,1152]{1,0:T(8,128)S(1)}, f32[128,1152]{1,0:T(8,128)S(1)}, u32[]{:S(2)}, u32[]{:S(2)}) collective-permute-start(f32[128,1152]{1,0:T(8,128)S(1)} %get-tuple-element.388), channel_id=1, source_target_pairs={{31,0},{0,1},{1,2},{2,3},{3,4},{4,5},{5,6},{6,7},{7,8},{8,9},{9,10... | collective-permute-start | bytes 1769480 | tf_op jit(solution)/shard_map/while/body/eval_jaxpr/ppermute | solution.py:10
  174.9 11.5 %collective-permute-start = (bf16[128,1152]{1,0:T(8,128)(2,1)}, bf16[128,1152]{1,0:T(8,128)(2,1)S(1)}, u32[]{:S(2)}, u32[]{:S(2)}) collective-permute-start(bf16[128,1152]{1,0:T(8,128)(2,1)} %get-tuple-element.387), channel_id=1, source_target_pairs={{31,0},{0,1},{1,2},{2,3},{3,4},{4,5},{5,6},{6,7},{7,8},{8,9},{9,10... | collective-permute-start | bytes 884744 | tf_op jit(solution)/shard_map/while/body/eval_jaxpr/ppermute | solution.py:10
  175.0 14.8 %collective-permute-start.1 = (f32[128,1152]{1,0:T(8,128)S(1)}, f32[128,1152]{1,0:T(8,128)S(1)}, u32[]{:S(2)}, u32[]{:S(2)}) collective-permute-start(f32[128,1152]{1,0:T(8,128)S(1)} %get-tuple-element.388), channel_id=1, source_target_pairs={{31,0},{0,1},{1,2},{2,3},{3,4},{4,5},{5,6},{6,7},{7,8},{8,9},{9,10... | collective-permute-start | bytes 1769480 | tf_op jit(solution)/shard_map/while/body/eval_jaxpr/ppermute | solution.py:10
  190.7 11.5 %collective-permute-start = (bf16[128,1152]{1,0:T(8,128)(2,1)}, bf16[128,1152]{1,0:T(8,128)(2,1)S(1)}, u32[]{:S(2)}, u32[]{:S(2)}) collective-permute-start(bf16[128,1152]{1,0:T(8,128)(2,1)} %get-tuple-element.387), channel_id=1, source_target_pairs={{31,0},{0,1},{1,2},{2,3},{3,4},{4,5},{5,6},{6,7},{7,8},{8,9},{9,10... | collective-permute-start | bytes 884744 | tf_op jit(solution)/shard_map/while/body/eval_jaxpr/ppermute | solution.py:10
  190.8 14.8 %collective-permute-start.1 = (f32[128,1152]{1,0:T(8,128)S(1)}, f32[128,1152]{1,0:T(8,128)S(1)}, u32[]{:S(2)}, u32[]{:S(2)}) collective-permute-start(f32[128,1152]{1,0:T(8,128)S(1)} %get-tuple-element.388), channel_id=1, source_target_pairs={{31,0},{0,1},{1,2},{2,3},{3,4},{4,5},{5,6},{6,7},{7,8},{8,9},{9,10... | collective-permute-start | bytes 1769480 | tf_op jit(solution)/shard_map/while/body/eval_jaxpr/ppermute | solution.py:10
  206.6 11.5 %collective-permute-start = (bf16[128,1152]{1,0:T(8,128)(2,1)}, bf16[128,1152]{1,0:T(8,128)(2,1)S(1)}, u32[]{:S(2)}, u32[]{:S(2)}) collective-permute-start(bf16[128,1152]{1,0:T(8,128)(2,1)} %get-tuple-element.387), channel_id=1, source_target_pairs={{31,0},{0,1},{1,2},{2,3},{3,4},{4,5},{5,6},{6,7},{7,8},{8,9},{9,10... | collective-permute-start | bytes 884744 | tf_op jit(solution)/shard_map/while/body/eval_jaxpr/ppermute | solution.py:10
  206.7 14.8 %collective-permute-start.1 = (f32[128,1152]{1,0:T(8,128)S(1)}, f32[128,1152]{1,0:T(8,128)S(1)}, u32[]{:S(2)}, u32[]{:S(2)}) collective-permute-start(f32[128,1152]{1,0:T(8,128)S(1)} %get-tuple-element.388), channel_id=1, source_target_pairs={{31,0},{0,1},{1,2},{2,3},{3,4},{4,5},{5,6},{6,7},{7,8},{8,9},{9,10... | collective-permute-start | bytes 1769480 | tf_op jit(solution)/shard_map/while/body/eval_jaxpr/ppermute | solution.py:10
  222.4 11.5 %collective-permute-start = (bf16[128,1152]{1,0:T(8,128)(2,1)}, bf16[128,1152]{1,0:T(8,128)(2,1)S(1)}, u32[]{:S(2)}, u32[]{:S(2)}) collective-permute-start(bf16[128,1152]{1,0:T(8,128)(2,1)} %get-tuple-element.387), channel_id=1, source_target_pairs={{31,0},{0,1},{1,2},{2,3},{3,4},{4,5},{5,6},{6,7},{7,8},{8,9},{9,10... | collective-permute-start | bytes 884744 | tf_op jit(solution)/shard_map/while/body/eval_jaxpr/ppermute | solution.py:10
  222.5 14.8 %collective-permute-start.1 = (f32[128,1152]{1,0:T(8,128)S(1)}, f32[128,1152]{1,0:T(8,128)S(1)}, u32[]{:S(2)}, u32[]{:S(2)}) collective-permute-start(f32[128,1152]{1,0:T(8,128)S(1)} %get-tuple-element.388), channel_id=1, source_target_pairs={{31,0},{0,1},{1,2},{2,3},{3,4},{4,5},{5,6},{6,7},{7,8},{8,9},{9,10... | collective-permute-start | bytes 1769480 | tf_op jit(solution)/shard_map/while/body/eval_jaxpr/ppermute | solution.py:10
  238.2 11.5 %collective-permute-start = (bf16[128,1152]{1,0:T(8,128)(2,1)}, bf16[128,1152]{1,0:T(8,128)(2,1)S(1)}, u32[]{:S(2)}, u32[]{:S(2)}) collective-permute-start(bf16[128,1152]{1,0:T(8,128)(2,1)} %get-tuple-element.387), channel_id=1, source_target_pairs={{31,0},{0,1},{1,2},{2,3},{3,4},{4,5},{5,6},{6,7},{7,8},{8,9},{9,10... | collective-permute-start | bytes 884744 | tf_op jit(solution)/shard_map/while/body/eval_jaxpr/ppermute | solution.py:10
  238.3 14.8 %collective-permute-start.1 = (f32[128,1152]{1,0:T(8,128)S(1)}, f32[128,1152]{1,0:T(8,128)S(1)}, u32[]{:S(2)}, u32[]{:S(2)}) collective-permute-start(f32[128,1152]{1,0:T(8,128)S(1)} %get-tuple-element.388), channel_id=1, source_target_pairs={{31,0},{0,1},{1,2},{2,3},{3,4},{4,5},{5,6},{6,7},{7,8},{8,9},{9,10... | collective-permute-start | bytes 1769480 | tf_op jit(solution)/shard_map/while/body/eval_jaxpr/ppermute | solution.py:10
  254.0 11.5 %collective-permute-start = (bf16[128,1152]{1,0:T(8,128)(2,1)}, bf16[128,1152]{1,0:T(8,128)(2,1)S(1)}, u32[]{:S(2)}, u32[]{:S(2)}) collective-permute-start(bf16[128,1152]{1,0:T(8,128)(2,1)} %get-tuple-element.387), channel_id=1, source_target_pairs={{31,0},{0,1},{1,2},{2,3},{3,4},{4,5},{5,6},{6,7},{7,8},{8,9},{9,10... | collective-permute-start | bytes 884744 | tf_op jit(solution)/shard_map/while/body/eval_jaxpr/ppermute | solution.py:10
  254.1 14.8 %collective-permute-start.1 = (f32[128,1152]{1,0:T(8,128)S(1)}, f32[128,1152]{1,0:T(8,128)S(1)}, u32[]{:S(2)}, u32[]{:S(2)}) collective-permute-start(f32[128,1152]{1,0:T(8,128)S(1)} %get-tuple-element.388), channel_id=1, source_target_pairs={{31,0},{0,1},{1,2},{2,3},{3,4},{4,5},{5,6},{6,7},{7,8},{8,9},{9,10... | collective-permute-start | bytes 1769480 | tf_op jit(solution)/shard_map/while/body/eval_jaxpr/ppermute | solution.py:10
  269.9 11.5 %collective-permute-start = (bf16[128,1152]{1,0:T(8,128)(2,1)}, bf16[128,1152]{1,0:T(8,128)(2,1)S(1)}, u32[]{:S(2)}, u32[]{:S(2)}) collective-permute-start(bf16[128,1152]{1,0:T(8,128)(2,1)} %get-tuple-element.387), channel_id=1, source_target_pairs={{31,0},{0,1},{1,2},{2,3},{3,4},{4,5},{5,6},{6,7},{7,8},{8,9},{9,10... | collective-permute-start | bytes 884744 | tf_op jit(solution)/shard_map/while/body/eval_jaxpr/ppermute | solution.py:10
  269.9 14.8 %collective-permute-start.1 = (f32[128,1152]{1,0:T(8,128)S(1)}, f32[128,1152]{1,0:T(8,128)S(1)}, u32[]{:S(2)}, u32[]{:S(2)}) collective-permute-start(f32[128,1152]{1,0:T(8,128)S(1)} %get-tuple-element.388), channel_id=1, source_target_pairs={{31,0},{0,1},{1,2},{2,3},{3,4},{4,5},{5,6},{6,7},{7,8},{8,9},{9,10... | collective-permute-start | bytes 1769480 | tf_op jit(solution)/shard_map/while/body/eval_jaxpr/ppermute | solution.py:10
  285.7 11.5 %collective-permute-start = (bf16[128,1152]{1,0:T(8,128)(2,1)}, bf16[128,1152]{1,0:T(8,128)(2,1)S(1)}, u32[]{:S(2)}, u32[]{:S(2)}) collective-permute-start(bf16[128,1152]{1,0:T(8,128)(2,1)} %get-tuple-element.387), channel_id=1, source_target_pairs={{31,0},{0,1},{1,2},{2,3},{3,4},{4,5},{5,6},{6,7},{7,8},{8,9},{9,10... | collective-permute-start | bytes 884744 | tf_op jit(solution)/shard_map/while/body/eval_jaxpr/ppermute | solution.py:10
  285.8 14.8 %collective-permute-start.1 = (f32[128,1152]{1,0:T(8,128)S(1)}, f32[128,1152]{1,0:T(8,128)S(1)}, u32[]{:S(2)}, u32[]{:S(2)}) collective-permute-start(f32[128,1152]{1,0:T(8,128)S(1)} %get-tuple-element.388), channel_id=1, source_target_pairs={{31,0},{0,1},{1,2},{2,3},{3,4},{4,5},{5,6},{6,7},{7,8},{8,9},{9,10... | collective-permute-start | bytes 1769480 | tf_op jit(solution)/shard_map/while/body/eval_jaxpr/ppermute | solution.py:10
  301.5 11.5 %collective-permute-start = (bf16[128,1152]{1,0:T(8,128)(2,1)}, bf16[128,1152]{1,0:T(8,128)(2,1)S(1)}, u32[]{:S(2)}, u32[]{:S(2)}) collective-permute-start(bf16[128,1152]{1,0:T(8,128)(2,1)} %get-tuple-element.387), channel_id=1, source_target_pairs={{31,0},{0,1},{1,2},{2,3},{3,4},{4,5},{5,6},{6,7},{7,8},{8,9},{9,10... | collective-permute-start | bytes 884744 | tf_op jit(solution)/shard_map/while/body/eval_jaxpr/ppermute | solution.py:10
  301.6 14.8 %collective-permute-start.1 = (f32[128,1152]{1,0:T(8,128)S(1)}, f32[128,1152]{1,0:T(8,128)S(1)}, u32[]{:S(2)}, u32[]{:S(2)}) collective-permute-start(f32[128,1152]{1,0:T(8,128)S(1)} %get-tuple-element.388), channel_id=1, source_target_pairs={{31,0},{0,1},{1,2},{2,3},{3,4},{4,5},{5,6},{6,7},{7,8},{8,9},{9,10... | collective-permute-start | bytes 1769480 | tf_op jit(solution)/shard_map/while/body/eval_jaxpr/ppermute | solution.py:10
  317.3 11.5 %collective-permute-start = (bf16[128,1152]{1,0:T(8,128)(2,1)}, bf16[128,1152]{1,0:T(8,128)(2,1)S(1)}, u32[]{:S(2)}, u32[]{:S(2)}) collective-permute-start(bf16[128,1152]{1,0:T(8,128)(2,1)} %get-tuple-element.387), channel_id=1, source_target_pairs={{31,0},{0,1},{1,2},{2,3},{3,4},{4,5},{5,6},{6,7},{7,8},{8,9},{9,10... | collective-permute-start | bytes 884744 | tf_op jit(solution)/shard_map/while/body/eval_jaxpr/ppermute | solution.py:10
  317.4 14.8 %collective-permute-start.1 = (f32[128,1152]{1,0:T(8,128)S(1)}, f32[128,1152]{1,0:T(8,128)S(1)}, u32[]{:S(2)}, u32[]{:S(2)}) collective-permute-start(f32[128,1152]{1,0:T(8,128)S(1)} %get-tuple-element.388), channel_id=1, source_target_pairs={{31,0},{0,1},{1,2},{2,3},{3,4},{4,5},{5,6},{6,7},{7,8},{8,9},{9,10... | collective-permute-start | bytes 1769480 | tf_op jit(solution)/shard_map/while/body/eval_jaxpr/ppermute | solution.py:10
  333.1 11.5 %collective-permute-start = (bf16[128,1152]{1,0:T(8,128)(2,1)}, bf16[128,1152]{1,0:T(8,128)(2,1)S(1)}, u32[]{:S(2)}, u32[]{:S(2)}) collective-permute-start(bf16[128,1152]{1,0:T(8,128)(2,1)} %get-tuple-element.387), channel_id=1, source_target_pairs={{31,0},{0,1},{1,2},{2,3},{3,4},{4,5},{5,6},{6,7},{7,8},{8,9},{9,10... | collective-permute-start | bytes 884744 | tf_op jit(solution)/shard_map/while/body/eval_jaxpr/ppermute | solution.py:10
  333.2 14.8 %collective-permute-start.1 = (f32[128,1152]{1,0:T(8,128)S(1)}, f32[128,1152]{1,0:T(8,128)S(1)}, u32[]{:S(2)}, u32[]{:S(2)}) collective-permute-start(f32[128,1152]{1,0:T(8,128)S(1)} %get-tuple-element.388), channel_id=1, source_target_pairs={{31,0},{0,1},{1,2},{2,3},{3,4},{4,5},{5,6},{6,7},{7,8},{8,9},{9,10... | collective-permute-start | bytes 1769480 | tf_op jit(solution)/shard_map/while/body/eval_jaxpr/ppermute | solution.py:10
  349.0 11.5 %collective-permute-start = (bf16[128,1152]{1,0:T(8,128)(2,1)}, bf16[128,1152]{1,0:T(8,128)(2,1)S(1)}, u32[]{:S(2)}, u32[]{:S(2)}) collective-permute-start(bf16[128,1152]{1,0:T(8,128)(2,1)} %get-tuple-element.387), channel_id=1, source_target_pairs={{31,0},{0,1},{1,2},{2,3},{3,4},{4,5},{5,6},{6,7},{7,8},{8,9},{9,10... | collective-permute-start | bytes 884744 | tf_op jit(solution)/shard_map/while/body/eval_jaxpr/ppermute | solution.py:10
  349.1 14.8 %collective-permute-start.1 = (f32[128,1152]{1,0:T(8,128)S(1)}, f32[128,1152]{1,0:T(8,128)S(1)}, u32[]{:S(2)}, u32[]{:S(2)}) collective-permute-start(f32[128,1152]{1,0:T(8,128)S(1)} %get-tuple-element.388), channel_id=1, source_target_pairs={{31,0},{0,1},{1,2},{2,3},{3,4},{4,5},{5,6},{6,7},{7,8},{8,9},{9,10... | collective-permute-start | bytes 1769480 | tf_op jit(solution)/shard_map/while/body/eval_jaxpr/ppermute | solution.py:10
  364.8 11.5 %collective-permute-start = (bf16[128,1152]{1,0:T(8,128)(2,1)}, bf16[128,1152]{1,0:T(8,128)(2,1)S(1)}, u32[]{:S(2)}, u32[]{:S(2)}) collective-permute-start(bf16[128,1152]{1,0:T(8,128)(2,1)} %get-tuple-element.387), channel_id=1, source_target_pairs={{31,0},{0,1},{1,2},{2,3},{3,4},{4,5},{5,6},{6,7},{7,8},{8,9},{9,10... | collective-permute-start | bytes 884744 | tf_op jit(solution)/shard_map/while/body/eval_jaxpr/ppermute | solution.py:10
  364.9 14.8 %collective-permute-start.1 = (f32[128,1152]{1,0:T(8,128)S(1)}, f32[128,1152]{1,0:T(8,128)S(1)}, u32[]{:S(2)}, u32[]{:S(2)}) collective-permute-start(f32[128,1152]{1,0:T(8,128)S(1)} %get-tuple-element.388), channel_id=1, source_target_pairs={{31,0},{0,1},{1,2},{2,3},{3,4},{4,5},{5,6},{6,7},{7,8},{8,9},{9,10... | collective-permute-start | bytes 1769480 | tf_op jit(solution)/shard_map/while/body/eval_jaxpr/ppermute | solution.py:10
  380.6 11.5 %collective-permute-start = (bf16[128,1152]{1,0:T(8,128)(2,1)}, bf16[128,1152]{1,0:T(8,128)(2,1)S(1)}, u32[]{:S(2)}, u32[]{:S(2)}) collective-permute-start(bf16[128,1152]{1,0:T(8,128)(2,1)} %get-tuple-element.387), channel_id=1, source_target_pairs={{31,0},{0,1},{1,2},{2,3},{3,4},{4,5},{5,6},{6,7},{7,8},{8,9},{9,10... | collective-permute-start | bytes 884744 | tf_op jit(solution)/shard_map/while/body/eval_jaxpr/ppermute | solution.py:10
  380.7 14.8 %collective-permute-start.1 = (f32[128,1152]{1,0:T(8,128)S(1)}, f32[128,1152]{1,0:T(8,128)S(1)}, u32[]{:S(2)}, u32[]{:S(2)}) collective-permute-start(f32[128,1152]{1,0:T(8,128)S(1)} %get-tuple-element.388), channel_id=1, source_target_pairs={{31,0},{0,1},{1,2},{2,3},{3,4},{4,5},{5,6},{6,7},{7,8},{8,9},{9,10... | collective-permute-start | bytes 1769480 | tf_op jit(solution)/shard_map/while/body/eval_jaxpr/ppermute | solution.py:10
  396.4 11.5 %collective-permute-start = (bf16[128,1152]{1,0:T(8,128)(2,1)}, bf16[128,1152]{1,0:T(8,128)(2,1)S(1)}, u32[]{:S(2)}, u32[]{:S(2)}) collective-permute-start(bf16[128,1152]{1,0:T(8,128)(2,1)} %get-tuple-element.387), channel_id=1, source_target_pairs={{31,0},{0,1},{1,2},{2,3},{3,4},{4,5},{5,6},{6,7},{7,8},{8,9},{9,10... | collective-permute-start | bytes 884744 | tf_op jit(solution)/shard_map/while/body/eval_jaxpr/ppermute | solution.py:10
  396.5 14.8 %collective-permute-start.1 = (f32[128,1152]{1,0:T(8,128)S(1)}, f32[128,1152]{1,0:T(8,128)S(1)}, u32[]{:S(2)}, u32[]{:S(2)}) collective-permute-start(f32[128,1152]{1,0:T(8,128)S(1)} %get-tuple-element.388), channel_id=1, source_target_pairs={{31,0},{0,1},{1,2},{2,3},{3,4},{4,5},{5,6},{6,7},{7,8},{8,9},{9,10... | collective-permute-start | bytes 1769480 | tf_op jit(solution)/shard_map/while/body/eval_jaxpr/ppermute | solution.py:10
  412.3 11.5 %collective-permute-start = (bf16[128,1152]{1,0:T(8,128)(2,1)}, bf16[128,1152]{1,0:T(8,128)(2,1)S(1)}, u32[]{:S(2)}, u32[]{:S(2)}) collective-permute-start(bf16[128,1152]{1,0:T(8,128)(2,1)} %get-tuple-element.387), channel_id=1, source_target_pairs={{31,0},{0,1},{1,2},{2,3},{3,4},{4,5},{5,6},{6,7},{7,8},{8,9},{9,10... | collective-permute-start | bytes 884744 | tf_op jit(solution)/shard_map/while/body/eval_jaxpr/ppermute | solution.py:10
  412.4 14.8 %collective-permute-start.1 = (f32[128,1152]{1,0:T(8,128)S(1)}, f32[128,1152]{1,0:T(8,128)S(1)}, u32[]{:S(2)}, u32[]{:S(2)}) collective-permute-start(f32[128,1152]{1,0:T(8,128)S(1)} %get-tuple-element.388), channel_id=1, source_target_pairs={{31,0},{0,1},{1,2},{2,3},{3,4},{4,5},{5,6},{6,7},{7,8},{8,9},{9,10... | collective-permute-start | bytes 1769480 | tf_op jit(solution)/shard_map/while/body/eval_jaxpr/ppermute | solution.py:10
  428.1 11.5 %collective-permute-start = (bf16[128,1152]{1,0:T(8,128)(2,1)}, bf16[128,1152]{1,0:T(8,128)(2,1)S(1)}, u32[]{:S(2)}, u32[]{:S(2)}) collective-permute-start(bf16[128,1152]{1,0:T(8,128)(2,1)} %get-tuple-element.387), channel_id=1, source_target_pairs={{31,0},{0,1},{1,2},{2,3},{3,4},{4,5},{5,6},{6,7},{7,8},{8,9},{9,10... | collective-permute-start | bytes 884744 | tf_op jit(solution)/shard_map/while/body/eval_jaxpr/ppermute | solution.py:10
  428.2 14.8 %collective-permute-start.1 = (f32[128,1152]{1,0:T(8,128)S(1)}, f32[128,1152]{1,0:T(8,128)S(1)}, u32[]{:S(2)}, u32[]{:S(2)}) collective-permute-start(f32[128,1152]{1,0:T(8,128)S(1)} %get-tuple-element.388), channel_id=1, source_target_pairs={{31,0},{0,1},{1,2},{2,3},{3,4},{4,5},{5,6},{6,7},{7,8},{8,9},{9,10... | collective-permute-start | bytes 1769480 | tf_op jit(solution)/shard_map/while/body/eval_jaxpr/ppermute | solution.py:10
  443.9 11.5 %collective-permute-start = (bf16[128,1152]{1,0:T(8,128)(2,1)}, bf16[128,1152]{1,0:T(8,128)(2,1)S(1)}, u32[]{:S(2)}, u32[]{:S(2)}) collective-permute-start(bf16[128,1152]{1,0:T(8,128)(2,1)} %get-tuple-element.387), channel_id=1, source_target_pairs={{31,0},{0,1},{1,2},{2,3},{3,4},{4,5},{5,6},{6,7},{7,8},{8,9},{9,10... | collective-permute-start | bytes 884744 | tf_op jit(solution)/shard_map/while/body/eval_jaxpr/ppermute | solution.py:10
  444.0 14.8 %collective-permute-start.1 = (f32[128,1152]{1,0:T(8,128)S(1)}, f32[128,1152]{1,0:T(8,128)S(1)}, u32[]{:S(2)}, u32[]{:S(2)}) collective-permute-start(f32[128,1152]{1,0:T(8,128)S(1)} %get-tuple-element.388), channel_id=1, source_target_pairs={{31,0},{0,1},{1,2},{2,3},{3,4},{4,5},{5,6},{6,7},{7,8},{8,9},{9,10... | collective-permute-start | bytes 1769480 | tf_op jit(solution)/shard_map/while/body/eval_jaxpr/ppermute | solution.py:10
  459.7 11.5 %collective-permute-start = (bf16[128,1152]{1,0:T(8,128)(2,1)}, bf16[128,1152]{1,0:T(8,128)(2,1)S(1)}, u32[]{:S(2)}, u32[]{:S(2)}) collective-permute-start(bf16[128,1152]{1,0:T(8,128)(2,1)} %get-tuple-element.387), channel_id=1, source_target_pairs={{31,0},{0,1},{1,2},{2,3},{3,4},{4,5},{5,6},{6,7},{7,8},{8,9},{9,10... | collective-permute-start | bytes 884744 | tf_op jit(solution)/shard_map/while/body/eval_jaxpr/ppermute | solution.py:10
  459.8 14.8 %collective-permute-start.1 = (f32[128,1152]{1,0:T(8,128)S(1)}, f32[128,1152]{1,0:T(8,128)S(1)}, u32[]{:S(2)}, u32[]{:S(2)}) collective-permute-start(f32[128,1152]{1,0:T(8,128)S(1)} %get-tuple-element.388), channel_id=1, source_target_pairs={{31,0},{0,1},{1,2},{2,3},{3,4},{4,5},{5,6},{6,7},{7,8},{8,9},{9,10... | collective-permute-start | bytes 1769480 | tf_op jit(solution)/shard_map/while/body/eval_jaxpr/ppermute | solution.py:10
  475.6 11.5 %collective-permute-start = (bf16[128,1152]{1,0:T(8,128)(2,1)}, bf16[128,1152]{1,0:T(8,128)(2,1)S(1)}, u32[]{:S(2)}, u32[]{:S(2)}) collective-permute-start(bf16[128,1152]{1,0:T(8,128)(2,1)} %get-tuple-element.387), channel_id=1, source_target_pairs={{31,0},{0,1},{1,2},{2,3},{3,4},{4,5},{5,6},{6,7},{7,8},{8,9},{9,10... | collective-permute-start | bytes 884744 | tf_op jit(solution)/shard_map/while/body/eval_jaxpr/ppermute | solution.py:10
  475.6 14.8 %collective-permute-start.1 = (f32[128,1152]{1,0:T(8,128)S(1)}, f32[128,1152]{1,0:T(8,128)S(1)}, u32[]{:S(2)}, u32[]{:S(2)}) collective-permute-start(f32[128,1152]{1,0:T(8,128)S(1)} %get-tuple-element.388), channel_id=1, source_target_pairs={{31,0},{0,1},{1,2},{2,3},{3,4},{4,5},{5,6},{6,7},{7,8},{8,9},{9,10... | collective-permute-start | bytes 1769480 | tf_op jit(solution)/shard_map/while/body/eval_jaxpr/ppermute | solution.py:10
  491.9 11.3 %collective-permute-start.2 = (bf16[128,1152]{1,0:T(8,128)(2,1)S(1)}, bf16[128,1152]{1,0:T(8,128)(2,1)S(1)}, u32[]{:S(2)}, u32[]{:S(2)}) collective-permute-start(bf16[128,1152]{1,0:T(8,128)(2,1)S(1)} %convert_element_type.28), channel_id=1, source_target_pairs={{31,0},{0,1},{1,2},{2,3},{3,4},{4,5},{5,6},{6,7},{7,8},{8,9},{9,10... | collective-permute-start | bytes 884744 | tf_op jit(solution)/shard_map/ppermute | solution.py:10
  (2 other events, 1.9 us)
where the time goes:
time: 511 us; the launch traced here: 504 us
  waiting for transfers between devices  339 us (66%)
  matrix products  112 us (22%)
  local copies, waits for them, and re-layouts  22.8 us (4%)
  starting transfers between devices  20.9 us (4%)
  other arithmetic  5.16 us (1%)
    ppermute x63, waiting for transfers between devices, passed_along(): return lax.ppermute(block, axis, route)  339 us
    dot_general x32, matrix products, submatrix_weight(): lax.dot_general(first_factor_matrix, second_factor_matrix, (((1,), (1,)),...  50.5 us
    dot_general x32, matrix products, submatrix_penalty_entries(): jnp.dot(match_weight_factor, submatrix_portion, preferred_element_type=jn...  32.5 us
    dot_general x32, matrix products, text_terms(): lax.dot_general(match_weight_factor, picture_gradient_total, (((0,), (0,)...  29.5 us
    while x31, local copies, waits for them, and re-layouts  22.3 us
    ppermute x63, starting transfers between devices, passed_along(): return lax.ppermute(block, axis, route)  20.9 us
  transfers between devices with their start and end apart: 63, of which 35 were waited for; matrix products, arithmetic and copies ran while one was open for 21% of the time, Pallas kernels for 0%

commit v1 on v0

v1 whole, which is shorter than its diff:
```python
import jax
import jax.numpy as jnp
from jax import lax
from jax.sharding import PartitionSpec as P

BF16 = jnp.bfloat16
F32 = jnp.float32
RING = 8
PLANE = 4


def along_z(rows, distance):
    route = [
        (z * PLANE + q, ((z + distance) % RING) * PLANE + q)
        for z in range(RING)
        for q in range(PLANE)
    ]
    return lax.ppermute(rows, "blk", route)


def across_x(rows):
    return lax.ppermute(rows, "blk", [(i, i ^ 2) for i in range(RING * PLANE)])


def across_core(rows):
    return lax.ppermute(rows, "blk", [(i, i ^ 1) for i in range(RING * PLANE)])


def normalize(feats):
    scale = 1.0 / jnp.sqrt(jnp.sum(feats * feats, axis=1, keepdims=True) + 1e-06)
    return (feats * scale, scale)


def back_norm(hat, scale, grad):
    return scale * (grad - hat * jnp.sum(hat * grad, axis=1, keepdims=True))


def plane_rows(rows):
    beside = across_x(rows)
    return jnp.concatenate([rows, across_core(rows), beside, across_core(beside)], 0)


def scores(mine, block, sharpness, shift):
    dots = lax.dot_general(
        mine, block, (((1,), (1,)), ((), ())), preferred_element_type=F32
    )
    return sharpness * dots + shift


def away_terms(mine, block, sharpness, shift, with_loss):
    logits = scores(mine, block, sharpness, shift)
    coeff = (jax.nn.sigmoid(logits) * sharpness).astype(BF16)
    grad = jnp.dot(coeff, block, preferred_element_type=F32)
    loss = jnp.sum(jax.nn.softplus(logits), axis=1) if with_loss else None
    return grad, loss


def home_terms(mine, block, sharpness, shift, with_loss):
    logits = scores(mine, block, sharpness, shift)
    n = block.shape[0]
    row = lax.broadcasted_iota(jnp.int32, logits.shape, 0)
    col = lax.broadcasted_iota(jnp.int32, logits.shape, 1)
    sign = jnp.where(row == col, F32(1.0), F32(-1.0))
    coeff = (-sign * jax.nn.sigmoid(-sign * logits) * sharpness).astype(BF16)
    grad = jnp.dot(coeff, block, preferred_element_type=F32)
    loss = jnp.sum(jax.nn.softplus(-sign * logits), axis=1) if with_loss else None
    return grad, loss


def gather_z(rows):
    half = rows.shape[0] // 2
    right = left = rows
    steps = []
    for _ in range(RING // 2 - 1):
        right, left = along_z(right, 1), along_z(left, -1)
        steps.append((right, left))
    steps.append((along_z(right[:half], 1), along_z(left[half:], -1)))
    return steps


def side(mine, own, steps, sharpness, shift, with_loss):
    grad, loss = home_terms(mine, own, sharpness, shift, with_loss)
    for pair in steps:
        more, more_loss = away_terms(
            mine, jnp.concatenate(pair, 0), sharpness, shift, with_loss
        )
        grad = grad + more
        if with_loss:
            loss = loss + more_loss
    return grad, loss


def sum_over_plane(part, n, sent_as):
    part = part.reshape((4, n) + part.shape[1:])
    for_core = part[1::2].astype(sent_as)
    kept = part[0::2] + across_core(for_core).astype(F32)
    return kept[0] + across_x(kept[1].astype(sent_as)).astype(F32)


def body(pictures, captions, sharpness_scale, offset_shift_vector):
    sharpness, shift = sharpness_scale[0], offset_shift_vector[0]
    n = pictures.shape[0]
    text_hat, text_scale = normalize(captions)
    text_low = text_hat.astype(BF16)
    image_hat, image_scale = normalize(pictures)
    image_low = image_hat.astype(BF16)

    text_steps = gather_z(text_low)
    images = plane_rows(image_low)
    image_steps = gather_z(image_low)
    texts = plane_rows(text_low)

    part_image, part_loss = side(images, text_low, text_steps, sharpness, shift, True)
    loss_rows = sum_over_plane(part_loss, n, F32)
    grad_image = back_norm(image_hat, image_scale, sum_over_plane(part_image, n, BF16))

    part_text, _ = side(texts, image_low, image_steps, sharpness, shift, False)
    grad_text = back_norm(text_hat, text_scale, sum_over_plane(part_text, n, BF16))
    return (loss_rows, grad_image, grad_text)


def solution(mesh):
    in_specs = (P(("group", "blk"), None), P(("group", "blk"), None), P(), P())
    out_specs = (P(("group", "blk")), P(("group", "blk"), None), P(("group", "blk"), None))
    return jax.shard_map(body, mesh=mesh, in_specs=in_specs, out_specs=out_specs, check_vma=False)
```

time: 511 us -> 132 us (0.26); the launches traced: 504 us -> 132 us
  waiting for transfers between devices: 339 us -> 22.1 us
  matrix products: 112 us -> 37.9 us
  starting transfers between devices: 20.9 us -> 40.5 us
    ppermute x63 -> x28, waiting for transfers between devices: 339 us -> 22.1 us  [the longest x5 11.2 us: across_x(): return lax.ppermute(rows, 'blk', [(i, i ^ 2) for i in range(RING * PLANE)])]
    dot_general x96 -> x15, matrix products: 112 us -> 37.9 us  [the longest x8 25.9 us: away_terms(): grad = jnp.dot(coeff, block, preferred_element_type=F32)]
    while x31 -> x0, local copies, waits for them, and re-layouts: 22.3 us -> none
    ppermute x63 -> x28, starting transfers between devices: 20.9 us -> 40.5 us  [the longest x16 24 us: along_z(): return lax.ppermute(rows, 'blk', route)]
    unnamed x6 -> x70, local copies, waits for them, and re-layouts: 0.52 us -> 7.16 us
    slice x0 -> x8, local copies, waits for them, and re-layouts: none -> 6.63 us  [the longest x4 5.1 us: gather_z(): steps.append((along_z(right[:half], 1), along_z(left[half:], -1)))]
    concatenate x0 -> x8, local copies, waits for them, and re-layouts: none -> 5.68 us  [side(): jnp.concatenate(pair, 0)]
  transfers between devices with their start and end apart: 63 -> 28, of which waited for: 35 -> 5; matrix products, arithmetic and copies ran while one was open for 21% -> 47% of each run, Pallas kernels for 0% -> 0%
where the time goes in v1:
time: 132 us
  starting transfers between devices  40.5 us (31%)
  matrix products  37.9 us (29%)
  waiting for transfers between devices  22.1 us (17%)
  local copies, waits for them, and re-layouts  19.6 us (15%)
  other arithmetic  8.91 us (7%)
  between operations  2.56 us (2%)
    dot_general x8, matrix products, away_terms(): grad = jnp.dot(coeff, block, preferred_element_type=F32)  25.9 us
    ppermute x16, starting transfers between devices, along_z(): return lax.ppermute(rows, 'blk', route)  24 us
    ppermute x7, starting transfers between devices, across_core(): return lax.ppermute(rows, 'blk', [(i, i ^ 1) for i in range(RING * PLANE)])  11.2 us
    ppermute x5, waiting for transfers between devices, across_x(): return lax.ppermute(rows, 'blk', [(i, i ^ 2) for i in range(RING * PLANE)])  11.2 us
    ppermute x16, waiting for transfers between devices, along_z(): return lax.ppermute(rows, 'blk', route)  10.9 us
    dot_general x5, matrix products, scores(): lax.dot_general(mine, block, (((1,), (1,)), ((), ())), preferred_element_...  7.64 us
    unnamed x70, local copies, waits for them, and re-layouts  7.16 us
    concatenate x8, local copies, waits for them, and re-layouts, side(): jnp.concatenate(pair, 0)  5.68 us
  transfers between devices with their start and end apart: 28, of which 5 were waited for; matrix products, arithmetic and copies ran while one was open for 47% of the time, Pallas kernels for 0%

profile of v1, /device:TPU:1, one launch (start us, length us, event | category | flops | bytes accessed | tf_op | source)
XLA Modules:
  0.0 131.5 jit_solution(14519819099891920630)
XLA Ops:
  0.6 1.2 multiply_reduce_fusion.3
  1.9 1.2 multiply_convert_fusion.4
  3.1 2.5 %collective-permute-start.18 = (bf16[128,1152]{1,0:T(8,128)(2,1)S(1)}, bf16[128,1152]{1,0:T(8,128)(2,1)S(1)}, u32[]{:S(2)}, u32[]{:S(2)}) collective-permute-start(bf16[128,1152]{1,0:T(8,128)(2,1)S(1)} %multiply_convert_fusion.4), channel_id=1, source_target_pairs={{0,4},{1,5},{2,6},{3,7},{4,8},{5,9},{6,10},{7,11},{8,12},{9,13},{1... | collective-permute-start | bytes 884744 | tf_op jit(solution)/shard_map/ppermute | solution.py:18
  5.6 1.2 multiply_reduce_fusion.2
  6.9 1.7 %collective-permute-start.3 = (bf16[128,1152]{1,0:T(8,128)(2,1)S(1)}, bf16[128,1152]{1,0:T(8,128)(2,1)S(1)}, u32[]{:S(2)}, u32[]{:S(2)}) collective-permute-start(bf16[128,1152]{1,0:T(8,128)(2,1)S(1)} %multiply_convert_fusion.3), channel_id=1, source_target_pairs={{0,4},{1,5},{2,6},{3,7},{4,8},{5,9},{6,10},{7,11},{8,12},{9,13},{1... | collective-permute-start | bytes 884744 | tf_op jit(solution)/shard_map/ppermute | solution.py:18
  8.7 1.2 collective-permute-start.16
  9.9 1.5 %collective-permute-start.15 = (bf16[128,1152]{1,0:T(8,128)(2,1)S(1)}, bf16[128,1152]{1,0:T(8,128)(2,1)S(1)}, u32[]{:S(2)}, u32[]{:S(2)}) collective-permute-start(bf16[128,1152]{1,0:T(8,128)(2,1)S(1)} %multiply_convert_fusion.3), channel_id=1, source_target_pairs={{0,1},{1,0},{2,3},{3,2},{4,5},{5,4},{6,7},{7,6},{8,9},{9,8},{10,11... | collective-permute-start | bytes 884744 | tf_op jit(solution)/shard_map/ppermute | solution.py:26
  11.4 1.9 %collective-permute-start.19 = (bf16[128,1152]{1,0:T(8,128)(2,1)S(1)}, bf16[128,1152]{1,0:T(8,128)(2,1)S(1)}, u32[]{:S(2)}, u32[]{:S(2)}) collective-permute-start(bf16[128,1152]{1,0:T(8,128)(2,1)S(1)} %multiply_convert_fusion.4), channel_id=1, source_target_pairs={{0,28},{1,29},{2,30},{3,31},{4,0},{5,1},{6,2},{7,3},{8,4},{9,5},{1... | collective-permute-start | bytes 884744 | tf_op jit(solution)/shard_map/ppermute | solution.py:18
  14.6 1.7 %collective-permute-done.18 = bf16[128,1152]{1,0:T(8,128)(2,1)S(1)} collective-permute-done((bf16[128,1152]{1,0:T(8,128)(2,1)S(1)}, bf16[128,1152]{1,0:T(8,128)(2,1)S(1)}, u32[]{:S(2)}, u32[]{:S(2)}) %collective-permute-start.18) | collective-permute-done | bytes 294944 | tf_op jit(solution)/shard_map/ppermute | solution.py:18
  16.3 1.2 collective-permute-start.1
  17.5 5.1 %collective-permute-done.3 = bf16[128,1152]{1,0:T(8,128)(2,1)S(1)} collective-permute-done((bf16[128,1152]{1,0:T(8,128)(2,1)S(1)}, bf16[128,1152]{1,0:T(8,128)(2,1)S(1)}, u32[]{:S(2)}, u32[]{:S(2)}) %collective-permute-start.3) | collective-permute-done | bytes 294944 | tf_op jit(solution)/shard_map/ppermute | solution.py:18
  22.6 1.1 collective-permute-start.4
  23.8 1.9 %collective-permute-start = (bf16[128,1152]{1,0:T(8,128)(2,1)S(1)}, bf16[128,1152]{1,0:T(8,128)(2,1)S(1)}, u32[]{:S(2)}, u32[]{:S(2)}) collective-permute-start(bf16[128,1152]{1,0:T(8,128)(2,1)S(1)} %multiply_convert_fusion.4), channel_id=1, source_target_pairs={{0,1},{1,0},{2,3},{3,2},{4,5},{5,4},{6,7},{7,6},{8,9},{9,8},{10,11... | collective-permute-start | bytes 884744 | tf_op jit(solution)/shard_map/ppermute | solution.py:26
  25.9 4.0 %collective-permute-done.4 = bf16[128,1152]{1,0:T(8,128)(2,1)S(1)} collective-permute-done((bf16[128,1152]{1,0:T(8,128)(2,1)S(1)}, bf16[128,1152]{1,0:T(8,128)(2,1)S(1)}, u32[]{:S(2)}, u32[]{:S(2)}) %collective-permute-start.4) | collective-permute-done | bytes 294944 | tf_op jit(solution)/shard_map/ppermute | solution.py:18
  30.0 2.7 %collective-permute-start.21 = (bf16[128,1152]{1,0:T(8,128)(2,1)S(1)}, bf16[128,1152]{1,0:T(8,128)(2,1)}, u32[]{:S(2)}, u32[]{:S(2)}) collective-permute-start(bf16[128,1152]{1,0:T(8,128)(2,1)S(1)} %collective-permute-done.19), channel_id=1, source_target_pairs={{0,28},{1,29},{2,30},{3,31},{4,0},{5,1},{6,2},{7,3},{8,4},{9,5},{1... | collective-permute-start | bytes 884744 | tf_op jit(solution)/shard_map/ppermute | solution.py:18
  32.7 0.7 fusion.54
  33.4 0.5 fusion.71
  33.9 1.3 %fusion.49 = (f32[512]{0:T(512)}, f32[512,256]{0,1:T(8,128)S(1)}) fusion(f32[]{:T(128)} %bitcast.66, bf16[256,1152]{1,0:T(8,128)(2,1)S(1)} %constant_dynamic-update-slice_fusion, bf16[128,1152]{1,0:T(8,128)(2,1)S(1)} %collective-permute-done.2, bf16[128,1152]{1,0:T(8,128)(2,1)S(1)} %collective-permute-done.1, ...), kind=kOutput, calls=%fused_computation.84 | convolution fusion | flops 307887616 | bytes 2295816 | tf_op jit(solution)/shard_map/dot_general | solution.py:44
  35.3 0.6 convolution_add_fusion.5
  35.9 2.7 %collective-permute-start.6 = (bf16[128,1152]{1,0:T(8,128)(2,1)S(1)}, bf16[128,1152]{1,0:T(8,128)(2,1)}, u32[]{:S(2)}, u32[]{:S(2)}) collective-permute-start(bf16[128,1152]{1,0:T(8,128)(2,1)S(1)} %collective-permute-done.4), channel_id=1, source_target_pairs={{0,28},{1,29},{2,30},{3,31},{4,0},{5,1},{6,2},{7,3},{8,4},{9,5},{1... | collective-permute-start | bytes 884744 | tf_op jit(solution)/shard_map/ppermute | solution.py:18
  38.7 4.6 %collective-permute-start.17 = (bf16[128,1152]{1,0:T(8,128)(2,1)S(1)}, bf16[128,1152]{1,0:T(8,128)(2,1)S(1)}, u32[]{:S(2)}, u32[]{:S(2)}) collective-permute-start(bf16[128,1152]{1,0:T(8,128)(2,1)S(1)} %collective-permute-done.16), channel_id=1, source_target_pairs={{0,1},{1,0},{2,3},{3,2},{4,5},{5,4},{6,7},{7,6},{8,9},{9,8},{10,11... | collective-permute-start | bytes 884744 | tf_op jit(solution)/shard_map/ppermute | solution.py:26
  43.3 1.0 constant_dynamic-update-slice_fusion.11
  44.6 1.0 constant_dynamic-update-slice_fusion.10
  45.6 2.7 %collective-permute-start.23 = (bf16[128,1152]{1,0:T(8,128)(2,1)}, bf16[128,1152]{1,0:T(8,128)(2,1)}, u32[]{:S(2)}, u32[]{:S(2)}) collective-permute-start(bf16[128,1152]{1,0:T(8,128)(2,1)} %collective-permute-done.21), channel_id=1, source_target_pairs={{0,28},{1,29},{2,30},{3,31},{4,0},{5,1},{6,2},{7,3},{8,4},{9,5},{1... | collective-permute-start | bytes 884744 | tf_op jit(solution)/shard_map/ppermute | solution.py:18
  48.3 1.0 constant_dynamic-update-slice_fusion.3
  49.4 1.0 constant_dynamic-update-slice_fusion.2
  50.5 2.1 %fusion.50 = (f32[512]{0:T(512)}, f32[512,256]{0,1:T(8,128)}) fusion(f32[]{:T(128)} %bitcast.71, bf16[256,1152]{1,0:T(8,128)(2,1)S(1)} %constant_dynamic-update-slice_fusion.2, bf16[128,1152]{1,0:T(8,128)(2,1)S(1)} %collective-permute-done.2, bf16[128,1152]{1,0:T(8,128)(2,1)S(1)} %collective-permute-done.1, bf16[128,1152]{1,0:T(8,128)(2,1)S(1)} %collective-permute-done, ...), kind=kOutput, calls=%fused_computation.85 | convolution fusion | flops 307887616 | bytes 2295816 | tf_op jit(solution)/shard_map/dot_general | solution.py:44
  52.6 2.7 %collective-permute-start.8 = (bf16[128,1152]{1,0:T(8,128)(2,1)}, bf16[128,1152]{1,0:T(8,128)(2,1)}, u32[]{:S(2)}, u32[]{:S(2)}) collective-permute-start(bf16[128,1152]{1,0:T(8,128)(2,1)} %collective-permute-done.6), channel_id=1, source_target_pairs={{0,28},{1,29},{2,30},{3,31},{4,0},{5,1},{6,2},{7,3},{8,4},{9,5},{1... | collective-permute-start | bytes 884744 | tf_op jit(solution)/shard_map/ppermute | solution.py:18
  55.2 0.7 copy-done.29
  55.9 3.8 %fusion.46 = f32[512,1152]{1,0:T(8,128)} fusion(bf16[128,1152]{1,0:T(8,128)(2,1)} %copy-done.8, f32[]{:T(128)} %bitcast.73, f32[]{:T(128)} %bitcast.60, bf16[128,1152]{1,0:T(8,128)(2,1)} %copy-done.29, bf16[128,1152]{1,0:T(8,128)(2,1)} %copy-done.19, bf16[128,1152]{1,0:T(8,128)(2,1)} %copy-done.24, bf16[128,1152]{1,0:T(8,128)(2,1)} %copy-done.5), kind=kOutput, calls=%fused_computation.69 | convolution fusion | flops 307494912 | bytes 3833864 | tf_op jit(solution)/shard_map/dot_general | solution.py:65
  59.7 5.0 %convolution_add_fusion.2 = f32[512,1152]{1,0:T(8,128)} fusion(f32[512,1152]{1,0:T(8,128)} %fusion.46, bf16[256,1152]{1,0:T(8,128)(2,1)} %copy-done.11, f32[]{:T(128)} %bitcast.69, f32[]{:T(128)} %bitcast.53, bf16[128,1152]{1,0:T(8,128)(2,1)} %copy-done.29, bf16[128,1152]{1,0:T(8,128)(2,1)} %copy-done.19, bf16[128,1152]{1,0:T(8,128)(2,1)} %copy-done.24, ...), kind=kOutput, calls=%fused_computation.3 | convolution fusion | flops 610205696 | bytes 6488072 | tf_op jit(solution)/shard_map/dot_general | solution.py:53
  64.8 5.0 %convolution_add_fusion.1 = f32[512,1152]{1,0:T(8,128)} fusion(f32[512,1152]{1,0:T(8,128)} %convolution_add_fusion.2, bf16[256,1152]{1,0:T(8,128)(2,1)} %copy-done.12, f32[]{:T(128)} %bitcast.68, f32[]{:T(128)} %bitcast.52, bf16[128,1152]{1,0:T(8,128)(2,1)} %copy-done.29, bf16[128,1152]{1,0:T(8,128)(2,1)} %copy-done.19, bf16[128,1152]{1,0:T(8,128)(2,1)} %copy-done.24, ...), kind=kOutput, calls=%fused_computation.2 | convolution fusion | flops 610205696 | bytes 6488072 | tf_op jit(solution)/shard_map/dot_general | solution.py:53
  69.8 3.1 %convolution_add_fusion.4 = f32[512,1152]{1,0:T(8,128)} fusion(f32[512,1152]{1,0:T(8,128)S(1)} %convolution_add_fusion.5, bf16[256,1152]{1,0:T(8,128)(2,1)S(1)} %constant_dynamic-update-slice_fusion.2, f32[512,256]{0,1:T(8,128)} %get-tuple-element.8, f32[]{:T(128)} %bitcast.56), kind=kOutput, calls=%fused_computation.6 | convolution fusion | flops 303235072 | bytes 5832708 | tf_op jit(solution)/shard_map/dot_general | solution.py:53
  72.9 1.0 slice.72
  74.0 0.9 slice.73
  74.9 2.7 %collective-permute-start.25 = (bf16[64,1152]{1,0:T(8,128)(2,1)S(1)}, bf16[64,1152]{1,0:T(8,128)(2,1)S(1)}, u32[]{:S(2)}, u32[]{:S(2)}) collective-permute-start(bf16[64,1152]{1,0:T(8,128)(2,1)S(1)} %slice.73), channel_id=1, source_target_pairs={{0,28},{1,29},{2,30},{3,31},{4,0},{5,1},{6,2},{7,3},{8,4},{9,5},{1... | collective-permute-start | bytes 442376 | tf_op jit(solution)/shard_map/ppermute | solution.py:18
  77.7 1.6 %slice.68 = bf16[64,1152]{1,0:T(8,128)(2,1)} slice(bf16[128,1152]{1,0:T(8,128)(2,1)} %collective-permute-done.7), slice={[0:64], [0:1152]} | slice | bytes 294912 | tf_op jit(solution)/shard_map/slice | solution.py:77
  79.3 1.6 %slice.69 = bf16[64,1152]{1,0:T(8,128)(2,1)} slice(bf16[128,1152]{1,0:T(8,128)(2,1)} %collective-permute-done.8), slice={[64:128], [0:1152]} | slice | bytes 294912 | tf_op jit(solution)/shard_map/slice | solution.py:77
  80.8 2.7 %collective-permute-start.10 = (bf16[64,1152]{1,0:T(8,128)(2,1)}, bf16[64,1152]{1,0:T(8,128)(2,1)}, u32[]{:S(2)}, u32[]{:S(2)}) collective-permute-start(bf16[64,1152]{1,0:T(8,128)(2,1)} %slice.69), channel_id=1, source_target_pairs={{0,28},{1,29},{2,30},{3,31},{4,0},{5,1},{6,2},{7,3},{8,4},{9,5},{1... | collective-permute-start | bytes 442376 | tf_op jit(solution)/shard_map/ppermute | solution.py:18
  83.5 1.7 %constant_dynamic-update-slice_fusion.13 = bf16[256,1152]{1,0:T(8,128)(2,1)} fusion(bf16[128,1152]{1,0:T(8,128)(2,1)} %collective-permute-done.22), kind=kLoop, calls=%fused_computation.142 | loop fusion | bytes 589824
  85.2 1.0 constant_dynamic-update-slice_fusion.5
  86.2 1.0 constant_dynamic-update-slice_fusion.4
  87.3 2.2 %fusion.51 = (f32[512]{0:T(512)}, f32[512,256]{0,1:T(8,128)}) fusion(f32[]{:T(128)} %bitcast.70, bf16[256,1152]{1,0:T(8,128)(2,1)S(1)} %constant_dynamic-update-slice_fusion.4, bf16[128,1152]{1,0:T(8,128)(2,1)S(1)} %copy-done.27, bf16[128,1152]{1,0:T(8,128)(2,1)S(1)} %copy-done.17, bf16[128,1152]{1,0:T(8,128)(2,1)S(1)} %copy-done.22, ...), kind=kOutput, calls=%fused_computation.86 | convolution fusion | flops 307887616 | bytes 2295816 | tf_op jit(solution)/shard_map/dot_general | solution.py:44
  89.4 1.7 %constant_dynamic-update-slice_fusion.12 = bf16[256,1152]{1,0:T(8,128)(2,1)} fusion(bf16[256,1152]{1,0:T(8,128)(2,1)} %constant_dynamic-update-slice_fusion.13, bf16[128,1152]{1,0:T(8,128)(2,1)} %collective-permute-done.23), kind=kLoop, calls=%fused_computation.141 | loop fusion | bytes 589824 | tf_op jit(solution)/shard_map/concatenate | solution.py:85
  91.2 2.4 %fusion.45 = f32[512,1152]{1,0:T(8,128)} fusion(bf16[128,1152]{1,0:T(8,128)(2,1)S(1)} %constant_dynamic-update-slice_fusion.14, f32[]{:T(128)} %bitcast.72, f32[]{:T(128)} %bitcast.61, bf16[128,1152]{1,0:T(8,128)(2,1)S(1)} %copy-done.30, bf16[128,1152]{1,0:T(8,128)(2,1)S(1)} %copy-done.20, bf16[128,1152]{1,0:T(8,128)(2,1)S(1)} %copy-done.25, ...), kind=kOutput, calls=%fused_computation.68 | convolution fusion | flops 307167232 | bytes 3833864 | tf_op jit(solution)/shard_map/dot_general | solution.py:53
  93.6 4.3 %fusion = f32[512,1152]{1,0:T(8,128)S(1)} fusion(f32[512,1152]{1,0:T(8,128)} %fusion.45, f32[512,1152]{1,0:T(8,128)} %convolution_add_fusion.1, bf16[256,1152]{1,0:T(8,128)(2,1)} %constant_dynamic-update-slice_fusion.12, f32[]{:T(128)} %bitcast.67, f32[]{:T(128)} %bitcast.54, bf16[128,1152]{1,0:T(8,128)(2,1)} %copy-done.29, ...), kind=kOutput, calls=%fused_computation.1 | convolution fusion | flops 610795520 | bytes 8847368 | tf_op jit(solution)/shard_map/dot_general | solution.py:53
  98.1 0.9 slice.65
  98.9 0.6 copy-done.3
  99.5 2.2 %collective-permute-start.26 = (bf16[2,128,1152]{2,1,0:T(8,128)(2,1)}, bf16[2,128,1152]{2,1,0:T(8,128)(2,1)}, u32[]{:S(2)}, u32[]{:S(2)}) collective-permute-start(bf16[2,128,1152]{2,1,0:T(8,128)(2,1)} %slice.65), channel_id=1, source_target_pairs={{0,1},{1,0},{2,3},{3,2},{4,5},{5,4},{6,7},{7,6},{8,9},{9,8},{10,11... | collective-permute-start | bytes 1769480 | tf_op jit(solution)/shard_map/ppermute | solution.py:26
  101.8 0.9 constant_dynamic-update-slice_fusion.7
  102.7 0.9 constant_dynamic-update-slice_fusion.6
  103.7 1.4 %fusion.55 = (f32[512]{0:T(512)S(1)}, f32[512,128]{0,1:T(8,128)}) fusion(f32[]{:T(128)} %bitcast.74, bf16[128,1152]{1,0:T(8,128)(2,1)S(1)} %constant_dynamic-update-slice_fusion.6, bf16[128,1152]{1,0:T(8,128)(2,1)S(1)} %copy-done.28, bf16[128,1152]{1,0:T(8,128)(2,1)S(1)} %copy-done.18, bf16[128,1152]{1,0:T(8,128)(2,1)S(1)} %copy-done.23, ...), kind=kOutput, calls=%fused_computation.95 | convolution fusion | flops 156302848 | bytes 1738760 | tf_op jit(solution)/shard_map/dot_general | solution.py:44
  105.1 0.6 slice.55
  105.7 3.1 %fusion.72 = f32[512,1152]{1,0:T(8,128)} fusion(bf16[128,1152]{1,0:T(8,128)(2,1)} %copy-done.7, f32[512,128]{0,1:T(8,128)} %get-tuple-element.4, f32[]{:T(128)} %bitcast.62), kind=kOutput, calls=%fused_computation.116 | convolution fusion | flops 151322624 | bytes 2916356 | tf_op jit(solution)/shard_map/dot_general | solution.py:53
  108.9 0.7 add.190
  109.5 1.2 collective-permute-start.12
  110.8 2.4 %fusion.1 = f32[512,1152]{1,0:T(8,128)S(1)} fusion(f32[512,1152]{1,0:T(8,128)} %fusion.72, f32[512,1152]{1,0:T(8,128)S(1)} %copy-done.2, bf16[256,1152]{1,0:T(8,128)(2,1)S(1)} %constant_dynamic-update-slice_fusion.4, f32[512,256]{0,1:T(8,128)} %get-tuple-element.6, f32[]{:T(128)} %bitcast.55), kind=kOutput, calls=%fused_computation.5 | convolution fusion | flops 303824896 | bytes 8192004 | tf_op jit(solution)/shard_map/dot_general | solution.py:53
  113.4 0.8 collective-permute-start.13
  114.9 1.2 convert_add_fusion
  116.6 1.3 collective-permute-start.14
  117.9 6.1 %collective-permute-done.27 = bf16[128,1152]{1,0:T(8,128)(2,1)S(1)} collective-permute-done((bf16[128,1152]{1,0:T(8,128)(2,1)S(1)}, bf16[128,1152]{1,0:T(8,128)(2,1)S(1)}, u32[]{:S(2)}, u32[]{:S(2)}) %collective-permute-start.27) | collective-permute-done | bytes 294944 | tf_op jit(solution)/shard_map/ppermute | solution.py:22
  124.2 1.0 subtract_multiply_fusion
  125.2 5.1 %collective-permute-done.14 = bf16[128,1152]{1,0:T(8,128)(2,1)S(1)} collective-permute-done((bf16[128,1152]{1,0:T(8,128)(2,1)S(1)}, bf16[128,1152]{1,0:T(8,128)(2,1)S(1)}, u32[]{:S(2)}, u32[]{:S(2)}) %collective-permute-start.14) | collective-permute-done | bytes 294944 | tf_op jit(solution)/shard_map/ppermute | solution.py:22
  130.6 1.0 subtract_multiply_fusion.1
  (113 shorter events, 3.0 us)
Async XLA Ops:
  0.6 6.2 %copy-start = (f32[128,1152]{1,0:T(8,128)S(1)}, f32[128,1152]{1,0:T(8,128)}, u32[]{:S(2)}) copy-start(f32[128,1152]{1,0:T(8,128)} %param.5) | copy-start | bytes 1769476
  3.1 47.4 %copy-start.8 = (bf16[128,1152]{1,0:T(8,128)(2,1)}, bf16[128,1152]{1,0:T(8,128)(2,1)S(1)}, u32[]{:S(2)}) copy-start(bf16[128,1152]{1,0:T(8,128)(2,1)S(1)} %multiply_convert_fusion.4) | copy-start | bytes 884740
  3.1 13.2 %collective-permute-start.18 = (bf16[128,1152]{1,0:T(8,128)(2,1)S(1)}, bf16[128,1152]{1,0:T(8,128)(2,1)S(1)}, u32[]{:S(2)}, u32[]{:S(2)}) collective-permute-start(bf16[128,1152]{1,0:T(8,128)(2,1)S(1)} %multiply_convert_fusion.4), channel_id=1, source_target_pairs={{0,4},{1,5},{2,6},{3,7},{4,8},{5,9},{6,10},{7,11},{8,12},{9,13},{1... | collective-permute-start | bytes 884744 | tf_op jit(solution)/shard_map/ppermute | solution.py:18
  6.9 26.5 %copy-start.5 = (bf16[128,1152]{1,0:T(8,128)(2,1)}, bf16[128,1152]{1,0:T(8,128)(2,1)S(1)}, u32[]{:S(2)}) copy-start(bf16[128,1152]{1,0:T(8,128)(2,1)S(1)} %multiply_convert_fusion.3) | copy-start | bytes 884740
  6.9 15.7 %collective-permute-start.3 = (bf16[128,1152]{1,0:T(8,128)(2,1)S(1)}, bf16[128,1152]{1,0:T(8,128)(2,1)S(1)}, u32[]{:S(2)}, u32[]{:S(2)}) collective-permute-start(bf16[128,1152]{1,0:T(8,128)(2,1)S(1)} %multiply_convert_fusion.3), channel_id=1, source_target_pairs={{0,4},{1,5},{2,6},{3,7},{4,8},{5,9},{6,10},{7,11},{8,12},{9,13},{1... | collective-permute-start | bytes 884744 | tf_op jit(solution)/shard_map/ppermute | solution.py:18
  8.7 27.2 %collective-permute-start.16 = (bf16[128,1152]{1,0:T(8,128)(2,1)S(1)}, bf16[128,1152]{1,0:T(8,128)(2,1)S(1)}, u32[]{:S(2)}, u32[]{:S(2)}) collective-permute-start(bf16[128,1152]{1,0:T(8,128)(2,1)S(1)} %multiply_convert_fusion.3), channel_id=1, source_target_pairs={{0,2},{1,3},{2,0},{3,1},{4,6},{5,7},{6,4},{7,5},{8,10},{9,11},{10,... | collective-permute-start | bytes 884744 | tf_op jit(solution)/shard_map/ppermute | solution.py:22
  9.9 42.7 %collective-permute-start.15 = (bf16[128,1152]{1,0:T(8,128)(2,1)S(1)}, bf16[128,1152]{1,0:T(8,128)(2,1)S(1)}, u32[]{:S(2)}, u32[]{:S(2)}) collective-permute-start(bf16[128,1152]{1,0:T(8,128)(2,1)S(1)} %multiply_convert_fusion.3), channel_id=1, source_target_pairs={{0,1},{1,0},{2,3},{3,2},{4,5},{5,4},{6,7},{7,6},{8,9},{9,8},{10,11... | collective-permute-start | bytes 884744 | tf_op jit(solution)/shard_map/ppermute | solution.py:26
  11.4 12.4 %collective-permute-start.19 = (bf16[128,1152]{1,0:T(8,128)(2,1)S(1)}, bf16[128,1152]{1,0:T(8,128)(2,1)S(1)}, u32[]{:S(2)}, u32[]{:S(2)}) collective-permute-start(bf16[128,1152]{1,0:T(8,128)(2,1)S(1)} %multiply_convert_fusion.4), channel_id=1, source_target_pairs={{0,28},{1,29},{2,30},{3,31},{4,0},{5,1},{6,2},{7,3},{8,4},{9,5},{1... | collective-permute-start | bytes 884744 | tf_op jit(solution)/shard_map/ppermute | solution.py:18
  16.3 9.4 %collective-permute-start.1 = (bf16[128,1152]{1,0:T(8,128)(2,1)S(1)}, bf16[128,1152]{1,0:T(8,128)(2,1)S(1)}, u32[]{:S(2)}, u32[]{:S(2)}) collective-permute-start(bf16[128,1152]{1,0:T(8,128)(2,1)S(1)} %multiply_convert_fusion.4), channel_id=1, source_target_pairs={{0,2},{1,3},{2,0},{3,1},{4,6},{5,7},{6,4},{7,5},{8,10},{9,11},{10,... | collective-permute-start | bytes 884744 | tf_op jit(solution)/shard_map/ppermute | solution.py:22
  22.6 7.3 %collective-permute-start.4 = (bf16[128,1152]{1,0:T(8,128)(2,1)S(1)}, bf16[128,1152]{1,0:T(8,128)(2,1)S(1)}, u32[]{:S(2)}, u32[]{:S(2)}) collective-permute-start(bf16[128,1152]{1,0:T(8,128)(2,1)S(1)} %multiply_convert_fusion.3), channel_id=1, source_target_pairs={{0,28},{1,29},{2,30},{3,31},{4,0},{5,1},{6,2},{7,3},{8,4},{9,5},{1... | collective-permute-start | bytes 884744 | tf_op jit(solution)/shard_map/ppermute | solution.py:18
  23.8 6.1 %collective-permute-start = (bf16[128,1152]{1,0:T(8,128)(2,1)S(1)}, bf16[128,1152]{1,0:T(8,128)(2,1)S(1)}, u32[]{:S(2)}, u32[]{:S(2)}) collective-permute-start(bf16[128,1152]{1,0:T(8,128)(2,1)S(1)} %multiply_convert_fusion.4), channel_id=1, source_target_pairs={{0,1},{1,0},{2,3},{3,2},{4,5},{5,4},{6,7},{7,6},{8,9},{9,8},{10,11... | collective-permute-start | bytes 884744 | tf_op jit(solution)/shard_map/ppermute | solution.py:26
  25.7 24.7 %copy-start.16 = (bf16[128,1152]{1,0:T(8,128)(2,1)}, bf16[128,1152]{1,0:T(8,128)(2,1)S(1)}, u32[]{:S(2)}) copy-start(bf16[128,1152]{1,0:T(8,128)(2,1)S(1)} %collective-permute-done.1) | copy-start | bytes 884740
  25.7 7.0 %collective-permute-start.2 = (bf16[128,1152]{1,0:T(8,128)(2,1)S(1)}, bf16[128,1152]{1,0:T(8,128)(2,1)S(1)}, u32[]{:S(2)}, u32[]{:S(2)}) collective-permute-start(bf16[128,1152]{1,0:T(8,128)(2,1)S(1)} %collective-permute-done.1), channel_id=1, source_target_pairs={{0,1},{1,0},{2,3},{3,2},{4,5},{5,4},{6,7},{7,6},{8,9},{9,8},{10,11... | collective-permute-start | bytes 884744 | tf_op jit(solution)/shard_map/ppermute | solution.py:26
  25.9 7.5 %copy-start.11 = (bf16[256,1152]{1,0:T(8,128)(2,1)}, bf16[256,1152]{1,0:T(8,128)(2,1)S(1)}, u32[]{:S(2)}) copy-start(bf16[256,1152]{1,0:T(8,128)(2,1)S(1)} %constant_dynamic-update-slice_fusion.8) | copy-start | bytes 1769476
  29.9 8.8 %collective-permute-start.20 = (bf16[128,1152]{1,0:T(8,128)(2,1)S(1)}, bf16[128,1152]{1,0:T(8,128)(2,1)}, u32[]{:S(2)}, u32[]{:S(2)}) collective-permute-start(bf16[128,1152]{1,0:T(8,128)(2,1)S(1)} %collective-permute-done.18), channel_id=1, source_target_pairs={{0,4},{1,5},{2,6},{3,7},{4,8},{5,9},{6,10},{7,11},{8,12},{9,13},{1... | collective-permute-start | bytes 884744 | tf_op jit(solution)/shard_map/ppermute | solution.py:18
  29.9 20.5 %copy-start.21 = (bf16[128,1152]{1,0:T(8,128)(2,1)}, bf16[128,1152]{1,0:T(8,128)(2,1)S(1)}, u32[]{:S(2)}) copy-start(bf16[128,1152]{1,0:T(8,128)(2,1)S(1)} %collective-permute-done) | copy-start | bytes 884740
  30.0 14.3 %collective-permute-start.21 = (bf16[128,1152]{1,0:T(8,128)(2,1)S(1)}, bf16[128,1152]{1,0:T(8,128)(2,1)}, u32[]{:S(2)}, u32[]{:S(2)}) collective-permute-start(bf16[128,1152]{1,0:T(8,128)(2,1)S(1)} %collective-permute-done.19), channel_id=1, source_target_pairs={{0,28},{1,29},{2,30},{3,31},{4,0},{5,1},{6,2},{7,3},{8,4},{9,5},{1... | collective-permute-start | bytes 884744 | tf_op jit(solution)/shard_map/ppermute | solution.py:18
  32.7 17.8 %copy-start.26 = (bf16[128,1152]{1,0:T(8,128)(2,1)}, bf16[128,1152]{1,0:T(8,128)(2,1)S(1)}, u32[]{:S(2)}) copy-start(bf16[128,1152]{1,0:T(8,128)(2,1)S(1)} %collective-permute-done.2) | copy-start | bytes 884740
  32.7 12.9 %collective-permute-start.5 = (bf16[128,1152]{1,0:T(8,128)(2,1)S(1)}, bf16[128,1152]{1,0:T(8,128)(2,1)}, u32[]{:S(2)}, u32[]{:S(2)}) collective-permute-start(bf16[128,1152]{1,0:T(8,128)(2,1)S(1)} %collective-permute-done.3), channel_id=1, source_target_pairs={{0,4},{1,5},{2,6},{3,7},{4,8},{5,9},{6,10},{7,11},{8,12},{9,13},{1... | collective-permute-start | bytes 884744 | tf_op jit(solution)/shard_map/ppermute | solution.py:18
  35.9 16.6 %copy-start.19 = (bf16[128,1152]{1,0:T(8,128)(2,1)}, bf16[128,1152]{1,0:T(8,128)(2,1)S(1)}, u32[]{:S(2)}) copy-start(bf16[128,1152]{1,0:T(8,128)(2,1)S(1)} %collective-permute-done.16) | copy-start | bytes 884740
  35.9 13.4 %collective-permute-start.6 = (bf16[128,1152]{1,0:T(8,128)(2,1)S(1)}, bf16[128,1152]{1,0:T(8,128)(2,1)}, u32[]{:S(2)}, u32[]{:S(2)}) collective-permute-start(bf16[128,1152]{1,0:T(8,128)(2,1)S(1)} %collective-permute-done.4), channel_id=1, source_target_pairs={{0,28},{1,29},{2,30},{3,31},{4,0},{5,1},{6,2},{7,3},{8,4},{9,5},{1... | collective-permute-start | bytes 884744 | tf_op jit(solution)/shard_map/ppermute | solution.py:18
  38.7 16.6 %collective-permute-start.17 = (bf16[128,1152]{1,0:T(8,128)(2,1)S(1)}, bf16[128,1152]{1,0:T(8,128)(2,1)S(1)}, u32[]{:S(2)}, u32[]{:S(2)}) collective-permute-start(bf16[128,1152]{1,0:T(8,128)(2,1)S(1)} %collective-permute-done.16), channel_id=1, source_target_pairs={{0,1},{1,0},{2,3},{3,2},{4,5},{5,4},{6,7},{7,6},{8,9},{9,8},{10,11... | collective-permute-start | bytes 884744 | tf_op jit(solution)/shard_map/ppermute | solution.py:26
  44.3 28.6 %collective-permute-start.22 = (bf16[128,1152]{1,0:T(8,128)(2,1)}, bf16[128,1152]{1,0:T(8,128)(2,1)}, u32[]{:S(2)}, u32[]{:S(2)}) collective-permute-start(bf16[128,1152]{1,0:T(8,128)(2,1)} %collective-permute-done.20), channel_id=1, source_target_pairs={{0,4},{1,5},{2,6},{3,7},{4,8},{5,9},{6,10},{7,11},{8,12},{9,13},{1... | collective-permute-start | bytes 884744 | tf_op jit(solution)/shard_map/ppermute | solution.py:18
  45.6 4.8 %copy-start.12 = (bf16[256,1152]{1,0:T(8,128)(2,1)}, bf16[256,1152]{1,0:T(8,128)(2,1)S(1)}, u32[]{:S(2)}) copy-start(bf16[256,1152]{1,0:T(8,128)(2,1)S(1)} %constant_dynamic-update-slice_fusion.10) | copy-start | bytes 1769476
  45.6 28.4 %collective-permute-start.23 = (bf16[128,1152]{1,0:T(8,128)(2,1)}, bf16[128,1152]{1,0:T(8,128)(2,1)}, u32[]{:S(2)}, u32[]{:S(2)}) collective-permute-start(bf16[128,1152]{1,0:T(8,128)(2,1)} %collective-permute-done.21), channel_id=1, source_target_pairs={{0,28},{1,29},{2,30},{3,31},{4,0},{5,1},{6,2},{7,3},{8,4},{9,5},{1... | collective-permute-start | bytes 884744 | tf_op jit(solution)/shard_map/ppermute | solution.py:18
  49.3 28.3 %collective-permute-start.7 = (bf16[128,1152]{1,0:T(8,128)(2,1)}, bf16[128,1152]{1,0:T(8,128)(2,1)}, u32[]{:S(2)}, u32[]{:S(2)}) collective-permute-start(bf16[128,1152]{1,0:T(8,128)(2,1)} %collective-permute-done.5), channel_id=1, source_target_pairs={{0,4},{1,5},{2,6},{3,7},{4,8},{5,9},{6,10},{7,11},{8,12},{9,13},{1... | collective-permute-start | bytes 884744 | tf_op jit(solution)/shard_map/ppermute | solution.py:18
  52.6 2.7 %copy-start.24 = (bf16[128,1152]{1,0:T(8,128)(2,1)}, bf16[128,1152]{1,0:T(8,128)(2,1)S(1)}, u32[]{:S(2)}) copy-start(bf16[128,1152]{1,0:T(8,128)(2,1)S(1)} %collective-permute-done.15) | copy-start | bytes 884740
  52.6 26.7 %collective-permute-start.8 = (bf16[128,1152]{1,0:T(8,128)(2,1)}, bf16[128,1152]{1,0:T(8,128)(2,1)}, u32[]{:S(2)}, u32[]{:S(2)}) collective-permute-start(bf16[128,1152]{1,0:T(8,128)(2,1)} %collective-permute-done.6), channel_id=1, source_target_pairs={{0,28},{1,29},{2,30},{3,31},{4,0},{5,1},{6,2},{7,3},{8,4},{9,5},{1... | collective-permute-start | bytes 884744 | tf_op jit(solution)/shard_map/ppermute | solution.py:18
  55.2 0.7 copy-start.29
  72.9 14.3 %copy-start.9 = (bf16[128,1152]{1,0:T(8,128)(2,1)S(1)}, bf16[128,1152]{1,0:T(8,128)(2,1)}, u32[]{:S(2)}) copy-start(bf16[128,1152]{1,0:T(8,128)(2,1)} %copy-done.8) | copy-start | bytes 884740
  72.9 14.3 %copy-start.17 = (bf16[128,1152]{1,0:T(8,128)(2,1)S(1)}, bf16[128,1152]{1,0:T(8,128)(2,1)}, u32[]{:S(2)}) copy-start(bf16[128,1152]{1,0:T(8,128)(2,1)} %copy-done.16) | copy-start | bytes 884740
  72.9 14.3 %copy-start.22 = (bf16[128,1152]{1,0:T(8,128)(2,1)S(1)}, bf16[128,1152]{1,0:T(8,128)(2,1)}, u32[]{:S(2)}) copy-start(bf16[128,1152]{1,0:T(8,128)(2,1)} %copy-done.21) | copy-start | bytes 884740
  72.9 14.4 %copy-start.27 = (bf16[128,1152]{1,0:T(8,128)(2,1)S(1)}, bf16[128,1152]{1,0:T(8,128)(2,1)}, u32[]{:S(2)}) copy-start(bf16[128,1152]{1,0:T(8,128)(2,1)} %copy-done.26) | copy-start | bytes 884740
  73.9 17.2 %collective-permute-start.24 = (bf16[64,1152]{1,0:T(8,128)(2,1)S(1)}, bf16[64,1152]{1,0:T(8,128)(2,1)S(1)}, u32[]{:S(2)}, u32[]{:S(2)}) collective-permute-start(bf16[64,1152]{1,0:T(8,128)(2,1)S(1)} %slice.72), channel_id=1, source_target_pairs={{0,4},{1,5},{2,6},{3,7},{4,8},{5,9},{6,10},{7,11},{8,12},{9,13},{1... | collective-permute-start | bytes 442376 | tf_op jit(solution)/shard_map/ppermute | solution.py:18
  74.9 16.2 %collective-permute-start.25 = (bf16[64,1152]{1,0:T(8,128)(2,1)S(1)}, bf16[64,1152]{1,0:T(8,128)(2,1)S(1)}, u32[]{:S(2)}, u32[]{:S(2)}) collective-permute-start(bf16[64,1152]{1,0:T(8,128)(2,1)S(1)} %slice.73), channel_id=1, source_target_pairs={{0,28},{1,29},{2,30},{3,31},{4,0},{5,1},{6,2},{7,3},{8,4},{9,5},{1... | collective-permute-start | bytes 442376 | tf_op jit(solution)/shard_map/ppermute | solution.py:18
  79.3 22.5 %collective-permute-start.9 = (bf16[64,1152]{1,0:T(8,128)(2,1)}, bf16[64,1152]{1,0:T(8,128)(2,1)}, u32[]{:S(2)}, u32[]{:S(2)}) collective-permute-start(bf16[64,1152]{1,0:T(8,128)(2,1)} %slice.68), channel_id=1, source_target_pairs={{0,4},{1,5},{2,6},{3,7},{4,8},{5,9},{6,10},{7,11},{8,12},{9,13},{1... | collective-permute-start | bytes 442376 | tf_op jit(solution)/shard_map/ppermute | solution.py:18
  80.8 21.9 %collective-permute-start.10 = (bf16[64,1152]{1,0:T(8,128)(2,1)}, bf16[64,1152]{1,0:T(8,128)(2,1)}, u32[]{:S(2)}, u32[]{:S(2)}) collective-permute-start(bf16[64,1152]{1,0:T(8,128)(2,1)} %slice.69), channel_id=1, source_target_pairs={{0,28},{1,29},{2,30},{3,31},{4,0},{5,1},{6,2},{7,3},{8,4},{9,5},{1... | collective-permute-start | bytes 442376 | tf_op jit(solution)/shard_map/ppermute | solution.py:18
  87.2 4.0 %copy-start.6 = (bf16[128,1152]{1,0:T(8,128)(2,1)S(1)}, bf16[128,1152]{1,0:T(8,128)(2,1)}, u32[]{:S(2)}) copy-start(bf16[128,1152]{1,0:T(8,128)(2,1)} %copy-done.5) | copy-start | bytes 884740
  87.2 4.0 %copy-start.20 = (bf16[128,1152]{1,0:T(8,128)(2,1)S(1)}, bf16[128,1152]{1,0:T(8,128)(2,1)}, u32[]{:S(2)}) copy-start(bf16[128,1152]{1,0:T(8,128)(2,1)} %copy-done.19) | copy-start | bytes 884740
  87.2 4.0 %copy-start.25 = (bf16[128,1152]{1,0:T(8,128)(2,1)S(1)}, bf16[128,1152]{1,0:T(8,128)(2,1)}, u32[]{:S(2)}) copy-start(bf16[128,1152]{1,0:T(8,128)(2,1)} %copy-done.24) | copy-start | bytes 884740
  87.3 4.0 %copy-start.30 = (bf16[128,1152]{1,0:T(8,128)(2,1)S(1)}, bf16[128,1152]{1,0:T(8,128)(2,1)}, u32[]{:S(2)}) copy-start(bf16[128,1152]{1,0:T(8,128)(2,1)} %copy-done.29) | copy-start | bytes 884740
  97.9 1.6 %copy-start.3 = (f32[512,1152]{1,0:T(8,128)}, f32[512,1152]{1,0:T(8,128)S(1)}, u32[]{:S(2)}) copy-start(f32[512,1152]{1,0:T(8,128)S(1)} %fusion) | copy-start | bytes 7077892
  97.9 5.7 %copy-start.10 = (bf16[128,1152]{1,0:T(8,128)(2,1)S(1)}, bf16[128,1152]{1,0:T(8,128)(2,1)}, u32[]{:S(2)}) copy-start(bf16[128,1152]{1,0:T(8,128)(2,1)} %copy-done.8) | copy-start | bytes 884740
  97.9 5.7 %copy-start.18 = (bf16[128,1152]{1,0:T(8,128)(2,1)S(1)}, bf16[128,1152]{1,0:T(8,128)(2,1)}, u32[]{:S(2)}) copy-start(bf16[128,1152]{1,0:T(8,128)(2,1)} %copy-done.16) | copy-start | bytes 884740
  97.9 5.7 %copy-start.23 = (bf16[128,1152]{1,0:T(8,128)(2,1)S(1)}, bf16[128,1152]{1,0:T(8,128)(2,1)}, u32[]{:S(2)}) copy-start(bf16[128,1152]{1,0:T(8,128)(2,1)} %copy-done.21) | copy-start | bytes 884740
  97.9 5.7 %copy-start.28 = (bf16[128,1152]{1,0:T(8,128)(2,1)S(1)}, bf16[128,1152]{1,0:T(8,128)(2,1)}, u32[]{:S(2)}) copy-start(bf16[128,1152]{1,0:T(8,128)(2,1)} %copy-done.26) | copy-start | bytes 884740
  99.5 15.2 %collective-permute-start.26 = (bf16[2,128,1152]{2,1,0:T(8,128)(2,1)}, bf16[2,128,1152]{2,1,0:T(8,128)(2,1)}, u32[]{:S(2)}, u32[]{:S(2)}) collective-permute-start(bf16[2,128,1152]{2,1,0:T(8,128)(2,1)} %slice.65), channel_id=1, source_target_pairs={{0,1},{1,0},{2,3},{3,2},{4,5},{5,4},{6,7},{7,6},{8,9},{9,8},{10,11... | collective-permute-start | bytes 1769480 | tf_op jit(solution)/shard_map/ppermute | solution.py:26
  103.6 1.5 %copy-start.7 = (bf16[128,1152]{1,0:T(8,128)(2,1)}, bf16[128,1152]{1,0:T(8,128)(2,1)S(1)}, u32[]{:S(2)}) copy-start(bf16[128,1152]{1,0:T(8,128)(2,1)S(1)} %constant_dynamic-update-slice_fusion.6) | copy-start | bytes 884740
  103.7 1.4 %copy-start.13 = (f32[512]{0:T(512)S(1)}, f32[512]{0:T(512)}, u32[]{:S(2)}) copy-start(f32[512]{0:T(512)} %get-tuple-element.11) | copy-start | bytes 6148
  103.7 1.4 %copy-start.14 = (f32[512]{0:T(512)S(1)}, f32[512]{0:T(512)}, u32[]{:S(2)}) copy-start(f32[512]{0:T(512)} %get-tuple-element.7) | copy-start | bytes 6148
  103.7 1.4 %copy-start.15 = (f32[512]{0:T(512)S(1)}, f32[512]{0:T(512)}, u32[]{:S(2)}) copy-start(f32[512]{0:T(512)} %get-tuple-element.5) | copy-start | bytes 6148
  105.1 5.7 %copy-start.2 = (f32[512,1152]{1,0:T(8,128)S(1)}, f32[512,1152]{1,0:T(8,128)}, u32[]{:S(2)}) copy-start(f32[512,1152]{1,0:T(8,128)} %convolution_add_fusion.4) | copy-start | bytes 7077892
  105.7 3.1 %collective-permute-start.11 = (f32[2,128]{1,0:T(2,128)}, f32[2,128]{1,0:T(2,128)}, u32[]{:S(2)}, u32[]{:S(2)}) collective-permute-start(f32[2,128]{1,0:T(2,128)} %slice.55), channel_id=1, source_target_pairs={{0,1},{1,0},{2,3},{3,2},{4,5},{5,4},{6,7},{7,6},{8,9},{9,8},{10,11... | collective-permute-start | bytes 3080 | tf_op jit(solution)/shard_map/ppermute | solution.py:26
  109.5 4.7 %collective-permute-start.12 = (f32[128]{0:T(128)S(1)}, f32[128]{0:T(128)S(1)}, u32[]{:S(2)}, u32[]{:S(2)}) collective-permute-start(f32[128]{0:T(128)S(1)} %slice_bitcast_fusion.2), channel_id=1, source_target_pairs={{0,2},{1,3},{2,0},{3,1},{4,6},{5,7},{6,4},{7,5},{8,10},{9,11},{10,... | collective-permute-start | bytes 1544 | tf_op jit(solution)/shard_map/ppermute | solution.py:22
  113.2 1.7 %copy-start.4 = (f32[512,1152]{1,0:T(8,128)S(1)}, f32[512,1152]{1,0:T(8,128)}, u32[]{:S(2)}) copy-start(f32[512,1152]{1,0:T(8,128)} %copy-done.3) | copy-start | bytes 7077892
  113.4 3.0 %collective-permute-start.13 = (bf16[2,128,1152]{2,1,0:T(8,128)(2,1)S(1)}, bf16[2,128,1152]{2,1,0:T(8,128)(2,1)S(1)}, u32[]{:S(2)}, u32[]{:S(2)}) collective-permute-start(bf16[2,128,1152]{2,1,0:T(8,128)(2,1)S(1)} %slice.59), channel_id=1, source_target_pairs={{0,1},{1,0},{2,3},{3,2},{4,5},{5,4},{6,7},{7,6},{8,9},{9,8},{10,11... | collective-permute-start | bytes 1769480 | tf_op jit(solution)/shard_map/ppermute | solution.py:26
  116.1 7.9 %collective-permute-start.27 = (bf16[128,1152]{1,0:T(8,128)(2,1)S(1)}, bf16[128,1152]{1,0:T(8,128)(2,1)S(1)}, u32[]{:S(2)}, u32[]{:S(2)}) collective-permute-start(bf16[128,1152]{1,0:T(8,128)(2,1)S(1)} %fusion.53), channel_id=1, source_target_pairs={{0,2},{1,3},{2,0},{3,1},{4,6},{5,7},{6,4},{7,5},{8,10},{9,11},{10,... | collective-permute-start | bytes 884744 | tf_op jit(solution)/shard_map/ppermute | solution.py:22
  116.6 13.8 %copy-start.1 = (f32[128,1152]{1,0:T(8,128)S(1)}, f32[128,1152]{1,0:T(8,128)}, u32[]{:S(2)}) copy-start(f32[128,1152]{1,0:T(8,128)} %param.4) | copy-start | bytes 1769476
  116.6 13.7 %collective-permute-start.14 = (bf16[128,1152]{1,0:T(8,128)(2,1)S(1)}, bf16[128,1152]{1,0:T(8,128)(2,1)S(1)}, u32[]{:S(2)}, u32[]{:S(2)}) collective-permute-start(bf16[128,1152]{1,0:T(8,128)(2,1)S(1)} %fusion.52), channel_id=1, source_target_pairs={{0,2},{1,3},{2,0},{3,1},{4,6},{5,7},{6,4},{7,5},{8,10},{9,11},{10,... | collective-permute-start | bytes 884744 | tf_op jit(solution)/shard_map/ppermute | solution.py:22

commit v2 on v1

v2 whole, which is shorter than its diff:
```python
import functools

import jax
import jax.numpy as jnp
from jax import lax
from jax.experimental import pallas as pl
from jax.experimental.pallas import tpu as pltpu
from jax.sharding import PartitionSpec as P

BF16 = jnp.bfloat16
F32 = jnp.float32
RING = 8
PLANE = 4
EXTRA = 16
SMEM = pl.BlockSpec(memory_space=pltpu.SMEM)
VMEM = pl.BlockSpec(memory_space=pltpu.VMEM)


def along_z(rows):
    route = [
        (z * PLANE + q, ((z + (-1 if q % 2 else 1)) % RING) * PLANE + q)
        for z in range(RING)
        for q in range(PLANE)
    ]
    return lax.ppermute(rows, "blk", route)


def across_x(rows):
    return lax.ppermute(rows, "blk", [(i, i ^ 2) for i in range(RING * PLANE)])


def across_core(rows):
    return lax.ppermute(rows, "blk", [(i, i ^ 1) for i in range(RING * PLANE)])


def run(kernel, ins, outs, scalars=(), flops=0, in_place=None):
    shapes = [
        pltpu.VMEM(shape, dtype) if near else jax.ShapeDtypeStruct(shape, dtype)
        for shape, dtype, near in outs
    ]
    ins = [pltpu.with_memory_space_constraint(a, pltpu.VMEM) for a in ins]
    return pl.pallas_call(
        kernel,
        out_shape=shapes,
        in_specs=[SMEM] * len(scalars) + [VMEM] * len(ins),
        out_specs=[VMEM] * len(shapes),
        input_output_aliases=in_place or {},
        cost_estimate=pl.CostEstimate(flops=flops, bytes_accessed=0, transcendentals=0),
        compiler_params=pltpu.CompilerParams(vmem_limit_bytes=24 << 20),
    )(*scalars, *ins)


def hat_of(feats):
    scale = 1.0 / jnp.sqrt(jnp.sum(feats * feats, axis=1, keepdims=True) + 1e-06)
    return feats * scale, scale


def normalize_kernel(*refs):
    for feats_ref, low_ref in zip(refs[:2], refs[2:]):
        low_ref[...] = hat_of(feats_ref[...])[0].astype(BF16)


def normalize(captions, pictures):
    return run(normalize_kernel, [captions, pictures], [(captions.shape, BF16, True)] * 2)


def terms(mine, block, sharpness, shift, with_loss, home):
    dots = lax.dot_general(
        mine, block, (((1,), (1,)), ((), ())), preferred_element_type=F32
    )
    logits = sharpness * dots + shift
    e = jnp.exp(-jnp.abs(logits))
    t = 1.0 / (1.0 + e)
    upper = logits >= 0.0
    coeff = jnp.where(upper, t, e * t) * sharpness
    if home is not None:
        row = lax.broadcasted_iota(jnp.int32, logits.shape, 0) + home
        col = lax.broadcasted_iota(jnp.int32, logits.shape, 1)
        partner = row == col
        coeff = jnp.where(partner, -(jnp.where(upper, e * t, t) * sharpness), coeff)
        logits = jnp.where(partner, -logits, logits)
    loss = jnp.maximum(logits, 0.0) + jnp.log1p(e) if with_loss else None
    return coeff.astype(BF16), loss


def step_kernel(n, blocks, first, last, with_loss, chip_first, scale_ref, shift_ref, *refs):
    refs = list(refs)
    sharpness, shift = scale_ref[0], shift_ref[0]
    block_refs = [refs.pop(0) for _ in range(blocks)]
    if first:
        parts = [refs.pop(0) for _ in range(PLANE)]
        mine_ref = refs.pop(0)
        for k, part in enumerate(parts):
            mine_ref[pl.ds(k * n, n), :] = part[...]
    else:
        mine_ref, before_ref = refs.pop(0), refs.pop(0)
        loss_before_ref = refs.pop(0) if with_loss else None
    total_ref = refs.pop(0)
    loss_ref = refs.pop(0) if with_loss else None
    block = block_refs[0][...]
    if blocks > 1:
        block = jnp.concatenate([b[...] for b in block_refs], 0)
    chunk = 2 * n
    losses = []
    for k in range(PLANE * n // chunk):
        rows = pl.ds(k * chunk, chunk)
        coeff, loss = terms(
            mine_ref[rows, :], block, sharpness, shift, with_loss, k * chunk if first else None
        )
        total = jnp.dot(coeff, block, preferred_element_type=F32)
        if not first:
            total = total + before_ref[rows, :]
        if last and chip_first:
            if k == 0:
                total_ref[...] = total
            else:
                refs[0][pl.ds(0, chunk), :] = total.astype(BF16)
        elif last:
            total_ref[pl.ds(k * n, n), :] = total[:n]
            refs[0][pl.ds(k * n, n), :] = total[n:].astype(BF16)
        else:
            total_ref[rows, :] = total
        if with_loss:
            loss = functools.reduce(
                jnp.add, [loss[:, c * n : c * n + n] for c in range(loss.shape[1] // n)]
            )
            if not first:
                loss = loss + loss_before_ref[rows, :]
            if last:
                losses.append(jnp.sum(loss.T, axis=0, keepdims=True))
            else:
                loss_ref[rows, :] = loss
    if last:
        out_ref = refs[0]
        out_ref[pl.ds(2 * n, EXTRA), :] = jnp.zeros((EXTRA, out_ref.shape[1]), BF16)
        if with_loss:
            mine, theirs = losses
            if not chip_first:
                mine = jnp.concatenate([l[:, :n] for l in losses], 1)
                theirs = jnp.concatenate([l[:, n:] for l in losses], 1)
            loss_ref[...] = jnp.broadcast_to(mine, loss_ref.shape)
            out_ref[pl.ds(2 * n, EXTRA), pl.ds(0, 2 * n)] = in_three(theirs)


def in_three(value):
    high = value.astype(BF16)
    rest = value - high.astype(F32)
    middle = rest.astype(BF16)
    low = (rest - middle.astype(F32)).astype(BF16)
    row = lax.broadcasted_iota(jnp.int32, (EXTRA, value.shape[1]), 0)
    parts = jnp.zeros((EXTRA, value.shape[1]), F32)
    for k, part in enumerate((high, middle, low)):
        parts = jnp.where(row == k, part.astype(F32), parts)
    return parts.astype(BF16)


def from_three(rows):
    return jnp.sum(rows.astype(F32), axis=0, keepdims=True)


def step(blocks, mine, scalars, n, total=None, loss=None, with_loss=False, last=False, chip_first=False):
    width = blocks[0].shape[1]
    first = total is None
    ins = list(blocks) + (list(mine) if first else [mine, total])
    if with_loss and not first:
        ins.append(loss)
    outs = [((PLANE * n, width), BF16, True)] if first else []
    if last:
        outs += [((2 * n, width), F32, True)]
        outs += [((8, 2 * n), F32, True)] if with_loss else []
        outs += [((2 * n + EXTRA, width), BF16, True)]
    else:
        outs += [((PLANE * n, width), F32, True)]
        outs += [((PLANE * n, n), F32, True)] if with_loss else []
    flops = 0
    kernel = functools.partial(step_kernel, n, len(blocks), first, last, with_loss, chip_first)
    return run(kernel, ins, outs, scalars, flops)


def pass_on_kernel(n, with_loss, kept_ref, *refs):
    loss_ref = refs[0] if with_loss else None
    got_ref, out_ref = refs[int(with_loss) : int(with_loss) + 2]
    other = kept_ref[pl.ds(n, n), :] + got_ref[pl.ds(n, n), :].astype(F32)
    out_ref[...] = other.astype(BF16)
    if with_loss:
        loss = loss_ref[0:1, pl.ds(n, n)] + from_three(got_ref[pl.ds(2 * n, EXTRA), pl.ds(n, n)])
        refs[-1][...] = in_three(loss)


def finish_kernel(n, with_loss, feats_ref, kept_ref, *refs):
    first_ref, second_ref = refs[:2]
    grad_ref = refs[4] if with_loss else refs[2]
    grad = (
        kept_ref[pl.ds(0, n), :]
        + first_ref[pl.ds(0, n), :].astype(F32)
        + second_ref[...].astype(F32)
    )
    hat, scale = hat_of(feats_ref[...])
    grad_ref[...] = scale * (grad - hat * jnp.sum(hat * grad, axis=1, keepdims=True))
    if with_loss:
        loss_ref, third_ref = refs[2:4]
        refs[5][...] = (
            loss_ref[0:1, pl.ds(0, n)]
            + from_three(first_ref[pl.ds(2 * n, EXTRA), pl.ds(0, n)])
            + from_three(third_ref[...])
        )


def pass_on(kept, got, loss=None):
    n, width = kept.shape[0] // 2, kept.shape[1]
    with_loss = loss is not None
    outs = [((n, width), BF16, True)] + ([((EXTRA, n), BF16, True)] if with_loss else [])
    return run(
        functools.partial(pass_on_kernel, n, with_loss),
        [kept, *([loss] if with_loss else []), got],
        outs,
    )


def finish(feats, kept, first, second, *losses):
    n, width = feats.shape
    with_loss = len(losses) > 0
    outs = [((n, width), F32, False)] + ([((1, n), F32, False)] if with_loss else [])
    return run(
        functools.partial(finish_kernel, n, with_loss),
        [feats, kept, first, second, *losses],
        outs,
    )


def after(value, *done):
    return lax.optimization_barrier((value, *done))[0]


def body(pictures, captions, sharpness_scale, offset_shift_vector):
    n = pictures.shape[0]
    scalars = (sharpness_scale, offset_shift_vector)
    text, image = normalize(captions, pictures)
    text_core, image_core = across_core(text), across_core(image)
    ta1, tb1 = along_z(text), along_z(text_core)
    ia1 = along_z(image)
    image_chip = across_x(image)
    images = [image, image_core, image_chip, across_core(image_chip)]
    text_chip = across_x(after(text, image_chip))
    texts = [text, text_core, text_chip, across_core(text_chip)]
    ta2 = along_z(ta1)
    tb2 = along_z(tb1)
    ib1 = along_z(after(image_core, ia1))
    mine_i, a0, loss = step([after(text, ia1)], images, scalars, n, with_loss=True)
    ta3 = along_z(ta2)
    a1, loss = step([ta1, after(tb1, ta2)], mine_i, scalars, n, a0, loss, True)
    tb3 = along_z(after(tb2, a0))
    a2, loss = step([ta2, after(tb2, text_chip)], mine_i, scalars, n, a1, loss, True)
    ta4 = along_z(after(ta3, a0))
    ia2 = along_z(after(ia1, ib1))
    mine_t, b0 = step([after(image, ib1)], texts, scalars, n)
    b1, = step([ia1, ib1], mine_t, scalars, n, b0)
    ib2 = along_z(after(ib1, ta3))
    ia3 = along_z(ia2)
    a3, loss = step([ta3, tb3], mine_i, scalars, n, a2, loss, True)
    ib3 = along_z(ib2)
    kept_i, loss, for_chip_i = step([ta4], mine_i, scalars, n, a3, loss, True, True, True)
    by_chip_i = across_x(for_chip_i)
    ia4 = along_z(ia3)
    b2, = step([ia2, ib2], mine_t, scalars, n, b1)
    b3, = step([ia3, ib3], mine_t, scalars, n, b2)
    kept, for_core = step([after(ia4, by_chip_i)], mine_t, scalars, n, b3, last=True)
    by_core = across_core(for_core)
    for_chip = pass_on(kept, by_core)[0]
    by_chip = across_x(for_chip)
    for_core_i, loss_low = pass_on(after(kept_i, for_chip), by_chip_i, loss)
    by_core_i = across_core(for_core_i)
    loss_by_core = across_core(loss_low)
    grad_image, loss_rows = finish(pictures, kept_i, by_chip_i, by_core_i, loss, loss_by_core)

    grad_text = finish(after(captions, grad_image), kept, by_core, by_chip)[0]
    return (loss_rows.reshape(n), grad_image, grad_text)


def solution(mesh):
    in_specs = (P(("group", "blk"), None), P(("group", "blk"), None), P(), P())
    out_specs = (P(("group", "blk")), P(("group", "blk"), None), P(("group", "blk"), None))
    return jax.shard_map(body, mesh=mesh, in_specs=in_specs, out_specs=out_specs, check_vma=False)
```

time: 132 us -> 77.3 us (0.59)
  matrix products: 37.9 us -> 0 us
  Pallas kernels: 0 us -> 18.4 us
  local copies, waits for them, and re-layouts: 19.6 us -> 2.14 us
  other arithmetic: 8.91 us -> 0 us
  waiting for transfers between devices: 22.1 us -> 14.9 us
    dot_general x15 -> x0, matrix products: 37.9 us -> none  [the longest x8 25.9 us: away_terms(): grad = jnp.dot(coeff, block, preferred_element_type=F32)]
    pallas_call x0 -> x15, Pallas kernels: none -> 18.4 us  [run(): pl.pallas_call(kernel, out_shape=shapes, in_specs=[SMEM] * len(scalars) +...]
    slice x8 -> x0, local copies, waits for them, and re-layouts: 6.63 us -> none  [the longest x4 5.1 us: gather_z(): steps.append((along_z(right[:half], 1), along_z(left[half:], -1)))]
    ppermute x5 -> x4, waiting for transfers between devices: 11.2 us -> 5.33 us  [across_x(): return lax.ppermute(rows, 'blk', [(i, i ^ 2) for i in range(RING * PLANE)])]
    concatenate x8 -> x0, local copies, waits for them, and re-layouts: 5.68 us -> none  [side(): jnp.concatenate(pair, 0)]
    unnamed x70 -> x8, local copies, waits for them, and re-layouts: 7.16 us -> 2.14 us
    ppermute x16 -> x14, waiting for transfers between devices: 10.9 us -> 7.06 us  [along_z(): return lax.ppermute(rows, 'blk', route)]
    reduce_sum x4 -> x0, other arithmetic: 2.87 us -> none  [the longest x2 2.43 us: normalize(): jnp.sum(feats * feats, axis=1, keepdims=True) + 1e-06]
  transfers between devices with their start and end apart: 28 -> 25, of which waited for: 5 -> 7; matrix products, arithmetic and copies ran while one was open for 47% -> 0% of each run, Pallas kernels for 0% -> 20%
where the time goes in v2:
time: 77.3 us; the launch traced here: 77.2 us
  starting transfers between devices  39.6 us (51%)
  Pallas kernels  18.4 us (24%)
  waiting for transfers between devices  14.9 us (19%)
  local copies, waits for them, and re-layouts  2.14 us (3%)
  between operations  2.1 us (3%)
    ppermute x14, starting transfers between devices, along_z(): return lax.ppermute(rows, 'blk', route)  26.1 us
    pallas_call x15, Pallas kernels, run(): pl.pallas_call(kernel, out_shape=shapes, in_specs=[SMEM] * len(scalars) +...  18.4 us
    ppermute x7, starting transfers between devices, across_core(): return lax.ppermute(rows, 'blk', [(i, i ^ 1) for i in range(RING * PLANE)])  8.86 us
    ppermute x14, waiting for transfers between devices, along_z(): return lax.ppermute(rows, 'blk', route)  7.06 us
    ppermute x4, waiting for transfers between devices, across_x(): return lax.ppermute(rows, 'blk', [(i, i ^ 2) for i in range(RING * PLANE)])  5.33 us
    ppermute x4, starting transfers between devices, across_x(): return lax.ppermute(rows, 'blk', [(i, i ^ 2) for i in range(RING * PLANE)])  4.58 us
    ppermute x7, waiting for transfers between devices, across_core(): return lax.ppermute(rows, 'blk', [(i, i ^ 1) for i in range(RING * PLANE)])  2.52 us
    unnamed x8, local copies, waits for them, and re-layouts  2.14 us
  transfers between devices with their start and end apart: 25, of which 7 were waited for; matrix products, arithmetic and copies ran while one was open for 0% of the time, Pallas kernels for 20%

profile of v2, /device:TPU:1, one launch (start us, length us, event | category | flops | bytes accessed | tf_op | source)
XLA Modules:
  0.0 77.2 jit_solution(10997774863479467895)
XLA Ops:
  0.6 0.0 copy-start
  0.6 1.1 %copy-done = f32[128,1152]{1,0:T(8,128)S(1)} copy-done((f32[128,1152]{1,0:T(8,128)S(1)}, f32[128,1152]{1,0:T(8,128)}, u32[]{:S(2)}) %copy-start) | copy-done | bytes 589848
  1.7 1.1 %copy-done.2 = f32[128,1152]{1,0:T(8,128)S(1)} copy-done((f32[128,1152]{1,0:T(8,128)S(1)}, f32[128,1152]{1,0:T(8,128)}, u32[]{:S(2)}) %copy-start.2) | copy-done | bytes 589848
  2.8 0.2 shard_map.67
  3.0 3.3 %collective-permute-start.8 = (bf16[128,1152]{1,0:T(8,128)(2,1)S(1)}, bf16[128,1152]{1,0:T(8,128)(2,1)S(1)}, u32[]{:S(2)}, u32[]{:S(2)}) collective-permute-start(bf16[128,1152]{1,0:T(8,128)(2,1)S(1)} %get-tuple-element.45.refs_0_.refs_1_), channel_id=1, source_target_pairs={{0,1},{1,0},{2,3},{3,2},{4,5},{5,4},{6,7},{7,6},{8,9},{9,8},{10,11... | collective-permute-start | bytes 884744 | tf_op jit(solution)/shard_map/ppermute | solution.py:33
  6.3 3.8 %collective-permute-start = (bf16[128,1152]{1,0:T(8,128)(2,1)S(1)}, bf16[128,1152]{1,0:T(8,128)(2,1)S(1)}, u32[]{:S(2)}, u32[]{:S(2)}) collective-permute-start(bf16[128,1152]{1,0:T(8,128)(2,1)S(1)} %get-tuple-element.45.refs_0_.refs_1_), channel_id=1, source_target_pairs={{0,4},{1,29},{2,6},{3,31},{4,8},{5,1},{6,10},{7,3},{8,12},{9,5},{1... | collective-permute-start | bytes 884744 | tf_op jit(solution)/shard_map/ppermute | solution.py:25
  10.1 1.2 %collective-permute-start.5 = (bf16[128,1152]{1,0:T(8,128)(2,1)S(1)}, bf16[128,1152]{1,0:T(8,128)(2,1)S(1)}, u32[]{:S(2)}, u32[]{:S(2)}) collective-permute-start(bf16[128,1152]{1,0:T(8,128)(2,1)S(1)} %get-tuple-element.60.refs_1_.refs_0_), channel_id=1, source_target_pairs={{0,2},{1,3},{2,0},{3,1},{4,6},{5,7},{6,4},{7,5},{8,10},{9,11},{10,... | collective-permute-start | bytes 884744 | tf_op jit(solution)/shard_map/ppermute | solution.py:29
  11.3 0.0 collective-permute-done.8.refs_2_
  11.4 0.7 collective-permute-start.9
  12.1 1.7 %collective-permute-done.refs_0_ = bf16[128,1152]{1,0:T(8,128)(2,1)S(1)} collective-permute-done((bf16[128,1152]{1,0:T(8,128)(2,1)S(1)}, bf16[128,1152]{1,0:T(8,128)(2,1)S(1)}, u32[]{:S(2)}, u32[]{:S(2)}) %collective-permute-start) | collective-permute-done | bytes 294944 | tf_op jit(solution)/shard_map/ppermute | solution.py:25
  13.8 3.1 %collective-permute-start.1 = (bf16[128,1152]{1,0:T(8,128)(2,1)S(1)}, bf16[128,1152]{1,0:T(8,128)(2,1)S(1)}, u32[]{:S(2)}, u32[]{:S(2)}) collective-permute-start(bf16[128,1152]{1,0:T(8,128)(2,1)S(1)} %collective-permute-done.refs_0_), channel_id=1, source_target_pairs={{0,4},{1,29},{2,6},{3,31},{4,8},{5,1},{6,10},{7,3},{8,12},{9,5},{1... | collective-permute-start | bytes 884744 | tf_op jit(solution)/shard_map/ppermute | solution.py:25
  16.9 0.0 collective-permute-start.3
  17.0 0.0 collective-permute-start.4
  17.0 0.0 collective-permute-done.5.refs_3_
  17.0 0.5 collective-permute-start.6
  17.5 2.7 %collective-permute-start.10 = (bf16[128,1152]{1,0:T(8,128)(2,1)S(1)}, bf16[128,1152]{1,0:T(8,128)(2,1)S(1)}, u32[]{:S(2)}, u32[]{:S(2)}) collective-permute-start(bf16[128,1152]{1,0:T(8,128)(2,1)S(1)} %collective-permute-done.9.refs_1_), channel_id=1, source_target_pairs={{0,4},{1,29},{2,6},{3,31},{4,8},{5,1},{6,10},{7,3},{8,12},{9,5},{1... | collective-permute-start | bytes 884744 | tf_op jit(solution)/shard_map/ppermute | solution.py:25
  20.1 0.5 collective-permute-done.1.refs_0_
  20.6 3.1 %collective-permute-start.2 = (bf16[128,1152]{1,0:T(8,128)(2,1)S(1)}, bf16[128,1152]{1,0:T(8,128)(2,1)S(1)}, u32[]{:S(2)}, u32[]{:S(2)}) collective-permute-start(bf16[128,1152]{1,0:T(8,128)(2,1)S(1)} %collective-permute-done.1.refs_0_), channel_id=1, source_target_pairs={{0,4},{1,29},{2,6},{3,31},{4,8},{5,1},{6,10},{7,3},{8,12},{9,5},{1... | collective-permute-start | bytes 884744 | tf_op jit(solution)/shard_map/ppermute | solution.py:25
  23.7 0.0 collective-permute-done.3.refs_0_
  23.8 3.1 %collective-permute-start.14 = (bf16[128,1152]{1,0:T(8,128)(2,1)S(1)}, bf16[128,1152]{1,0:T(8,128)(2,1)S(1)}, u32[]{:S(2)}, u32[]{:S(2)}) collective-permute-start(bf16[128,1152]{1,0:T(8,128)(2,1)S(1)} %collective-permute-done.4.refs_2_), channel_id=1, source_target_pairs={{0,4},{1,29},{2,6},{3,31},{4,8},{5,1},{6,10},{7,3},{8,12},{9,5},{1... | collective-permute-start | bytes 884744 | tf_op jit(solution)/shard_map/ppermute | solution.py:25
  28.2 1.3 %collective-permute-start.12 = (bf16[128,1152]{1,0:T(8,128)(2,1)S(1)}, bf16[128,1152]{1,0:T(8,128)(2,1)S(1)}, u32[]{:S(2)}, u32[]{:S(2)}) collective-permute-start(bf16[128,1152]{1,0:T(8,128)(2,1)S(1)} %get-tuple-element.45.refs_0_.refs_1_), channel_id=1, source_target_pairs={{0,2},{1,3},{2,0},{3,1},{4,6},{5,7},{6,4},{7,5},{8,10},{9,11},{10,... | collective-permute-start | bytes 884744 | tf_op jit(solution)/shard_map/ppermute | solution.py:29
  29.5 0.0 collective-permute-done.6.refs_4_
  29.5 1.3 %shard_map.68 = (bf16[512,1152]{1,0:T(8,128)(2,1)S(1)}, f32[512,1152]{1,0:T(8,128)S(1)}, f32[512,128]{1,0:T(8,128)S(1)}) custom-call(f32[1]{0:T(128)S(6)} %copy.7.scale_ref, f32[1]{0:T(128)S(6)} %copy.8.shift_ref, bf16[128,1152]{1,0:T(8,128)(2,1)S(1)} %get-tuple-element.45.refs_0_.refs_1_, bf16[128,1152]{1,0:T(8,128)(2,1)S(1)} %get-tuple-element.60.refs_1_.refs_0_, ...), custom_call_target="tpu_custom_call" | custom-call | tf_op jit(solution)/shard_map/pallas_call | solution.py:42
  30.7 0.0 collective-permute-done.10.refs_1_
  30.8 0.1 collective-permute-start.11
  30.8 0.0 collective-permute-done.2.refs_0_
  30.9 2.3 %collective-permute-start.7 = (bf16[128,1152]{1,0:T(8,128)(2,1)S(1)}, bf16[128,1152]{1,0:T(8,128)(2,1)S(1)}, u32[]{:S(2)}, u32[]{:S(2)}) collective-permute-start(bf16[128,1152]{1,0:T(8,128)(2,1)S(1)} %collective-permute-done.2.refs_0_), channel_id=1, source_target_pairs={{0,4},{1,29},{2,6},{3,31},{4,8},{5,1},{6,10},{7,3},{8,12},{9,5},{1... | collective-permute-start | bytes 884744 | tf_op jit(solution)/shard_map/ppermute | solution.py:25
  33.2 0.0 collective-permute-done.14.refs_1_
  33.2 3.1 %collective-permute-start.15 = (bf16[128,1152]{1,0:T(8,128)(2,1)S(1)}, bf16[128,1152]{1,0:T(8,128)(2,1)S(1)}, u32[]{:S(2)}, u32[]{:S(2)}) collective-permute-start(bf16[128,1152]{1,0:T(8,128)(2,1)S(1)} %collective-permute-done.3.refs_0_), channel_id=1, source_target_pairs={{0,4},{1,29},{2,6},{3,31},{4,8},{5,1},{6,10},{7,3},{8,12},{9,5},{1... | collective-permute-start | bytes 884744 | tf_op jit(solution)/shard_map/ppermute | solution.py:25
  36.3 1.9 %shard_map.69 = (f32[512,1152]{1,0:T(8,128)S(1)}, f32[512,128]{1,0:T(8,128)S(1)}) custom-call(f32[1]{0:T(128)S(6)} %copy.7.scale_ref, f32[1]{0:T(128)S(6)} %copy.8.shift_ref, bf16[128,1152]{1,0:T(8,128)(2,1)S(1)} %collective-permute-done.refs_0_, bf16[128,1152]{1,0:T(8,128)(2,1)S(1)} %collective-permute-done.9.refs_1_, ...), custom_call_target="tpu_custom_call" | custom-call | tf_op jit(solution)/shard_map/pallas_call | solution.py:42
  38.3 1.9 %shard_map.70 = (f32[512,1152]{1,0:T(8,128)S(1)}, f32[512,128]{1,0:T(8,128)S(1)}) custom-call(f32[1]{0:T(128)S(6)} %copy.7.scale_ref, f32[1]{0:T(128)S(6)} %copy.8.shift_ref, bf16[128,1152]{1,0:T(8,128)(2,1)S(1)} %collective-permute-done.1.refs_0_, bf16[128,1152]{1,0:T(8,128)(2,1)S(1)} %collective-permute-done.10.refs_1_, ...), custom_call_target="tpu_custom_call" | custom-call | tf_op jit(solution)/shard_map/pallas_call | solution.py:42
  40.2 1.9 %shard_map.71 = (f32[512,1152]{1,0:T(8,128)S(1)}, f32[512,128]{1,0:T(8,128)S(1)}) custom-call(f32[1]{0:T(128)S(6)} %copy.7.scale_ref, f32[1]{0:T(128)S(6)} %copy.8.shift_ref, bf16[128,1152]{1,0:T(8,128)(2,1)S(1)} %collective-permute-done.2.refs_0_, bf16[128,1152]{1,0:T(8,128)(2,1)S(1)} %collective-permute-done.11.refs_1_, ...), custom_call_target="tpu_custom_call" | custom-call | tf_op jit(solution)/shard_map/pallas_call | solution.py:42
  42.1 1.2 %shard_map.72 = (f32[256,1152]{1,0:T(8,128)S(1)}, f32[8,256]{1,0:T(8,128)S(1)}, bf16[272,1152]{1,0:T(8,128)(2,1)S(1)}) custom-call(f32[1]{0:T(128)S(6)} %copy.7.scale_ref, f32[1]{0:T(128)S(6)} %copy.8.shift_ref, bf16[128,1152]{1,0:T(8,128)(2,1)S(1)} %collective-permute-done.7.refs_0_, bf16[512,1152]{1,0:T(8,128)(2,1)S(1)} %get-tuple-element.43.refs_2_.refs_1_, ...), custom_call_target="tpu_custom_call" | custom-call | tf_op jit(solution)/shard_map/pallas_call | solution.py:42
  43.4 1.3 %collective-permute-start.13 = (bf16[272,1152]{1,0:T(8,128)(2,1)S(1)}, bf16[272,1152]{1,0:T(8,128)(2,1)S(1)}, u32[]{:S(2)}, u32[]{:S(2)}) collective-permute-start(bf16[272,1152]{1,0:T(8,128)(2,1)S(1)} %get-tuple-element.56), channel_id=1, source_target_pairs={{0,2},{1,3},{2,0},{3,1},{4,6},{5,7},{6,4},{7,5},{8,10},{9,11},{10,... | collective-permute-start | bytes 1880072 | tf_op jit(solution)/shard_map/ppermute | solution.py:29
  44.7 0.5 collective-permute-start.19
  45.2 0.0 collective-permute-done.15.refs_0_
  45.2 0.6 collective-permute-start.16
  45.8 1.7 %collective-permute-start.18 = (bf16[128,1152]{1,0:T(8,128)(2,1)S(1)}, bf16[128,1152]{1,0:T(8,128)(2,1)S(1)}, u32[]{:S(2)}, u32[]{:S(2)}) collective-permute-start(bf16[128,1152]{1,0:T(8,128)(2,1)S(1)} %collective-permute-done.12.refs_3_), channel_id=1, source_target_pairs={{0,1},{1,0},{2,3},{3,2},{4,5},{5,4},{6,7},{7,6},{8,9},{9,8},{10,11... | collective-permute-start | bytes 884744 | tf_op jit(solution)/shard_map/ppermute | solution.py:33
  47.5 3.0 %collective-permute-done.19.refs_1_ = bf16[128,1152]{1,0:T(8,128)(2,1)S(1)} collective-permute-done((bf16[128,1152]{1,0:T(8,128)(2,1)S(1)}, bf16[128,1152]{1,0:T(8,128)(2,1)S(1)}, u32[]{:S(2)}, u32[]{:S(2)}) %collective-permute-start.19) | collective-permute-done | bytes 294944 | tf_op jit(solution)/shard_map/ppermute | solution.py:25
  50.6 1.4 %collective-permute-start.20 = (bf16[128,1152]{1,0:T(8,128)(2,1)S(1)}, bf16[128,1152]{1,0:T(8,128)(2,1)S(1)}, u32[]{:S(2)}, u32[]{:S(2)}) collective-permute-start(bf16[128,1152]{1,0:T(8,128)(2,1)S(1)} %collective-permute-done.19.refs_1_), channel_id=1, source_target_pairs={{0,4},{1,29},{2,6},{3,31},{4,8},{5,1},{6,10},{7,3},{8,12},{9,5},{1... | collective-permute-start | bytes 884744 | tf_op jit(solution)/shard_map/ppermute | solution.py:25
  52.0 1.7 %collective-permute-done.16.refs_0_ = bf16[128,1152]{1,0:T(8,128)(2,1)S(1)} collective-permute-done((bf16[128,1152]{1,0:T(8,128)(2,1)S(1)}, bf16[128,1152]{1,0:T(8,128)(2,1)S(1)}, u32[]{:S(2)}, u32[]{:S(2)}) %collective-permute-start.16) | collective-permute-done | bytes 294944 | tf_op jit(solution)/shard_map/ppermute | solution.py:25
  53.7 1.4 %collective-permute-start.17 = (bf16[128,1152]{1,0:T(8,128)(2,1)S(1)}, bf16[128,1152]{1,0:T(8,128)(2,1)S(1)}, u32[]{:S(2)}, u32[]{:S(2)}) collective-permute-start(bf16[128,1152]{1,0:T(8,128)(2,1)S(1)} %collective-permute-done.16.refs_0_), channel_id=1, source_target_pairs={{0,4},{1,29},{2,6},{3,31},{4,8},{5,1},{6,10},{7,3},{8,12},{9,5},{1... | collective-permute-start | bytes 884744 | tf_op jit(solution)/shard_map/ppermute | solution.py:25
  55.2 0.0 collective-permute-done.18.refs_4_
  55.2 1.2 %shard_map.73 = (bf16[512,1152]{1,0:T(8,128)(2,1)S(1)}, f32[512,1152]{1,0:T(8,128)S(1)}) custom-call(f32[1]{0:T(128)S(6)} %copy.7.scale_ref, f32[1]{0:T(128)S(6)} %copy.8.shift_ref, bf16[128,1152]{1,0:T(8,128)(2,1)S(1)} %get-tuple-element.60.refs_1_.refs_0_, bf16[128,1152]{1,0:T(8,128)(2,1)S(1)} %get-tuple-element.45.refs_0_.refs_1_, ...), custom_call_target="tpu_custom_call" | custom-call | tf_op jit(solution)/shard_map/pallas_call | solution.py:42
  56.4 1.7 %shard_map.74.refs_3_ = f32[512,1152]{1,0:T(8,128)S(1)} custom-call(f32[1]{0:T(128)S(6)} %copy.7.scale_ref, f32[1]{0:T(128)S(6)} %copy.8.shift_ref, bf16[128,1152]{1,0:T(8,128)(2,1)S(1)} %collective-permute-done.3.refs_0_, bf16[128,1152]{1,0:T(8,128)(2,1)S(1)} %collective-permute-done.14.refs_1_, bf16[512,1152]{1,0:T(8,128)(2,1)S(1)} %get-tuple-element.61.refs_2_.refs_1_, ...), custom_call_target="tpu_custom_call" | custom-call | tf_op jit(solution)/shard_map/pallas_call | solution.py:42
  58.1 1.7 %shard_map.75.refs_3_ = f32[512,1152]{1,0:T(8,128)S(1)} custom-call(f32[1]{0:T(128)S(6)} %copy.7.scale_ref, f32[1]{0:T(128)S(6)} %copy.8.shift_ref, bf16[128,1152]{1,0:T(8,128)(2,1)S(1)} %collective-permute-done.15.refs_0_, bf16[128,1152]{1,0:T(8,128)(2,1)S(1)} %collective-permute-done.19.refs_1_, bf16[512,1152]{1,0:T(8,128)(2,1)S(1)} %get-tuple-element.61.refs_2_.refs_1_, ...), custom_call_target="tpu_custom_call" | custom-call | tf_op jit(solution)/shard_map/pallas_call | solution.py:42
  59.8 0.0 collective-permute-done.20.refs_1_
  59.9 1.7 %shard_map.76.refs_2_ = f32[512,1152]{1,0:T(8,128)S(1)} custom-call(f32[1]{0:T(128)S(6)} %copy.7.scale_ref, f32[1]{0:T(128)S(6)} %copy.8.shift_ref, bf16[128,1152]{1,0:T(8,128)(2,1)S(1)} %collective-permute-done.16.refs_0_, bf16[128,1152]{1,0:T(8,128)(2,1)S(1)} %collective-permute-done.20.refs_1_, bf16[512,1152]{1,0:T(8,128)(2,1)S(1)} %get-tuple-element.61.refs_2_.refs_1_, ...), custom_call_target="tpu_custom_call" | custom-call | tf_op jit(solution)/shard_map/pallas_call | solution.py:42
  61.6 0.0 collective-permute-done.17.refs_0_
  61.6 1.2 %shard_map.77 = (f32[256,1152]{1,0:T(8,128)S(1)}, bf16[272,1152]{1,0:T(8,128)(2,1)S(1)}) custom-call(f32[1]{0:T(128)S(6)} %copy.7.scale_ref, f32[1]{0:T(128)S(6)} %copy.8.shift_ref, bf16[128,1152]{1,0:T(8,128)(2,1)S(1)} %collective-permute-done.17.refs_0_, bf16[512,1152]{1,0:T(8,128)(2,1)S(1)} %get-tuple-element.61.refs_2_.refs_1_, ...), custom_call_target="tpu_custom_call" | custom-call | tf_op jit(solution)/shard_map/pallas_call | solution.py:42
  62.8 0.0 copy-start.3
  62.8 2.4 %collective-permute-start.21 = (bf16[272,1152]{1,0:T(8,128)(2,1)S(1)}, bf16[272,1152]{1,0:T(8,128)(2,1)S(1)}, u32[]{:S(2)}, u32[]{:S(2)}) collective-permute-start(bf16[272,1152]{1,0:T(8,128)(2,1)S(1)} %get-tuple-element.65), channel_id=1, source_target_pairs={{0,1},{1,0},{2,3},{3,2},{4,5},{5,4},{6,7},{7,6},{8,9},{9,8},{10,11... | collective-permute-start | bytes 1880072 | tf_op jit(solution)/shard_map/ppermute | solution.py:33
  65.3 1.7 %collective-permute-done.21.refs_0_ = bf16[272,1152]{1,0:T(8,128)(2,1)S(1)} collective-permute-done((bf16[272,1152]{1,0:T(8,128)(2,1)S(1)}, bf16[272,1152]{1,0:T(8,128)(2,1)S(1)}, u32[]{:S(2)}, u32[]{:S(2)}) %collective-permute-start.21) | collective-permute-done | bytes 626720 | tf_op jit(solution)/shard_map/ppermute | solution.py:33
  67.0 0.1 shard_map.78
  67.0 0.0 copy-start.1
  67.0 0.1 shard_map.79
  67.1 0.5 collective-permute-start.22
  67.6 0.8 collective-permute-start.24
  68.3 0.4 collective-permute-start.23
  68.8 0.8 %collective-permute-done.23.refs_3_ = bf16[16,128]{1,0:T(8,128)(2,1)S(1)} collective-permute-done((bf16[16,128]{1,0:T(8,128)(2,1)S(1)}, bf16[16,128]{1,0:T(8,128)(2,1)S(1)}, u32[]{:S(2)}, u32[]{:S(2)}) %collective-permute-start.23) | collective-permute-done | bytes 4128 | tf_op jit(solution)/shard_map/ppermute | solution.py:33
  69.6 0.0 collective-permute-done.22.refs_1_
  69.6 1.1 %shard_map.80 = (f32[128,1152]{1,0:T(8,128)}, f32[1,128]{1,0:T(1,128)}) custom-call(f32[128,1152]{1,0:T(8,128)S(1)} %copy-done.3, f32[256,1152]{1,0:T(8,128)S(1)} %get-tuple-element.66.kept_ref, bf16[272,1152]{1,0:T(8,128)(2,1)S(1)} %collective-permute-done.13.refs_1_.refs_0_, bf16[128,1152]{1,0:T(8,128)(2,1)S(1)} %collective-permute-done.22.refs_1_, ...), custom_call_target="tpu_custom_call" | custom-call | tf_op jit(solution)/shard_map/pallas_call | solution.py:42
  70.7 5.3 %collective-permute-done.24.refs_1_ = bf16[128,1152]{1,0:T(8,128)(2,1)S(1)} collective-permute-done((bf16[128,1152]{1,0:T(8,128)(2,1)S(1)}, bf16[128,1152]{1,0:T(8,128)(2,1)S(1)}, u32[]{:S(2)}, u32[]{:S(2)}) %collective-permute-start.24) | collective-permute-done | bytes 294944 | tf_op jit(solution)/shard_map/ppermute | solution.py:29
  76.0 1.1 %shard_map.81 = f32[128,1152]{1,0:T(8,128)} custom-call(f32[128,1152]{1,0:T(8,128)S(1)} %copy-done.1, f32[256,1152]{1,0:T(8,128)S(1)} %get-tuple-element.64.kept_ref, bf16[272,1152]{1,0:T(8,128)(2,1)S(1)} %collective-permute-done.21.refs_0_, bf16[128,1152]{1,0:T(8,128)(2,1)S(1)} %collective-permute-done.24.refs_1_), custom_call_target="tpu_custom_call" | custom-call | tf_op jit(solution)/shard_map/pallas_call | solution.py:42
  (9 shorter events, 0.0 us)
Async XLA Ops:
  0.6 1.1 %copy-start = (f32[128,1152]{1,0:T(8,128)S(1)}, f32[128,1152]{1,0:T(8,128)}, u32[]{:S(2)}) copy-start(f32[128,1152]{1,0:T(8,128)} %feats_ref.2) | copy-start | bytes 1769476
  1.7 1.1 %copy-start.2 = (f32[128,1152]{1,0:T(8,128)S(1)}, f32[128,1152]{1,0:T(8,128)}, u32[]{:S(2)}) copy-start(f32[128,1152]{1,0:T(8,128)} %feats_ref.1) | copy-start | bytes 1769476
  3.0 8.4 %collective-permute-start.8 = (bf16[128,1152]{1,0:T(8,128)(2,1)S(1)}, bf16[128,1152]{1,0:T(8,128)(2,1)S(1)}, u32[]{:S(2)}, u32[]{:S(2)}) collective-permute-start(bf16[128,1152]{1,0:T(8,128)(2,1)S(1)} %get-tuple-element.45.refs_0_.refs_1_), channel_id=1, source_target_pairs={{0,1},{1,0},{2,3},{3,2},{4,5},{5,4},{6,7},{7,6},{8,9},{9,8},{10,11... | collective-permute-start | bytes 884744 | tf_op jit(solution)/shard_map/ppermute | solution.py:33
  6.3 7.5 %collective-permute-start = (bf16[128,1152]{1,0:T(8,128)(2,1)S(1)}, bf16[128,1152]{1,0:T(8,128)(2,1)S(1)}, u32[]{:S(2)}, u32[]{:S(2)}) collective-permute-start(bf16[128,1152]{1,0:T(8,128)(2,1)S(1)} %get-tuple-element.45.refs_0_.refs_1_), channel_id=1, source_target_pairs={{0,4},{1,29},{2,6},{3,31},{4,8},{5,1},{6,10},{7,3},{8,12},{9,5},{1... | collective-permute-start | bytes 884744 | tf_op jit(solution)/shard_map/ppermute | solution.py:25
  10.1 6.8 %collective-permute-start.5 = (bf16[128,1152]{1,0:T(8,128)(2,1)S(1)}, bf16[128,1152]{1,0:T(8,128)(2,1)S(1)}, u32[]{:S(2)}, u32[]{:S(2)}) collective-permute-start(bf16[128,1152]{1,0:T(8,128)(2,1)S(1)} %get-tuple-element.60.refs_1_.refs_0_), channel_id=1, source_target_pairs={{0,2},{1,3},{2,0},{3,1},{4,6},{5,7},{6,4},{7,5},{8,10},{9,11},{10,... | collective-permute-start | bytes 884744 | tf_op jit(solution)/shard_map/ppermute | solution.py:29
  11.4 6.1 %collective-permute-start.9 = (bf16[128,1152]{1,0:T(8,128)(2,1)S(1)}, bf16[128,1152]{1,0:T(8,128)(2,1)S(1)}, u32[]{:S(2)}, u32[]{:S(2)}) collective-permute-start(bf16[128,1152]{1,0:T(8,128)(2,1)S(1)} %collective-permute-done.8.refs_2_), channel_id=1, source_target_pairs={{0,4},{1,29},{2,6},{3,31},{4,8},{5,1},{6,10},{7,3},{8,12},{9,5},{1... | collective-permute-start | bytes 884744 | tf_op jit(solution)/shard_map/ppermute | solution.py:25
  13.8 6.8 %collective-permute-start.1 = (bf16[128,1152]{1,0:T(8,128)(2,1)S(1)}, bf16[128,1152]{1,0:T(8,128)(2,1)S(1)}, u32[]{:S(2)}, u32[]{:S(2)}) collective-permute-start(bf16[128,1152]{1,0:T(8,128)(2,1)S(1)} %collective-permute-done.refs_0_), channel_id=1, source_target_pairs={{0,4},{1,29},{2,6},{3,31},{4,8},{5,1},{6,10},{7,3},{8,12},{9,5},{1... | collective-permute-start | bytes 884744 | tf_op jit(solution)/shard_map/ppermute | solution.py:25
  16.9 6.8 %collective-permute-start.3 = (bf16[128,1152]{1,0:T(8,128)(2,1)S(1)}, bf16[128,1152]{1,0:T(8,128)(2,1)S(1)}, u32[]{:S(2)}, u32[]{:S(2)}) collective-permute-start(bf16[128,1152]{1,0:T(8,128)(2,1)S(1)} %get-tuple-element.60.refs_1_.refs_0_), channel_id=1, source_target_pairs={{0,4},{1,29},{2,6},{3,31},{4,8},{5,1},{6,10},{7,3},{8,12},{9,5},{1... | collective-permute-start | bytes 884744 | tf_op jit(solution)/shard_map/ppermute | solution.py:25
  17.0 6.8 %collective-permute-start.4 = (bf16[128,1152]{1,0:T(8,128)(2,1)S(1)}, bf16[128,1152]{1,0:T(8,128)(2,1)S(1)}, u32[]{:S(2)}, u32[]{:S(2)}) collective-permute-start(bf16[128,1152]{1,0:T(8,128)(2,1)S(1)} %get-tuple-element.60.refs_1_.refs_0_), channel_id=1, source_target_pairs={{0,1},{1,0},{2,3},{3,2},{4,5},{5,4},{6,7},{7,6},{8,9},{9,8},{10,11... | collective-permute-start | bytes 884744 | tf_op jit(solution)/shard_map/ppermute | solution.py:33
  17.0 12.5 %collective-permute-start.6 = (bf16[128,1152]{1,0:T(8,128)(2,1)S(1)}, bf16[128,1152]{1,0:T(8,128)(2,1)S(1)}, u32[]{:S(2)}, u32[]{:S(2)}) collective-permute-start(bf16[128,1152]{1,0:T(8,128)(2,1)S(1)} %collective-permute-done.5.refs_3_), channel_id=1, source_target_pairs={{0,1},{1,0},{2,3},{3,2},{4,5},{5,4},{6,7},{7,6},{8,9},{9,8},{10,11... | collective-permute-start | bytes 884744 | tf_op jit(solution)/shard_map/ppermute | solution.py:33
  17.5 13.3 %collective-permute-start.10 = (bf16[128,1152]{1,0:T(8,128)(2,1)S(1)}, bf16[128,1152]{1,0:T(8,128)(2,1)S(1)}, u32[]{:S(2)}, u32[]{:S(2)}) collective-permute-start(bf16[128,1152]{1,0:T(8,128)(2,1)S(1)} %collective-permute-done.9.refs_1_), channel_id=1, source_target_pairs={{0,4},{1,29},{2,6},{3,31},{4,8},{5,1},{6,10},{7,3},{8,12},{9,5},{1... | collective-permute-start | bytes 884744 | tf_op jit(solution)/shard_map/ppermute | solution.py:25
  20.6 10.3 %collective-permute-start.2 = (bf16[128,1152]{1,0:T(8,128)(2,1)S(1)}, bf16[128,1152]{1,0:T(8,128)(2,1)S(1)}, u32[]{:S(2)}, u32[]{:S(2)}) collective-permute-start(bf16[128,1152]{1,0:T(8,128)(2,1)S(1)} %collective-permute-done.1.refs_0_), channel_id=1, source_target_pairs={{0,4},{1,29},{2,6},{3,31},{4,8},{5,1},{6,10},{7,3},{8,12},{9,5},{1... | collective-permute-start | bytes 884744 | tf_op jit(solution)/shard_map/ppermute | solution.py:25
  23.8 9.5 %collective-permute-start.14 = (bf16[128,1152]{1,0:T(8,128)(2,1)S(1)}, bf16[128,1152]{1,0:T(8,128)(2,1)S(1)}, u32[]{:S(2)}, u32[]{:S(2)}) collective-permute-start(bf16[128,1152]{1,0:T(8,128)(2,1)S(1)} %collective-permute-done.4.refs_2_), channel_id=1, source_target_pairs={{0,4},{1,29},{2,6},{3,31},{4,8},{5,1},{6,10},{7,3},{8,12},{9,5},{1... | collective-permute-start | bytes 884744 | tf_op jit(solution)/shard_map/ppermute | solution.py:25
  28.2 10.1 %collective-permute-start.12 = (bf16[128,1152]{1,0:T(8,128)(2,1)S(1)}, bf16[128,1152]{1,0:T(8,128)(2,1)S(1)}, u32[]{:S(2)}, u32[]{:S(2)}) collective-permute-start(bf16[128,1152]{1,0:T(8,128)(2,1)S(1)} %get-tuple-element.45.refs_0_.refs_1_), channel_id=1, source_target_pairs={{0,2},{1,3},{2,0},{3,1},{4,6},{5,7},{6,4},{7,5},{8,10},{9,11},{10,... | collective-permute-start | bytes 884744 | tf_op jit(solution)/shard_map/ppermute | solution.py:29
  30.8 9.4 %collective-permute-start.11 = (bf16[128,1152]{1,0:T(8,128)(2,1)S(1)}, bf16[128,1152]{1,0:T(8,128)(2,1)S(1)}, u32[]{:S(2)}, u32[]{:S(2)}) collective-permute-start(bf16[128,1152]{1,0:T(8,128)(2,1)S(1)} %collective-permute-done.10.refs_1_), channel_id=1, source_target_pairs={{0,4},{1,29},{2,6},{3,31},{4,8},{5,1},{6,10},{7,3},{8,12},{9,5},{1... | collective-permute-start | bytes 884744 | tf_op jit(solution)/shard_map/ppermute | solution.py:25
  30.9 11.3 %collective-permute-start.7 = (bf16[128,1152]{1,0:T(8,128)(2,1)S(1)}, bf16[128,1152]{1,0:T(8,128)(2,1)S(1)}, u32[]{:S(2)}, u32[]{:S(2)}) collective-permute-start(bf16[128,1152]{1,0:T(8,128)(2,1)S(1)} %collective-permute-done.2.refs_0_), channel_id=1, source_target_pairs={{0,4},{1,29},{2,6},{3,31},{4,8},{5,1},{6,10},{7,3},{8,12},{9,5},{1... | collective-permute-start | bytes 884744 | tf_op jit(solution)/shard_map/ppermute | solution.py:25
  33.2 12.0 %collective-permute-start.15 = (bf16[128,1152]{1,0:T(8,128)(2,1)S(1)}, bf16[128,1152]{1,0:T(8,128)(2,1)S(1)}, u32[]{:S(2)}, u32[]{:S(2)}) collective-permute-start(bf16[128,1152]{1,0:T(8,128)(2,1)S(1)} %collective-permute-done.3.refs_0_), channel_id=1, source_target_pairs={{0,4},{1,29},{2,6},{3,31},{4,8},{5,1},{6,10},{7,3},{8,12},{9,5},{1... | collective-permute-start | bytes 884744 | tf_op jit(solution)/shard_map/ppermute | solution.py:25
  43.4 18.2 %collective-permute-start.13 = (bf16[272,1152]{1,0:T(8,128)(2,1)S(1)}, bf16[272,1152]{1,0:T(8,128)(2,1)S(1)}, u32[]{:S(2)}, u32[]{:S(2)}) collective-permute-start(bf16[272,1152]{1,0:T(8,128)(2,1)S(1)} %get-tuple-element.56), channel_id=1, source_target_pairs={{0,2},{1,3},{2,0},{3,1},{4,6},{5,7},{6,4},{7,5},{8,10},{9,11},{10,... | collective-permute-start | bytes 1880072 | tf_op jit(solution)/shard_map/ppermute | solution.py:29
  44.7 5.9 %collective-permute-start.19 = (bf16[128,1152]{1,0:T(8,128)(2,1)S(1)}, bf16[128,1152]{1,0:T(8,128)(2,1)S(1)}, u32[]{:S(2)}, u32[]{:S(2)}) collective-permute-start(bf16[128,1152]{1,0:T(8,128)(2,1)S(1)} %collective-permute-done.14.refs_1_), channel_id=1, source_target_pairs={{0,4},{1,29},{2,6},{3,31},{4,8},{5,1},{6,10},{7,3},{8,12},{9,5},{1... | collective-permute-start | bytes 884744 | tf_op jit(solution)/shard_map/ppermute | solution.py:25
  45.2 8.5 %collective-permute-start.16 = (bf16[128,1152]{1,0:T(8,128)(2,1)S(1)}, bf16[128,1152]{1,0:T(8,128)(2,1)S(1)}, u32[]{:S(2)}, u32[]{:S(2)}) collective-permute-start(bf16[128,1152]{1,0:T(8,128)(2,1)S(1)} %collective-permute-done.15.refs_0_), channel_id=1, source_target_pairs={{0,4},{1,29},{2,6},{3,31},{4,8},{5,1},{6,10},{7,3},{8,12},{9,5},{1... | collective-permute-start | bytes 884744 | tf_op jit(solution)/shard_map/ppermute | solution.py:25
  45.8 9.3 %collective-permute-start.18 = (bf16[128,1152]{1,0:T(8,128)(2,1)S(1)}, bf16[128,1152]{1,0:T(8,128)(2,1)S(1)}, u32[]{:S(2)}, u32[]{:S(2)}) collective-permute-start(bf16[128,1152]{1,0:T(8,128)(2,1)S(1)} %collective-permute-done.12.refs_3_), channel_id=1, source_target_pairs={{0,1},{1,0},{2,3},{3,2},{4,5},{5,4},{6,7},{7,6},{8,9},{9,8},{10,11... | collective-permute-start | bytes 884744 | tf_op jit(solution)/shard_map/ppermute | solution.py:33
  50.6 9.3 %collective-permute-start.20 = (bf16[128,1152]{1,0:T(8,128)(2,1)S(1)}, bf16[128,1152]{1,0:T(8,128)(2,1)S(1)}, u32[]{:S(2)}, u32[]{:S(2)}) collective-permute-start(bf16[128,1152]{1,0:T(8,128)(2,1)S(1)} %collective-permute-done.19.refs_1_), channel_id=1, source_target_pairs={{0,4},{1,29},{2,6},{3,31},{4,8},{5,1},{6,10},{7,3},{8,12},{9,5},{1... | collective-permute-start | bytes 884744 | tf_op jit(solution)/shard_map/ppermute | solution.py:25
  53.7 7.9 %collective-permute-start.17 = (bf16[128,1152]{1,0:T(8,128)(2,1)S(1)}, bf16[128,1152]{1,0:T(8,128)(2,1)S(1)}, u32[]{:S(2)}, u32[]{:S(2)}) collective-permute-start(bf16[128,1152]{1,0:T(8,128)(2,1)S(1)} %collective-permute-done.16.refs_0_), channel_id=1, source_target_pairs={{0,4},{1,29},{2,6},{3,31},{4,8},{5,1},{6,10},{7,3},{8,12},{9,5},{1... | collective-permute-start | bytes 884744 | tf_op jit(solution)/shard_map/ppermute | solution.py:25
  62.8 6.8 %copy-start.3 = (f32[128,1152]{1,0:T(8,128)S(1)}, f32[128,1152]{1,0:T(8,128)}, u32[]{:S(2)}) copy-start(f32[128,1152]{1,0:T(8,128)} %feats_ref.1) | copy-start | bytes 1769476
  62.8 4.1 %collective-permute-start.21 = (bf16[272,1152]{1,0:T(8,128)(2,1)S(1)}, bf16[272,1152]{1,0:T(8,128)(2,1)S(1)}, u32[]{:S(2)}, u32[]{:S(2)}) collective-permute-start(bf16[272,1152]{1,0:T(8,128)(2,1)S(1)} %get-tuple-element.65), channel_id=1, source_target_pairs={{0,1},{1,0},{2,3},{3,2},{4,5},{5,4},{6,7},{7,6},{8,9},{9,8},{10,11... | collective-permute-start | bytes 1880072 | tf_op jit(solution)/shard_map/ppermute | solution.py:33
  67.0 9.0 %copy-start.1 = (f32[128,1152]{1,0:T(8,128)S(1)}, f32[128,1152]{1,0:T(8,128)}, u32[]{:S(2)}) copy-start(f32[128,1152]{1,0:T(8,128)} %feats_ref.2) | copy-start | bytes 1769476
  67.1 2.5 %collective-permute-start.22 = (bf16[128,1152]{1,0:T(8,128)(2,1)S(1)}, bf16[128,1152]{1,0:T(8,128)(2,1)S(1)}, u32[]{:S(2)}, u32[]{:S(2)}) collective-permute-start(bf16[128,1152]{1,0:T(8,128)(2,1)S(1)} %get-tuple-element.68), channel_id=1, source_target_pairs={{0,1},{1,0},{2,3},{3,2},{4,5},{5,4},{6,7},{7,6},{8,9},{9,8},{10,11... | collective-permute-start | bytes 884744 | tf_op jit(solution)/shard_map/ppermute | solution.py:33
  67.6 8.5 %collective-permute-start.24 = (bf16[128,1152]{1,0:T(8,128)(2,1)S(1)}, bf16[128,1152]{1,0:T(8,128)(2,1)S(1)}, u32[]{:S(2)}, u32[]{:S(2)}) collective-permute-start(bf16[128,1152]{1,0:T(8,128)(2,1)S(1)} %shard_map.78), channel_id=1, source_target_pairs={{0,2},{1,3},{2,0},{3,1},{4,6},{5,7},{6,4},{7,5},{8,10},{9,11},{10,... | collective-permute-start | bytes 884744 | tf_op jit(solution)/shard_map/ppermute | solution.py:29
  68.3 1.3 %collective-permute-start.23 = (bf16[16,128]{1,0:T(8,128)(2,1)S(1)}, bf16[16,128]{1,0:T(8,128)(2,1)S(1)}, u32[]{:S(2)}, u32[]{:S(2)}) collective-permute-start(bf16[16,128]{1,0:T(8,128)(2,1)S(1)} %get-tuple-element.69), channel_id=1, source_target_pairs={{0,1},{1,0},{2,3},{3,2},{4,5},{5,4},{6,7},{7,6},{8,9},{9,8},{10,11... | collective-permute-start | bytes 12296 | tf_op jit(solution)/shard_map/ppermute | solution.py:33

commit v3 on v2

--- a/solution.py
+++ b/solution.py
@@ -252,13 +252,13 @@
     tb3 = along_z(after(tb2, a0))
     a2, loss = step([ta2, after(tb2, text_chip)], mine_i, scalars, n, a1, loss, True)
     ta4 = along_z(after(ta3, a0))
-    ia2 = along_z(after(ia1, ib1))
+    ia2 = along_z(after(ia1, tb1))
     mine_t, b0 = step([after(image, ib1)], texts, scalars, n)
     b1, = step([ia1, ib1], mine_t, scalars, n, b0)
-    ib2 = along_z(after(ib1, ta3))
+    ib2 = along_z(after(ib1, tb2))
     ia3 = along_z(ia2)
     a3, loss = step([ta3, tb3], mine_i, scalars, n, a2, loss, True)
-    ib3 = along_z(ib2)
+    ib3 = along_z(after(ib2, b1))
     kept_i, loss, for_chip_i = step([ta4], mine_i, scalars, n, a3, loss, True, True, True)
     by_chip_i = across_x(for_chip_i)
     ia4 = along_z(ia3)

time: 77.3 us -> 76.8 us (level)
  starting transfers between devices: 39.6 us -> 35.2 us
  waiting for transfers between devices: 14.9 us -> 18.7 us
    ppermute x14, starting transfers between devices: 26.1 us -> 21 us  [along_z(): return lax.ppermute(rows, 'blk', route)]
    ppermute x14, waiting for transfers between devices: 7.06 us -> 10.6 us  [along_z(): return lax.ppermute(rows, 'blk', route)]
    ppermute x7, starting transfers between devices: 8.86 us -> 9.83 us  [across_core(): return lax.ppermute(rows, 'blk', [(i, i ^ 1) for i in range(RING * PLANE)])]
  transfers between devices with their start and end apart: 25 -> 25, of which waited for: 7 -> 9; matrix products, arithmetic and copies ran while one was open for 0% -> 0% of each run, Pallas kernels for 20% -> 21%
where the time goes in v3:
time: 76.8 us; the launch traced here: 76.6 us
  starting transfers between devices  35.2 us (46%)
  waiting for transfers between devices  18.7 us (24%)
  Pallas kernels  18.4 us (24%)
  local copies, waits for them, and re-layouts  2.14 us (3%)
  between operations  2.07 us (3%)
    ppermute x14, starting transfers between devices, along_z(): return lax.ppermute(rows, 'blk', route)  21 us
    pallas_call x15, Pallas kernels, run(): pl.pallas_call(kernel, out_shape=shapes, in_specs=[SMEM] * len(scalars) +...  18.4 us
    ppermute x14, waiting for transfers between devices, along_z(): return lax.ppermute(rows, 'blk', route)  10.6 us
    ppermute x7, starting transfers between devices, across_core(): return lax.ppermute(rows, 'blk', [(i, i ^ 1) for i in range(RING * PLANE)])  9.83 us
    ppermute x4, waiting for transfers between devices, across_x(): return lax.ppermute(rows, 'blk', [(i, i ^ 2) for i in range(RING * PLANE)])  5.51 us
    ppermute x4, starting transfers between devices, across_x(): return lax.ppermute(rows, 'blk', [(i, i ^ 2) for i in range(RING * PLANE)])  4.38 us
    ppermute x7, waiting for transfers between devices, across_core(): return lax.ppermute(rows, 'blk', [(i, i ^ 1) for i in range(RING * PLANE)])  2.52 us
    unnamed x8, local copies, waits for them, and re-layouts  2.14 us
  transfers between devices with their start and end apart: 25, of which 9 were waited for; matrix products, arithmetic and copies ran while one was open for 0% of the time, Pallas kernels for 21%

profile of v3, /device:TPU:1, one launch (start us, length us, event | category | flops | bytes accessed | tf_op | source)
XLA Modules:
  0.0 76.6 jit_solution(108470740171846611)
XLA Ops:
  0.6 0.0 copy-start
  0.6 1.1 %copy-done = f32[128,1152]{1,0:T(8,128)S(1)} copy-done((f32[128,1152]{1,0:T(8,128)S(1)}, f32[128,1152]{1,0:T(8,128)}, u32[]{:S(2)}) %copy-start) | copy-done | bytes 589848
  1.7 1.1 %copy-done.2 = f32[128,1152]{1,0:T(8,128)S(1)} copy-done((f32[128,1152]{1,0:T(8,128)S(1)}, f32[128,1152]{1,0:T(8,128)}, u32[]{:S(2)}) %copy-start.2) | copy-done | bytes 589848
  2.8 0.2 shard_map.67
  3.0 3.3 %collective-permute-start.8 = (bf16[128,1152]{1,0:T(8,128)(2,1)S(1)}, bf16[128,1152]{1,0:T(8,128)(2,1)S(1)}, u32[]{:S(2)}, u32[]{:S(2)}) collective-permute-start(bf16[128,1152]{1,0:T(8,128)(2,1)S(1)} %get-tuple-element.46.refs_0_.refs_1_), channel_id=1, source_target_pairs={{0,1},{1,0},{2,3},{3,2},{4,5},{5,4},{6,7},{7,6},{8,9},{9,8},{10,11... | collective-permute-start | bytes 884744 | tf_op jit(solution)/shard_map/ppermute | solution.py:33
  6.3 3.8 %collective-permute-start = (bf16[128,1152]{1,0:T(8,128)(2,1)S(1)}, bf16[128,1152]{1,0:T(8,128)(2,1)S(1)}, u32[]{:S(2)}, u32[]{:S(2)}) collective-permute-start(bf16[128,1152]{1,0:T(8,128)(2,1)S(1)} %get-tuple-element.46.refs_0_.refs_1_), channel_id=1, source_target_pairs={{0,4},{1,29},{2,6},{3,31},{4,8},{5,1},{6,10},{7,3},{8,12},{9,5},{1... | collective-permute-start | bytes 884744 | tf_op jit(solution)/shard_map/ppermute | solution.py:25
  10.1 1.2 %collective-permute-start.5 = (bf16[128,1152]{1,0:T(8,128)(2,1)S(1)}, bf16[128,1152]{1,0:T(8,128)(2,1)S(1)}, u32[]{:S(2)}, u32[]{:S(2)}) collective-permute-start(bf16[128,1152]{1,0:T(8,128)(2,1)S(1)} %get-tuple-element.61.refs_1_.refs_0_), channel_id=1, source_target_pairs={{0,2},{1,3},{2,0},{3,1},{4,6},{5,7},{6,4},{7,5},{8,10},{9,11},{10,... | collective-permute-start | bytes 884744 | tf_op jit(solution)/shard_map/ppermute | solution.py:29
  11.3 0.0 collective-permute-done.8.refs_2_
  11.4 0.7 collective-permute-start.9
  12.1 1.7 %collective-permute-done.refs_0_ = bf16[128,1152]{1,0:T(8,128)(2,1)S(1)} collective-permute-done((bf16[128,1152]{1,0:T(8,128)(2,1)S(1)}, bf16[128,1152]{1,0:T(8,128)(2,1)S(1)}, u32[]{:S(2)}, u32[]{:S(2)}) %collective-permute-start) | collective-permute-done | bytes 294944 | tf_op jit(solution)/shard_map/ppermute | solution.py:25
  13.8 3.1 %collective-permute-start.1 = (bf16[128,1152]{1,0:T(8,128)(2,1)S(1)}, bf16[128,1152]{1,0:T(8,128)(2,1)S(1)}, u32[]{:S(2)}, u32[]{:S(2)}) collective-permute-start(bf16[128,1152]{1,0:T(8,128)(2,1)S(1)} %collective-permute-done.refs_0_), channel_id=1, source_target_pairs={{0,4},{1,29},{2,6},{3,31},{4,8},{5,1},{6,10},{7,3},{8,12},{9,5},{1... | collective-permute-start | bytes 884744 | tf_op jit(solution)/shard_map/ppermute | solution.py:25
  16.9 0.0 collective-permute-start.3
  17.0 0.0 collective-permute-start.4
  17.0 0.0 collective-permute-done.5.refs_3_
  17.0 0.5 collective-permute-start.6
  17.5 0.0 collective-permute-done.9.refs_1_
  17.5 2.7 %collective-permute-start.10 = (bf16[128,1152]{1,0:T(8,128)(2,1)S(1)}, bf16[128,1152]{1,0:T(8,128)(2,1)S(1)}, u32[]{:S(2)}, u32[]{:S(2)}) collective-permute-start(bf16[128,1152]{1,0:T(8,128)(2,1)S(1)} %collective-permute-done.9.refs_1_), channel_id=1, source_target_pairs={{0,4},{1,29},{2,6},{3,31},{4,8},{5,1},{6,10},{7,3},{8,12},{9,5},{1... | collective-permute-start | bytes 884744 | tf_op jit(solution)/shard_map/ppermute | solution.py:25
  20.1 0.5 collective-permute-done.1.refs_0_
  20.6 3.1 %collective-permute-start.2 = (bf16[128,1152]{1,0:T(8,128)(2,1)S(1)}, bf16[128,1152]{1,0:T(8,128)(2,1)S(1)}, u32[]{:S(2)}, u32[]{:S(2)}) collective-permute-start(bf16[128,1152]{1,0:T(8,128)(2,1)S(1)} %collective-permute-done.1.refs_0_), channel_id=1, source_target_pairs={{0,4},{1,29},{2,6},{3,31},{4,8},{5,1},{6,10},{7,3},{8,12},{9,5},{1... | collective-permute-start | bytes 884744 | tf_op jit(solution)/shard_map/ppermute | solution.py:25
  25.0 1.3 %collective-permute-start.12 = (bf16[128,1152]{1,0:T(8,128)(2,1)S(1)}, bf16[128,1152]{1,0:T(8,128)(2,1)S(1)}, u32[]{:S(2)}, u32[]{:S(2)}) collective-permute-start(bf16[128,1152]{1,0:T(8,128)(2,1)S(1)} %get-tuple-element.46.refs_0_.refs_1_), channel_id=1, source_target_pairs={{0,2},{1,3},{2,0},{3,1},{4,6},{5,7},{6,4},{7,5},{8,10},{9,11},{10,... | collective-permute-start | bytes 884744 | tf_op jit(solution)/shard_map/ppermute | solution.py:29
  26.3 0.0 collective-permute-done.4.refs_2_
  26.3 0.0 collective-permute-done.6.refs_4_
  26.3 1.3 %shard_map.68 = (bf16[512,1152]{1,0:T(8,128)(2,1)S(1)}, f32[512,1152]{1,0:T(8,128)S(1)}, f32[512,128]{1,0:T(8,128)S(1)}) custom-call(f32[1]{0:T(128)S(6)} %copy.7.scale_ref, f32[1]{0:T(128)S(6)} %copy.8.shift_ref, bf16[128,1152]{1,0:T(8,128)(2,1)S(1)} %get-tuple-element.46.refs_0_.refs_1_, bf16[128,1152]{1,0:T(8,128)(2,1)S(1)} %get-tuple-element.61.refs_1_.refs_0_, ...), custom_call_target="tpu_custom_call" | custom-call | tf_op jit(solution)/shard_map/pallas_call | solution.py:42
  27.6 0.0 collective-permute-done.10.refs_1_
  27.6 2.4 %collective-permute-start.11 = (bf16[128,1152]{1,0:T(8,128)(2,1)S(1)}, bf16[128,1152]{1,0:T(8,128)(2,1)S(1)}, u32[]{:S(2)}, u32[]{:S(2)}) collective-permute-start(bf16[128,1152]{1,0:T(8,128)(2,1)S(1)} %collective-permute-done.10.refs_1_), channel_id=1, source_target_pairs={{0,4},{1,29},{2,6},{3,31},{4,8},{5,1},{6,10},{7,3},{8,12},{9,5},{1... | collective-permute-start | bytes 884744 | tf_op jit(solution)/shard_map/ppermute | solution.py:25
  30.0 0.0 collective-permute-done.2.refs_0_
  30.1 3.1 %collective-permute-start.7 = (bf16[128,1152]{1,0:T(8,128)(2,1)S(1)}, bf16[128,1152]{1,0:T(8,128)(2,1)S(1)}, u32[]{:S(2)}, u32[]{:S(2)}) collective-permute-start(bf16[128,1152]{1,0:T(8,128)(2,1)S(1)} %collective-permute-done.2.refs_0_), channel_id=1, source_target_pairs={{0,4},{1,29},{2,6},{3,31},{4,8},{5,1},{6,10},{7,3},{8,12},{9,5},{1... | collective-permute-start | bytes 884744 | tf_op jit(solution)/shard_map/ppermute | solution.py:25
  33.2 0.0 collective-permute-start.17
  33.2 0.0 collective-permute-start.14
  33.3 1.9 %shard_map.69 = (f32[512,1152]{1,0:T(8,128)S(1)}, f32[512,128]{1,0:T(8,128)S(1)}) custom-call(f32[1]{0:T(128)S(6)} %copy.7.scale_ref, f32[1]{0:T(128)S(6)} %copy.8.shift_ref, bf16[128,1152]{1,0:T(8,128)(2,1)S(1)} %collective-permute-done.refs_0_, bf16[128,1152]{1,0:T(8,128)(2,1)S(1)} %collective-permute-done.9.refs_1_, ...), custom_call_target="tpu_custom_call" | custom-call | tf_op jit(solution)/shard_map/pallas_call | solution.py:42
  35.2 0.0 collective-permute-done.12.refs_3_
  35.2 1.9 %shard_map.70 = (f32[512,1152]{1,0:T(8,128)S(1)}, f32[512,128]{1,0:T(8,128)S(1)}) custom-call(f32[1]{0:T(128)S(6)} %copy.7.scale_ref, f32[1]{0:T(128)S(6)} %copy.8.shift_ref, bf16[128,1152]{1,0:T(8,128)(2,1)S(1)} %collective-permute-done.1.refs_0_, bf16[128,1152]{1,0:T(8,128)(2,1)S(1)} %collective-permute-done.10.refs_1_, ...), custom_call_target="tpu_custom_call" | custom-call | tf_op jit(solution)/shard_map/pallas_call | solution.py:42
  37.1 0.0 collective-permute-done.11.refs_1_
  37.1 1.9 %shard_map.71 = (f32[512,1152]{1,0:T(8,128)S(1)}, f32[512,128]{1,0:T(8,128)S(1)}) custom-call(f32[1]{0:T(128)S(6)} %copy.7.scale_ref, f32[1]{0:T(128)S(6)} %copy.8.shift_ref, bf16[128,1152]{1,0:T(8,128)(2,1)S(1)} %collective-permute-done.2.refs_0_, bf16[128,1152]{1,0:T(8,128)(2,1)S(1)} %collective-permute-done.11.refs_1_, ...), custom_call_target="tpu_custom_call" | custom-call | tf_op jit(solution)/shard_map/pallas_call | solution.py:42
  39.1 1.2 %shard_map.72 = (f32[256,1152]{1,0:T(8,128)S(1)}, f32[8,256]{1,0:T(8,128)S(1)}, bf16[272,1152]{1,0:T(8,128)(2,1)S(1)}) custom-call(f32[1]{0:T(128)S(6)} %copy.7.scale_ref, f32[1]{0:T(128)S(6)} %copy.8.shift_ref, bf16[128,1152]{1,0:T(8,128)(2,1)S(1)} %collective-permute-done.7.refs_0_, bf16[512,1152]{1,0:T(8,128)(2,1)S(1)} %get-tuple-element.44.refs_2_.refs_1_, ...), custom_call_target="tpu_custom_call" | custom-call | tf_op jit(solution)/shard_map/pallas_call | solution.py:42
  40.3 1.3 %collective-permute-start.13 = (bf16[272,1152]{1,0:T(8,128)(2,1)S(1)}, bf16[272,1152]{1,0:T(8,128)(2,1)S(1)}, u32[]{:S(2)}, u32[]{:S(2)}) collective-permute-start(bf16[272,1152]{1,0:T(8,128)(2,1)S(1)} %get-tuple-element.57), channel_id=1, source_target_pairs={{0,2},{1,3},{2,0},{3,1},{4,6},{5,7},{6,4},{7,5},{8,10},{9,11},{10,... | collective-permute-start | bytes 1880072 | tf_op jit(solution)/shard_map/ppermute | solution.py:29
  41.6 2.7 %collective-permute-start.18 = (bf16[128,1152]{1,0:T(8,128)(2,1)S(1)}, bf16[128,1152]{1,0:T(8,128)(2,1)S(1)}, u32[]{:S(2)}, u32[]{:S(2)}) collective-permute-start(bf16[128,1152]{1,0:T(8,128)(2,1)S(1)} %collective-permute-done.12.refs_3_), channel_id=1, source_target_pairs={{0,1},{1,0},{2,3},{3,2},{4,5},{5,4},{6,7},{7,6},{8,9},{9,8},{10,11... | collective-permute-start | bytes 884744 | tf_op jit(solution)/shard_map/ppermute | solution.py:33
  44.4 0.0 collective-permute-done.14.refs_0_
  44.4 1.9 %collective-permute-start.15 = (bf16[128,1152]{1,0:T(8,128)(2,1)S(1)}, bf16[128,1152]{1,0:T(8,128)(2,1)S(1)}, u32[]{:S(2)}, u32[]{:S(2)}) collective-permute-start(bf16[128,1152]{1,0:T(8,128)(2,1)S(1)} %collective-permute-done.14.refs_0_), channel_id=1, source_target_pairs={{0,4},{1,29},{2,6},{3,31},{4,8},{5,1},{6,10},{7,3},{8,12},{9,5},{1... | collective-permute-start | bytes 884744 | tf_op jit(solution)/shard_map/ppermute | solution.py:25
  46.3 0.0 collective-permute-done.18.refs_4_
  46.3 1.2 %shard_map.73 = (bf16[512,1152]{1,0:T(8,128)(2,1)S(1)}, f32[512,1152]{1,0:T(8,128)S(1)}) custom-call(f32[1]{0:T(128)S(6)} %copy.7.scale_ref, f32[1]{0:T(128)S(6)} %copy.8.shift_ref, bf16[128,1152]{1,0:T(8,128)(2,1)S(1)} %get-tuple-element.61.refs_1_.refs_0_, bf16[128,1152]{1,0:T(8,128)(2,1)S(1)} %get-tuple-element.46.refs_0_.refs_1_, ...), custom_call_target="tpu_custom_call" | custom-call | tf_op jit(solution)/shard_map/pallas_call | solution.py:42
  47.5 1.7 %shard_map.74.refs_3_ = f32[512,1152]{1,0:T(8,128)S(1)} custom-call(f32[1]{0:T(128)S(6)} %copy.7.scale_ref, f32[1]{0:T(128)S(6)} %copy.8.shift_ref, bf16[128,1152]{1,0:T(8,128)(2,1)S(1)} %collective-permute-done.3.refs_0_, bf16[128,1152]{1,0:T(8,128)(2,1)S(1)} %collective-permute-done.17.refs_1_, bf16[512,1152]{1,0:T(8,128)(2,1)S(1)} %get-tuple-element.62.refs_2_.refs_1_, ...), custom_call_target="tpu_custom_call" | custom-call | tf_op jit(solution)/shard_map/pallas_call | solution.py:42
  49.3 2.4 %collective-permute-done.19.refs_1_ = bf16[128,1152]{1,0:T(8,128)(2,1)S(1)} collective-permute-done((bf16[128,1152]{1,0:T(8,128)(2,1)S(1)}, bf16[128,1152]{1,0:T(8,128)(2,1)S(1)}, u32[]{:S(2)}, u32[]{:S(2)}) %collective-permute-start.19) | collective-permute-done | bytes 294944 | tf_op jit(solution)/shard_map/ppermute | solution.py:25
  51.6 3.2 %collective-permute-done.15.refs_0_ = bf16[128,1152]{1,0:T(8,128)(2,1)S(1)} collective-permute-done((bf16[128,1152]{1,0:T(8,128)(2,1)S(1)}, bf16[128,1152]{1,0:T(8,128)(2,1)S(1)}, u32[]{:S(2)}, u32[]{:S(2)}) %collective-permute-start.15) | collective-permute-done | bytes 294944 | tf_op jit(solution)/shard_map/ppermute | solution.py:25
  54.8 0.0 collective-permute-start.16
  54.8 1.7 %shard_map.75.refs_3_ = f32[512,1152]{1,0:T(8,128)S(1)} custom-call(f32[1]{0:T(128)S(6)} %copy.7.scale_ref, f32[1]{0:T(128)S(6)} %copy.8.shift_ref, bf16[128,1152]{1,0:T(8,128)(2,1)S(1)} %collective-permute-done.14.refs_0_, bf16[128,1152]{1,0:T(8,128)(2,1)S(1)} %collective-permute-done.19.refs_1_, bf16[512,1152]{1,0:T(8,128)(2,1)S(1)} %get-tuple-element.62.refs_2_.refs_1_, ...), custom_call_target="tpu_custom_call" | custom-call | tf_op jit(solution)/shard_map/pallas_call | solution.py:42
  56.5 1.4 %collective-permute-done.20.refs_1_ = bf16[128,1152]{1,0:T(8,128)(2,1)S(1)} collective-permute-done((bf16[128,1152]{1,0:T(8,128)(2,1)S(1)}, bf16[128,1152]{1,0:T(8,128)(2,1)S(1)}, u32[]{:S(2)}, u32[]{:S(2)}) %collective-permute-start.20) | collective-permute-done | bytes 294944 | tf_op jit(solution)/shard_map/ppermute | solution.py:25
  58.0 1.7 %shard_map.76.refs_2_ = f32[512,1152]{1,0:T(8,128)S(1)} custom-call(f32[1]{0:T(128)S(6)} %copy.7.scale_ref, f32[1]{0:T(128)S(6)} %copy.8.shift_ref, bf16[128,1152]{1,0:T(8,128)(2,1)S(1)} %collective-permute-done.15.refs_0_, bf16[128,1152]{1,0:T(8,128)(2,1)S(1)} %collective-permute-done.20.refs_1_, bf16[512,1152]{1,0:T(8,128)(2,1)S(1)} %get-tuple-element.62.refs_2_.refs_1_, ...), custom_call_target="tpu_custom_call" | custom-call | tf_op jit(solution)/shard_map/pallas_call | solution.py:42
  59.7 1.4 %collective-permute-done.16.refs_0_ = bf16[128,1152]{1,0:T(8,128)(2,1)S(1)} collective-permute-done((bf16[128,1152]{1,0:T(8,128)(2,1)S(1)}, bf16[128,1152]{1,0:T(8,128)(2,1)S(1)}, u32[]{:S(2)}, u32[]{:S(2)}) %collective-permute-start.16) | collective-permute-done | bytes 294944 | tf_op jit(solution)/shard_map/ppermute | solution.py:25
  61.1 1.2 %shard_map.77 = (f32[256,1152]{1,0:T(8,128)S(1)}, bf16[272,1152]{1,0:T(8,128)(2,1)S(1)}) custom-call(f32[1]{0:T(128)S(6)} %copy.7.scale_ref, f32[1]{0:T(128)S(6)} %copy.8.shift_ref, bf16[128,1152]{1,0:T(8,128)(2,1)S(1)} %collective-permute-done.16.refs_0_, bf16[512,1152]{1,0:T(8,128)(2,1)S(1)} %get-tuple-element.62.refs_2_.refs_1_, ...), custom_call_target="tpu_custom_call" | custom-call | tf_op jit(solution)/shard_map/pallas_call | solution.py:42
  62.3 0.0 copy-start.3
  62.3 2.4 %collective-permute-start.21 = (bf16[272,1152]{1,0:T(8,128)(2,1)S(1)}, bf16[272,1152]{1,0:T(8,128)(2,1)S(1)}, u32[]{:S(2)}, u32[]{:S(2)}) collective-permute-start(bf16[272,1152]{1,0:T(8,128)(2,1)S(1)} %get-tuple-element.67), channel_id=1, source_target_pairs={{0,1},{1,0},{2,3},{3,2},{4,5},{5,4},{6,7},{7,6},{8,9},{9,8},{10,11... | collective-permute-start | bytes 1880072 | tf_op jit(solution)/shard_map/ppermute | solution.py:33
  64.7 1.7 %collective-permute-done.21.refs_0_ = bf16[272,1152]{1,0:T(8,128)(2,1)S(1)} collective-permute-done((bf16[272,1152]{1,0:T(8,128)(2,1)S(1)}, bf16[272,1152]{1,0:T(8,128)(2,1)S(1)}, u32[]{:S(2)}, u32[]{:S(2)}) %collective-permute-start.21) | collective-permute-done | bytes 626720 | tf_op jit(solution)/shard_map/ppermute | solution.py:33
  66.4 0.1 shard_map.78
  66.4 0.0 copy-start.1
  66.5 0.1 shard_map.79
  66.5 0.5 collective-permute-start.22
  67.0 0.6 collective-permute-start.24
  67.6 0.4 collective-permute-start.23
  68.0 0.8 %collective-permute-done.23.refs_3_ = bf16[16,128]{1,0:T(8,128)(2,1)S(1)} collective-permute-done((bf16[16,128]{1,0:T(8,128)(2,1)S(1)}, bf16[16,128]{1,0:T(8,128)(2,1)S(1)}, u32[]{:S(2)}, u32[]{:S(2)}) %collective-permute-start.23) | collective-permute-done | bytes 4128 | tf_op jit(solution)/shard_map/ppermute | solution.py:33
  68.8 0.0 collective-permute-done.22.refs_1_
  68.8 1.1 %shard_map.80 = (f32[128,1152]{1,0:T(8,128)}, f32[1,128]{1,0:T(1,128)}) custom-call(f32[128,1152]{1,0:T(8,128)S(1)} %copy-done.3, f32[256,1152]{1,0:T(8,128)S(1)} %get-tuple-element.68.kept_ref, bf16[272,1152]{1,0:T(8,128)(2,1)S(1)} %collective-permute-done.13.refs_1_.refs_0_, bf16[128,1152]{1,0:T(8,128)(2,1)S(1)} %collective-permute-done.22.refs_1_, ...), custom_call_target="tpu_custom_call" | custom-call | tf_op jit(solution)/shard_map/pallas_call | solution.py:42
  69.9 5.5 %collective-permute-done.24.refs_1_ = bf16[128,1152]{1,0:T(8,128)(2,1)S(1)} collective-permute-done((bf16[128,1152]{1,0:T(8,128)(2,1)S(1)}, bf16[128,1152]{1,0:T(8,128)(2,1)S(1)}, u32[]{:S(2)}, u32[]{:S(2)}) %collective-permute-start.24) | collective-permute-done | bytes 294944 | tf_op jit(solution)/shard_map/ppermute | solution.py:29
  75.5 1.1 %shard_map.81 = f32[128,1152]{1,0:T(8,128)} custom-call(f32[128,1152]{1,0:T(8,128)S(1)} %copy-done.1, f32[256,1152]{1,0:T(8,128)S(1)} %get-tuple-element.66.kept_ref, bf16[272,1152]{1,0:T(8,128)(2,1)S(1)} %collective-permute-done.21.refs_0_, bf16[128,1152]{1,0:T(8,128)(2,1)S(1)} %collective-permute-done.24.refs_1_), custom_call_target="tpu_custom_call" | custom-call | tf_op jit(solution)/shard_map/pallas_call | solution.py:42
  (9 shorter events, 0.0 us)
Async XLA Ops:
  0.6 1.1 %copy-start = (f32[128,1152]{1,0:T(8,128)S(1)}, f32[128,1152]{1,0:T(8,128)}, u32[]{:S(2)}) copy-start(f32[128,1152]{1,0:T(8,128)} %feats_ref.2) | copy-start | bytes 1769476
  1.7 1.1 %copy-start.2 = (f32[128,1152]{1,0:T(8,128)S(1)}, f32[128,1152]{1,0:T(8,128)}, u32[]{:S(2)}) copy-start(f32[128,1152]{1,0:T(8,128)} %feats_ref.1) | copy-start | bytes 1769476
  3.0 8.4 %collective-permute-start.8 = (bf16[128,1152]{1,0:T(8,128)(2,1)S(1)}, bf16[128,1152]{1,0:T(8,128)(2,1)S(1)}, u32[]{:S(2)}, u32[]{:S(2)}) collective-permute-start(bf16[128,1152]{1,0:T(8,128)(2,1)S(1)} %get-tuple-element.46.refs_0_.refs_1_), channel_id=1, source_target_pairs={{0,1},{1,0},{2,3},{3,2},{4,5},{5,4},{6,7},{7,6},{8,9},{9,8},{10,11... | collective-permute-start | bytes 884744 | tf_op jit(solution)/shard_map/ppermute | solution.py:33
  6.3 7.5 %collective-permute-start = (bf16[128,1152]{1,0:T(8,128)(2,1)S(1)}, bf16[128,1152]{1,0:T(8,128)(2,1)S(1)}, u32[]{:S(2)}, u32[]{:S(2)}) collective-permute-start(bf16[128,1152]{1,0:T(8,128)(2,1)S(1)} %get-tuple-element.46.refs_0_.refs_1_), channel_id=1, source_target_pairs={{0,4},{1,29},{2,6},{3,31},{4,8},{5,1},{6,10},{7,3},{8,12},{9,5},{1... | collective-permute-start | bytes 884744 | tf_op jit(solution)/shard_map/ppermute | solution.py:25
  10.1 6.8 %collective-permute-start.5 = (bf16[128,1152]{1,0:T(8,128)(2,1)S(1)}, bf16[128,1152]{1,0:T(8,128)(2,1)S(1)}, u32[]{:S(2)}, u32[]{:S(2)}) collective-permute-start(bf16[128,1152]{1,0:T(8,128)(2,1)S(1)} %get-tuple-element.61.refs_1_.refs_0_), channel_id=1, source_target_pairs={{0,2},{1,3},{2,0},{3,1},{4,6},{5,7},{6,4},{7,5},{8,10},{9,11},{10,... | collective-permute-start | bytes 884744 | tf_op jit(solution)/shard_map/ppermute | solution.py:29
  11.4 6.1 %collective-permute-start.9 = (bf16[128,1152]{1,0:T(8,128)(2,1)S(1)}, bf16[128,1152]{1,0:T(8,128)(2,1)S(1)}, u32[]{:S(2)}, u32[]{:S(2)}) collective-permute-start(bf16[128,1152]{1,0:T(8,128)(2,1)S(1)} %collective-permute-done.8.refs_2_), channel_id=1, source_target_pairs={{0,4},{1,29},{2,6},{3,31},{4,8},{5,1},{6,10},{7,3},{8,12},{9,5},{1... | collective-permute-start | bytes 884744 | tf_op jit(solution)/shard_map/ppermute | solution.py:25
  13.8 6.8 %collective-permute-start.1 = (bf16[128,1152]{1,0:T(8,128)(2,1)S(1)}, bf16[128,1152]{1,0:T(8,128)(2,1)S(1)}, u32[]{:S(2)}, u32[]{:S(2)}) collective-permute-start(bf16[128,1152]{1,0:T(8,128)(2,1)S(1)} %collective-permute-done.refs_0_), channel_id=1, source_target_pairs={{0,4},{1,29},{2,6},{3,31},{4,8},{5,1},{6,10},{7,3},{8,12},{9,5},{1... | collective-permute-start | bytes 884744 | tf_op jit(solution)/shard_map/ppermute | solution.py:25
  16.9 8.1 %collective-permute-start.3 = (bf16[128,1152]{1,0:T(8,128)(2,1)S(1)}, bf16[128,1152]{1,0:T(8,128)(2,1)S(1)}, u32[]{:S(2)}, u32[]{:S(2)}) collective-permute-start(bf16[128,1152]{1,0:T(8,128)(2,1)S(1)} %get-tuple-element.61.refs_1_.refs_0_), channel_id=1, source_target_pairs={{0,4},{1,29},{2,6},{3,31},{4,8},{5,1},{6,10},{7,3},{8,12},{9,5},{1... | collective-permute-start | bytes 884744 | tf_op jit(solution)/shard_map/ppermute | solution.py:25
  17.0 9.4 %collective-permute-start.4 = (bf16[128,1152]{1,0:T(8,128)(2,1)S(1)}, bf16[128,1152]{1,0:T(8,128)(2,1)S(1)}, u32[]{:S(2)}, u32[]{:S(2)}) collective-permute-start(bf16[128,1152]{1,0:T(8,128)(2,1)S(1)} %get-tuple-element.61.refs_1_.refs_0_), channel_id=1, source_target_pairs={{0,1},{1,0},{2,3},{3,2},{4,5},{5,4},{6,7},{7,6},{8,9},{9,8},{10,11... | collective-permute-start | bytes 884744 | tf_op jit(solution)/shard_map/ppermute | solution.py:33
  17.0 9.4 %collective-permute-start.6 = (bf16[128,1152]{1,0:T(8,128)(2,1)S(1)}, bf16[128,1152]{1,0:T(8,128)(2,1)S(1)}, u32[]{:S(2)}, u32[]{:S(2)}) collective-permute-start(bf16[128,1152]{1,0:T(8,128)(2,1)S(1)} %collective-permute-done.5.refs_3_), channel_id=1, source_target_pairs={{0,1},{1,0},{2,3},{3,2},{4,5},{5,4},{6,7},{7,6},{8,9},{9,8},{10,11... | collective-permute-start | bytes 884744 | tf_op jit(solution)/shard_map/ppermute | solution.py:33
  17.5 10.1 %collective-permute-start.10 = (bf16[128,1152]{1,0:T(8,128)(2,1)S(1)}, bf16[128,1152]{1,0:T(8,128)(2,1)S(1)}, u32[]{:S(2)}, u32[]{:S(2)}) collective-permute-start(bf16[128,1152]{1,0:T(8,128)(2,1)S(1)} %collective-permute-done.9.refs_1_), channel_id=1, source_target_pairs={{0,4},{1,29},{2,6},{3,31},{4,8},{5,1},{6,10},{7,3},{8,12},{9,5},{1... | collective-permute-start | bytes 884744 | tf_op jit(solution)/shard_map/ppermute | solution.py:25
  20.6 9.5 %collective-permute-start.2 = (bf16[128,1152]{1,0:T(8,128)(2,1)S(1)}, bf16[128,1152]{1,0:T(8,128)(2,1)S(1)}, u32[]{:S(2)}, u32[]{:S(2)}) collective-permute-start(bf16[128,1152]{1,0:T(8,128)(2,1)S(1)} %collective-permute-done.1.refs_0_), channel_id=1, source_target_pairs={{0,4},{1,29},{2,6},{3,31},{4,8},{5,1},{6,10},{7,3},{8,12},{9,5},{1... | collective-permute-start | bytes 884744 | tf_op jit(solution)/shard_map/ppermute | solution.py:25
  25.0 10.2 %collective-permute-start.12 = (bf16[128,1152]{1,0:T(8,128)(2,1)S(1)}, bf16[128,1152]{1,0:T(8,128)(2,1)S(1)}, u32[]{:S(2)}, u32[]{:S(2)}) collective-permute-start(bf16[128,1152]{1,0:T(8,128)(2,1)S(1)} %get-tuple-element.46.refs_0_.refs_1_), channel_id=1, source_target_pairs={{0,2},{1,3},{2,0},{3,1},{4,6},{5,7},{6,4},{7,5},{8,10},{9,11},{10,... | collective-permute-start | bytes 884744 | tf_op jit(solution)/shard_map/ppermute | solution.py:29
  27.6 9.5 %collective-permute-start.11 = (bf16[128,1152]{1,0:T(8,128)(2,1)S(1)}, bf16[128,1152]{1,0:T(8,128)(2,1)S(1)}, u32[]{:S(2)}, u32[]{:S(2)}) collective-permute-start(bf16[128,1152]{1,0:T(8,128)(2,1)S(1)} %collective-permute-done.10.refs_1_), channel_id=1, source_target_pairs={{0,4},{1,29},{2,6},{3,31},{4,8},{5,1},{6,10},{7,3},{8,12},{9,5},{1... | collective-permute-start | bytes 884744 | tf_op jit(solution)/shard_map/ppermute | solution.py:25
  30.1 9.0 %collective-permute-start.7 = (bf16[128,1152]{1,0:T(8,128)(2,1)S(1)}, bf16[128,1152]{1,0:T(8,128)(2,1)S(1)}, u32[]{:S(2)}, u32[]{:S(2)}) collective-permute-start(bf16[128,1152]{1,0:T(8,128)(2,1)S(1)} %collective-permute-done.2.refs_0_), channel_id=1, source_target_pairs={{0,4},{1,29},{2,6},{3,31},{4,8},{5,1},{6,10},{7,3},{8,12},{9,5},{1... | collective-permute-start | bytes 884744 | tf_op jit(solution)/shard_map/ppermute | solution.py:25
  33.2 11.2 %collective-permute-start.17 = (bf16[128,1152]{1,0:T(8,128)(2,1)S(1)}, bf16[128,1152]{1,0:T(8,128)(2,1)S(1)}, u32[]{:S(2)}, u32[]{:S(2)}) collective-permute-start(bf16[128,1152]{1,0:T(8,128)(2,1)S(1)} %collective-permute-done.4.refs_2_), channel_id=1, source_target_pairs={{0,4},{1,29},{2,6},{3,31},{4,8},{5,1},{6,10},{7,3},{8,12},{9,5},{1... | collective-permute-start | bytes 884744 | tf_op jit(solution)/shard_map/ppermute | solution.py:25
  33.2 11.1 %collective-permute-start.14 = (bf16[128,1152]{1,0:T(8,128)(2,1)S(1)}, bf16[128,1152]{1,0:T(8,128)(2,1)S(1)}, u32[]{:S(2)}, u32[]{:S(2)}) collective-permute-start(bf16[128,1152]{1,0:T(8,128)(2,1)S(1)} %collective-permute-done.3.refs_0_), channel_id=1, source_target_pairs={{0,4},{1,29},{2,6},{3,31},{4,8},{5,1},{6,10},{7,3},{8,12},{9,5},{1... | collective-permute-start | bytes 884744 | tf_op jit(solution)/shard_map/ppermute | solution.py:25
  40.3 20.8 %collective-permute-start.13 = (bf16[272,1152]{1,0:T(8,128)(2,1)S(1)}, bf16[272,1152]{1,0:T(8,128)(2,1)S(1)}, u32[]{:S(2)}, u32[]{:S(2)}) collective-permute-start(bf16[272,1152]{1,0:T(8,128)(2,1)S(1)} %get-tuple-element.57), channel_id=1, source_target_pairs={{0,2},{1,3},{2,0},{3,1},{4,6},{5,7},{6,4},{7,5},{8,10},{9,11},{10,... | collective-permute-start | bytes 1880072 | tf_op jit(solution)/shard_map/ppermute | solution.py:29
  41.6 4.7 %collective-permute-start.18 = (bf16[128,1152]{1,0:T(8,128)(2,1)S(1)}, bf16[128,1152]{1,0:T(8,128)(2,1)S(1)}, u32[]{:S(2)}, u32[]{:S(2)}) collective-permute-start(bf16[128,1152]{1,0:T(8,128)(2,1)S(1)} %collective-permute-done.12.refs_3_), channel_id=1, source_target_pairs={{0,1},{1,0},{2,3},{3,2},{4,5},{5,4},{6,7},{7,6},{8,9},{9,8},{10,11... | collective-permute-start | bytes 884744 | tf_op jit(solution)/shard_map/ppermute | solution.py:33
  44.4 7.3 %collective-permute-start.19 = (bf16[128,1152]{1,0:T(8,128)(2,1)S(1)}, bf16[128,1152]{1,0:T(8,128)(2,1)S(1)}, u32[]{:S(2)}, u32[]{:S(2)}) collective-permute-start(bf16[128,1152]{1,0:T(8,128)(2,1)S(1)} %collective-permute-done.17.refs_1_), channel_id=1, source_target_pairs={{0,4},{1,29},{2,6},{3,31},{4,8},{5,1},{6,10},{7,3},{8,12},{9,5},{1... | collective-permute-start | bytes 884744 | tf_op jit(solution)/shard_map/ppermute | solution.py:25
  44.4 10.4 %collective-permute-start.15 = (bf16[128,1152]{1,0:T(8,128)(2,1)S(1)}, bf16[128,1152]{1,0:T(8,128)(2,1)S(1)}, u32[]{:S(2)}, u32[]{:S(2)}) collective-permute-start(bf16[128,1152]{1,0:T(8,128)(2,1)S(1)} %collective-permute-done.14.refs_0_), channel_id=1, source_target_pairs={{0,4},{1,29},{2,6},{3,31},{4,8},{5,1},{6,10},{7,3},{8,12},{9,5},{1... | collective-permute-start | bytes 884744 | tf_op jit(solution)/shard_map/ppermute | solution.py:25
  51.6 6.3 %collective-permute-start.20 = (bf16[128,1152]{1,0:T(8,128)(2,1)S(1)}, bf16[128,1152]{1,0:T(8,128)(2,1)S(1)}, u32[]{:S(2)}, u32[]{:S(2)}) collective-permute-start(bf16[128,1152]{1,0:T(8,128)(2,1)S(1)} %collective-permute-done.19.refs_1_), channel_id=1, source_target_pairs={{0,4},{1,29},{2,6},{3,31},{4,8},{5,1},{6,10},{7,3},{8,12},{9,5},{1... | collective-permute-start | bytes 884744 | tf_op jit(solution)/shard_map/ppermute | solution.py:25
  54.8 6.3 %collective-permute-start.16 = (bf16[128,1152]{1,0:T(8,128)(2,1)S(1)}, bf16[128,1152]{1,0:T(8,128)(2,1)S(1)}, u32[]{:S(2)}, u32[]{:S(2)}) collective-permute-start(bf16[128,1152]{1,0:T(8,128)(2,1)S(1)} %collective-permute-done.15.refs_0_), channel_id=1, source_target_pairs={{0,4},{1,29},{2,6},{3,31},{4,8},{5,1},{6,10},{7,3},{8,12},{9,5},{1... | collective-permute-start | bytes 884744 | tf_op jit(solution)/shard_map/ppermute | solution.py:25
  62.3 6.5 %copy-start.3 = (f32[128,1152]{1,0:T(8,128)S(1)}, f32[128,1152]{1,0:T(8,128)}, u32[]{:S(2)}) copy-start(f32[128,1152]{1,0:T(8,128)} %feats_ref.1) | copy-start | bytes 1769476
  62.3 4.0 %collective-permute-start.21 = (bf16[272,1152]{1,0:T(8,128)(2,1)S(1)}, bf16[272,1152]{1,0:T(8,128)(2,1)S(1)}, u32[]{:S(2)}, u32[]{:S(2)}) collective-permute-start(bf16[272,1152]{1,0:T(8,128)(2,1)S(1)} %get-tuple-element.67), channel_id=1, source_target_pairs={{0,1},{1,0},{2,3},{3,2},{4,5},{5,4},{6,7},{7,6},{8,9},{9,8},{10,11... | collective-permute-start | bytes 1880072 | tf_op jit(solution)/shard_map/ppermute | solution.py:33
  66.4 9.0 %copy-start.1 = (f32[128,1152]{1,0:T(8,128)S(1)}, f32[128,1152]{1,0:T(8,128)}, u32[]{:S(2)}) copy-start(f32[128,1152]{1,0:T(8,128)} %feats_ref.2) | copy-start | bytes 1769476
  66.5 2.3 %collective-permute-start.22 = (bf16[128,1152]{1,0:T(8,128)(2,1)S(1)}, bf16[128,1152]{1,0:T(8,128)(2,1)S(1)}, u32[]{:S(2)}, u32[]{:S(2)}) collective-permute-start(bf16[128,1152]{1,0:T(8,128)(2,1)S(1)} %get-tuple-element.70), channel_id=1, source_target_pairs={{0,1},{1,0},{2,3},{3,2},{4,5},{5,4},{6,7},{7,6},{8,9},{9,8},{10,11... | collective-permute-start | bytes 884744 | tf_op jit(solution)/shard_map/ppermute | solution.py:33
  67.0 8.5 %collective-permute-start.24 = (bf16[128,1152]{1,0:T(8,128)(2,1)S(1)}, bf16[128,1152]{1,0:T(8,128)(2,1)S(1)}, u32[]{:S(2)}, u32[]{:S(2)}) collective-permute-start(bf16[128,1152]{1,0:T(8,128)(2,1)S(1)} %shard_map.78), channel_id=1, source_target_pairs={{0,2},{1,3},{2,0},{3,1},{4,6},{5,7},{6,4},{7,5},{8,10},{9,11},{10,... | collective-permute-start | bytes 884744 | tf_op jit(solution)/shard_map/ppermute | solution.py:29
  67.6 1.3 %collective-permute-start.23 = (bf16[16,128]{1,0:T(8,128)(2,1)S(1)}, bf16[16,128]{1,0:T(8,128)(2,1)S(1)}, u32[]{:S(2)}, u32[]{:S(2)}) collective-permute-start(bf16[16,128]{1,0:T(8,128)(2,1)S(1)} %get-tuple-element.71), channel_id=1, source_target_pairs={{0,1},{1,0},{2,3},{3,2},{4,5},{5,4},{6,7},{7,6},{8,9},{9,8},{10,11... | collective-permute-start | bytes 12296 | tf_op jit(solution)/shard_map/ppermute | solution.py:33
